TPU v7x, 32 devices: a whole 2x2x4 slice. The times are simulated.
32 devices in a mesh: hid: 8 (over z, x), mod: 4 (over y, core).
Axes of the slice: x: 2, y: 2, z: 4, core: 2. Of those that a mesh axis runs over, the one named last changes fastest.
Arguments:
- tokens: bfloat16 [128, 8192], P('hid', 'mod'), may hold values from -6 to 6
- grad_output: bfloat16 [128, 8192], P('hid', 'mod'), may hold values from -6 to 6
- gate_weight: bfloat16 [8192, 28672], P('mod', 'hid'), may hold values from -0.0625 to 0.0625
- up_weight: bfloat16 [8192, 28672], P('mod', 'hid'), may hold values from -0.0625 to 0.0625
- down_weight: bfloat16 [28672, 8192], P('hid', 'mod'), may hold values from -0.03125 to 0.03125
Outputs:
- grad_tokens: bfloat16 [128, 8192], P('hid', 'mod')
- grad_gate: bfloat16 [8192, 28672], P('mod', 'hid')
- grad_up: bfloat16 [8192, 28672], P('mod', 'hid')
- grad_down: bfloat16 [28672, 8192], P('hid', 'mod')
All inputs are finite; a program needn't handle non-finite values.
Results may differ from a plain program's by a relative error of at most 0.0049.
Values may be sent and summed in bfloat16 or wider, within the bound.
No kernel may reach another device: no remote copies, remote signals or barrier semaphores. Data moves between devices by JAX's collectives and lax.ppermute only.
A program may use at most 128 MiB of HBM per device.

v0:
```python
import jax
import jax.numpy as jnp
from jax import lax
from jax.sharding import PartitionSpec as P


def swiglu_back(gate, up, grad_hidden):
    sigmoid_gate = jax.nn.sigmoid(gate)
    active = gate * sigmoid_gate
    hidden = (active * up).astype(jnp.bfloat16)
    up_back = (grad_hidden * active).astype(jnp.bfloat16)
    slope = sigmoid_gate * (1.0 + gate * (1.0 - sigmoid_gate))
    gate_back = (grad_hidden * up * slope).astype(jnp.bfloat16)
    return (hidden, gate_back, up_back)


def shards(tokens, grad_output, gate_weight, up_weight, down_weight):
    inputs, cotangent = (
        lax.all_gather(tokens, "hid", axis=0, tiled=True),
        lax.all_gather(grad_output, "hid", axis=0, tiled=True),
    )
    contract_cols = (((1,), (1,)), ((), ()))
    contract_rows = (((0,), (0,)), ((), ()))
    part_gate = jnp.dot(inputs, gate_weight, preferred_element_type=jnp.float32)
    part_up = jnp.dot(inputs, up_weight, preferred_element_type=jnp.float32)
    part_hidden = lax.dot_general(
        cotangent, down_weight, contract_cols, preferred_element_type=jnp.float32
    )
    gate, up, grad_hidden = lax.psum((part_gate, part_up, part_hidden), "mod")
    hidden, gate_back, up_back = swiglu_back(gate, up, grad_hidden)
    grad_down = lax.dot_general(
        hidden, cotangent, contract_rows, preferred_element_type=jnp.float32
    ).astype(jnp.bfloat16)
    grad_gate = lax.dot_general(
        inputs, gate_back, contract_rows, preferred_element_type=jnp.float32
    ).astype(jnp.bfloat16)
    grad_up = lax.dot_general(
        inputs, up_back, contract_rows, preferred_element_type=jnp.float32
    ).astype(jnp.bfloat16)
    total = lax.dot_general(
        gate_back, gate_weight, contract_cols, preferred_element_type=jnp.float32
    )
    summed = lax.psum_scatter(
        total
        + lax.dot_general(up_back, up_weight, contract_cols, preferred_element_type=jnp.float32),
        "hid",
        scatter_dimension=0,
        tiled=True,
    )
    grad_tokens = summed.astype(jnp.bfloat16)
    return (grad_tokens, grad_gate, grad_up, grad_down)


def solution(mesh):
    placed = (P("hid", "mod"), P("hid", "mod"), P("mod", "hid"), P("mod", "hid"), P("hid", "mod"))
    return jax.shard_map(
        shards,
        mesh=mesh,
        in_specs=placed,
        out_specs=(P("hid", "mod"), P("mod", "hid"), P("mod", "hid"), P("hid", "mod")),
        check_vma=False,
    )
```

profile of v0, /device:TPU:0, one launch (start us, length us, event | category | flops | bytes accessed | tf_op | source)
XLA Modules:
  0.0 309.4 jit_solution(10183936005475767630)
XLA Ops:
  7.2 0.0 all-reduce.3.cloned.1.call-start
  7.2 33.2 %all_gather.7 = bf16[128,2048]{1,0:T(8,128)(2,1)S(1)} all-gather(bf16[16,2048]{1,0:T(8,128)(2,1)} %param.5), channel_id=1, replica_groups=mesh['hid'=8,'mod'=4] {'hid'}, dimensions={0}, use_global_device_ids=true | all-gather | bytes 589824 | tf_op jit(solution)/shard_map/all_gather | solution.py:19
  40.4 31.4 %all_gather.6 = bf16[128,2048]{1,0:T(8,128)(2,1)S(1)} all-gather(bf16[16,2048]{1,0:T(8,128)(2,1)} %param.6), channel_id=1, replica_groups=mesh['hid'=8,'mod'=4] {'hid'}, dimensions={0}, use_global_device_ids=true | all-gather | bytes 589824 | tf_op jit(solution)/shard_map/all_gather | solution.py:20
  71.8 0.0 copy-start
  71.8 8.6 %fusion.7 = f32[128,3584]{1,0:T(8,128)} fusion(bf16[128,2048]{1,0:T(8,128)(2,1)S(1)} %all_gather.7, bf16[2048,3584]{1,0:T(8,128)(2,1)} %param.7), kind=kOutput, calls=%fused_computation.14 | convolution fusion | flops 1879048192 | bytes 17039360 | tf_op jit(solution)/shard_map/dot_general | solution.py:24
  80.5 1.4 copy-done
  81.9 3.4 %fusion.6 = f32[128,3584]{1,0:T(8,128)} fusion(bf16[128,2048]{1,0:T(8,128)(2,1)S(1)} %all_gather.7, bf16[2048,3584]{1,0:T(8,128)(2,1)S(1)} %copy-done), kind=kOutput, calls=%fused_computation.13 | convolution fusion | flops 1879048192 | bytes 17039360 | tf_op jit(solution)/shard_map/dot_general | solution.py:25
  85.2 11.3 %fusion.5 = f32[128,3584]{1,0:T(8,128)} fusion(bf16[128,2048]{1,0:T(8,128)(2,1)S(1)} %all_gather.6, bf16[3584,2048]{1,0:T(8,128)(2,1)} %param.9), kind=kOutput, calls=%fused_computation.12 | convolution fusion | flops 1879048192 | bytes 17039360 | tf_op jit(solution)/shard_map/dot_general | solution.py:26
  96.6 0.0 all-reduce.3.cloned.1.call-update
  96.6 0.2 reduce-scatter.2.cloned.1.call-start
  96.8 108.4 %all-reduce.3.cloned.1.call-done = (f32[128,3584]{1,0:T(8,128)}, f32[128,3584]{1,0:T(8,128)}, f32[128,3584]{1,0:T(8,128)}) async-done(((f32[128,3584]{1,0:T(8,128)}, f32[128,3584]{1,0:T(8,128)}, f32[128,3584]{1,0:T(8,128)}), (f32[128,3584]{1,0:T(8,128)}, f32[128,3584]{1,0:T(8,128)}, f32[128,3584]{1,0:T(8,128)})) %all-reduce.3.cloned.1.call-update) | async-done | bytes 5505040 | tf_op jit(solution)/shard_map/psum | solution.py:29
  205.2 3.6 %multiply_convert_fusion.1 = (bf16[128,3584]{1,0:T(8,128)(2,1)S(1)}, bf16[128,3584]{1,0:T(8,128)(2,1)S(1)}) fusion(f32[128,3584]{1,0:T(8,128)} %get-tuple-element.9, f32[128,3584]{1,0:T(8,128)} %get-tuple-element.8, f32[128,3584]{1,0:T(8,128)} %get-tuple-element.10), kind=kLoop, calls=%fused_computation.7 | loop fusion | flops 5963776 | bytes 7340032 | tf_op jit(solution)/shard_map/convert_element_type | solution.py:11
  208.8 9.9 %fusion.8 = f32[128,2048]{1,0:T(8,128)S(1)} fusion(bf16[128,3584]{1,0:T(8,128)(2,1)S(1)} %get-tuple-element.12, bf16[2048,3584]{1,0:T(8,128)(2,1)} %param.7), kind=kOutput, calls=%fused_computation.15 | convolution fusion | flops 1879048192 | bytes 16646144 | tf_op jit(solution)/shard_map/dot_general | solution.py:40
  218.7 7.6 %fusion = bf16[2048,3584]{0,1:T(8,128)(2,1)} fusion(bf16[128,3584]{1,0:T(8,128)(2,1)S(1)} %get-tuple-element.12, bf16[128,2048]{1,0:T(8,128)(2,1)S(1)} %all_gather.7), kind=kOutput, calls=%fused_computation.3 | convolution fusion | flops 1886388224 | bytes 16121856 | tf_op jit(solution)/shard_map/dot_general | solution.py:34
  226.3 10.9 %convolution_add_fusion = f32[128,2048]{1,0:T(8,128)} fusion(f32[128,2048]{1,0:T(8,128)S(1)} %fusion.8, bf16[128,3584]{1,0:T(8,128)(2,1)S(1)} %get-tuple-element.11, bf16[2048,3584]{1,0:T(8,128)(2,1)} %param.8), kind=kOutput, calls=%fused_computation.5 | convolution fusion | flops 1879310336 | bytes 17694720 | tf_op jit(solution)/shard_map/dot_general | solution.py:45
  237.2 0.0 reduce-scatter.2.cloned.1.call-update
  237.2 18.7 %copy.9 = bf16[2048,3584]{1,0:T(8,128)(2,1)} copy(bf16[2048,3584]{0,1:T(8,128)(2,1)} %fusion) | data formatting | bytes 29360128
  255.9 7.6 %fusion.1 = bf16[2048,3584]{0,1:T(8,128)(2,1)} fusion(bf16[128,3584]{1,0:T(8,128)(2,1)S(1)} %get-tuple-element.11, bf16[128,2048]{1,0:T(8,128)(2,1)S(1)} %all_gather.7), kind=kOutput, calls=%fused_computation.4 | convolution fusion | flops 1886388224 | bytes 16121856 | tf_op jit(solution)/shard_map/dot_general | solution.py:37
  263.4 0.0 copy-start.1
  263.4 18.8 %copy.10 = bf16[2048,3584]{1,0:T(8,128)(2,1)} copy(bf16[2048,3584]{0,1:T(8,128)(2,1)} %fusion.1) | data formatting | bytes 29360128
  282.2 0.0 copy-done.1
  282.2 9.1 %convolution_convert_fusion = bf16[3584,2048]{1,0:T(8,128)(2,1)} fusion(bf16[128,2048]{1,0:T(8,128)(2,1)S(1)} %all_gather.6, f32[128,3584]{1,0:T(8,128)} %get-tuple-element.10, f32[128,3584]{1,0:T(8,128)S(1)} %copy-done.1), kind=kOutput, calls=%fused_computation | convolution fusion | flops 1889140736 | bytes 18874368 | tf_op jit(solution)/shard_map/dot_general | solution.py:31
  291.3 9.7 %reduce-scatter.2.cloned.1.call-done = f32[16,2048]{1,0:T(8,128)} async-done(((f32[128,2048]{1,0:T(8,128)}), f32[16,2048]{1,0:T(8,128)}) %reduce-scatter.2.cloned.1.call-update) | async-done | bytes 131088 | tf_op jit(solution)/shard_map/reduce_scatter | solution.py:43
  301.0 1.5 convert_element_type.29
Async XLA Ops:
  7.2 198.1 %all-reduce.3.cloned.1.call-start = ((), (), s32[]{:S(2)}) async-start(), calls=%async_computation.2 | async-start | bytes 11010048 | tf_op jit(solution)/shard_map/psum | solution.py:29
  71.8 10.0 %copy-start = (bf16[2048,3584]{1,0:T(8,128)(2,1)S(1)}, bf16[2048,3584]{1,0:T(8,128)(2,1)}, u32[]{:S(2)}) copy-start(bf16[2048,3584]{1,0:T(8,128)(2,1)} %param.8) | copy-start | bytes 44040196
  96.6 204.4 %reduce-scatter.2.cloned.1.call-start = ((), (), s32[]{:S(2)}) async-start(), calls=%async_computation.1 | async-start | bytes 1179648 | tf_op jit(solution)/shard_map/reduce_scatter | solution.py:43
  263.4 18.8 %copy-start.1 = (f32[128,3584]{1,0:T(8,128)S(1)}, f32[128,3584]{1,0:T(8,128)}, u32[]{:S(2)}) copy-start(f32[128,3584]{1,0:T(8,128)} %get-tuple-element.8) | copy-start | bytes 5505028
Sparse Core Ops, SparseCore 0:
  96.7 108.4 all-reduce.2
  237.3 63.6 reduce-scatter.1
where the time goes:
time: 311 us; the launch traced here: 309 us
  waiting for transfers between devices  118 us (38%)
  matrix products  68.4 us (22%)
  blocking collectives  64.6 us (21%)
  local copies, waits for them, and re-layouts  38.9 us (13%)
  between operations  14.1 us (5%)
  other arithmetic  5.1 us (2%)
    psum x1, waiting for transfers between devices, shards(): gate, up, grad_hidden = lax.psum((part_gate, part_up, part_hidden), 'mod')  108 us
    unnamed x6, local copies, waits for them, and re-layouts  38.9 us
    all_gather x1, blocking collectives, shards(): lax.all_gather(tokens, 'hid', axis=0, tiled=True)  33.2 us
    all_gather x1, blocking collectives, shards(): lax.all_gather(grad_output, 'hid', axis=0, tiled=True)  31.4 us
    dot_general x1, matrix products, shards(): lax.dot_general(cotangent, down_weight, contract_cols, preferred_element_...  11.3 us
    dot_general x1, matrix products, shards(): lax.dot_general(up_back, up_weight, contract_cols, preferred_element_type...  10.9 us
    dot_general x1, matrix products, shards(): lax.dot_general(gate_back, gate_weight, contract_cols, preferred_element_...  9.93 us
    reduce_scatter x1, waiting for transfers between devices, shards(): lax.psum_scatter(total + lax.dot_general(up_back, up_weight, contract_col...  9.67 us
  transfers between devices with their start and end apart: 2, of which 2 were waited for; matrix products, arithmetic and copies ran while one was open for 17% of the time, Pallas kernels for 0%

commit v1 on v0

v1 whole, which is shorter than its diff:
```python
import functools

import jax
import jax.numpy as jnp
from jax import lax
from jax.experimental import pallas as pl
from jax.experimental.pallas import tpu as pltpu
from jax.sharding import PartitionSpec as P

F32 = jnp.float32
BF16 = jnp.bfloat16
ROWS = (((1,), (0,)), ((), ()))
COLS = (((1,), (1,)), ((), ()))
GATE_EDGES = (0, 6, 8, 11, 13, 14)
DOWN_EDGES = (0, 0, 6, 8, 11, 14)
SPAN_EDGES = (0, 6, 11, 14)
ANYWHERE = pl.BlockSpec(memory_space=pl.ANY)
RESIDENT = pl.BlockSpec(memory_space=pltpu.VMEM)


def params(mib):
    return pltpu.CompilerParams(vmem_limit_bytes=mib * 2**20)


def cost(macs, nbytes, scale=1):
    return pl.CostEstimate(
        flops=2 * macs // scale, bytes_accessed=nbytes // scale, transcendentals=0
    )


def pinned(weight):
    return pltpu.with_memory_space_constraint(weight, pltpu.HBM)


def forward_kernel(jobs, tile, kinds, *refs):
    n = len(kinds)
    rows = dict(zip(sorted({kind for kind, _ in kinds}), refs))
    weights = dict(zip(kinds, refs[len(rows) : len(rows) + n]))
    keep, send, tall, wide, sems = refs[-5:]
    half = keep.shape[0]
    steps, used = [], [0, 0]
    for (kind, name), first, tiles in jobs:
        for i in range(tiles):
            take = pl.ds((first + i) * tile, tile)
            down = int(kind == "g")
            source = weights[(kind, name)].at[(take,) if down else (slice(None), take)]
            target = (tall, wide)[down].at[used[down]]
            used[down] += 1
            steps.append((kind, target, pltpu.make_async_copy(source, target, sems.at[len(steps)])))
    for _, _, copy in steps:
        copy.start()
    for i, (kind, target, copy) in enumerate(steps):
        copy.wait()
        value = lax.dot_general(
            rows[kind][...],
            target[...],
            ROWS if kind == "x" else COLS,
            preferred_element_type=F32,
        )
        put = pl.ds(i * tile, tile)
        keep[:, put] = value[:half]
        send[:, put] = value[half:].astype(BF16)


def forward_part(rows, weights, jobs, tile, after=()):
    kinds = sorted({key for key, _, _ in jobs})
    used = [rows[kind] for kind in sorted({kind for kind, _ in kinds})]
    t, d = used[0].shape
    n_wide = sum(tiles for key, _, tiles in jobs if key[0] == "g")
    n_tall = sum(tiles for key, _, tiles in jobs if key[0] == "x")
    total = (n_wide + n_tall) * tile
    return pl.pallas_call(
        functools.partial(forward_kernel, jobs, tile, kinds),
        in_specs=[RESIDENT] * len(used) + [ANYWHERE] * (len(kinds) + len(after)),
        out_specs=[RESIDENT] * 2,
        out_shape=[
            jax.ShapeDtypeStruct((t // 2, total), F32),
            jax.ShapeDtypeStruct((t // 2, total), BF16),
        ],
        scratch_shapes=[
            pltpu.VMEM((max(n_tall, 1), d, tile), BF16),
            pltpu.VMEM((max(n_wide, 1), tile, d), BF16),
            pltpu.SemaphoreType.DMA((n_tall + n_wide,)),
        ],
        compiler_params=params(28),
        cost_estimate=cost(2 * t * d * total, 2 * d * total, 32),
        name="forward_part",
    )(*used, *[weights[key] for key in kinds], *after)


def step_of(d):
    return 512 if d % 512 == 0 else d


def joined(mine, peer, slot):
    return jnp.concatenate([mine[slot], peer[slot]], axis=0)


def input_kernel(has_prev, first, *refs):
    mine, peer, wg, wu, *others = refs
    prev = others[0]
    out, gate_buf, up_buf, sems = refs[-4:]
    step = step_of(out.shape[1])
    parts = [pl.ds(at, step) for at in range(0, out.shape[1], step)]
    cols = pl.ds(first, mine.shape[2])
    copies = [
        (
            pltpu.make_async_copy(wg.at[part, cols], gate_buf.at[part], sems.at[0, i]),
            pltpu.make_async_copy(wu.at[part, cols], up_buf.at[part], sems.at[1, i]),
        )
        for i, part in enumerate(parts)
    ]
    for pair in copies:
        for copy in pair:
            copy.start()
    gb = joined(mine, peer, 1)
    ub = joined(mine, peer, 2)
    for part, pair in zip(parts, copies):
        pair[0].wait()
        value = lax.dot_general(gb, gate_buf[part, :], COLS, preferred_element_type=F32)
        pair[1].wait()
        value += lax.dot_general(ub, up_buf[part, :], COLS, preferred_element_type=F32)
        out[:, part] = value + prev[:, part] if has_prev else value


def input_part(prev, mine, peer, wg, wu, first, after):
    t, d, span = 2 * mine.shape[1], wg.shape[0], mine.shape[2]
    has_prev = prev is not None
    return pl.pallas_call(
        functools.partial(input_kernel, has_prev, first),
        in_specs=[RESIDENT] * 2
        + [ANYWHERE] * 2
        + [RESIDENT] * int(has_prev)
        + [ANYWHERE] * len(after),
        out_specs=RESIDENT,
        out_shape=jax.ShapeDtypeStruct((t, d), F32),
        scratch_shapes=[
            pltpu.VMEM((d, span), BF16),
            pltpu.VMEM((d, span), BF16),
            pltpu.SemaphoreType.DMA((2, d // step_of(d))),
        ],
        compiler_params=params(28),
        cost_estimate=cost(2 * t * d * span, 4 * d * span),
        name="input_part",
    )(mine, peer, wg, wu, *([prev] if has_prev else []), *after)


def weight_kernel(firsts, tile, *refs):
    n = len(firsts)
    x, g = refs[:2]
    acts = [(refs[2 + 2 * i], refs[3 + 2 * i]) for i in range(n)]
    grad_gate, grad_up, grad_down, xt, gate_buf, up_buf, down_buf, sems = refs[-8:]
    d = x.shape[1]
    step = step_of(d)
    xt[...] = x[...].T
    copies = []

    def out(source, target):
        copy = pltpu.make_async_copy(source, target, sems.at[len(copies)])
        copy.start()
        copies.append(copy)

    start = 0
    for first, (mine, peer) in zip(firsts, acts):
        span = mine.shape[2]
        held, cols = pl.ds(start, span), pl.ds(first, span)
        gb = joined(mine, peer, 1)
        ub = joined(mine, peer, 2)
        ht = joined(mine, peer, 0).T
        for at in range(0, d, step):
            part = pl.ds(at, step)
            rows = xt[part, :]
            for value, buf, grad in ((gb, gate_buf, grad_gate), (ub, up_buf, grad_up)):
                buf[part, held] = lax.dot_general(
                    rows, value, ROWS, preferred_element_type=F32
                ).astype(BF16)
                out(buf.at[part, held], grad.at[part, cols])
        for at in range(0, span, tile):
            part = pl.ds(start + at, tile)
            down_buf[part, :] = lax.dot_general(
                ht[at : at + tile], g[...], ROWS, preferred_element_type=F32
            ).astype(BF16)
            out(down_buf.at[part], grad_down.at[pl.ds(first + at, tile)])
        start += span
    for copy in copies:
        copy.wait()


def weight_part(prev, x, g, acts, firsts, tile, hidden, after):
    t, d = x.shape
    prev = [] if prev is None else list(prev)
    spans = [mine.shape[2] for mine, _ in acts]
    total = sum(spans)
    n_copies = len(acts) * 2 * (d // step_of(d)) + total // tile
    flat = [array for pair in acts for array in pair]
    return pl.pallas_call(
        functools.partial(weight_kernel, firsts, tile),
        in_specs=[RESIDENT] * (2 + len(flat)) + [ANYWHERE] * (len(prev) + len(after)),
        out_specs=[ANYWHERE] * 3,
        out_shape=[
            jax.ShapeDtypeStruct((d, hidden), BF16),
            jax.ShapeDtypeStruct((d, hidden), BF16),
            jax.ShapeDtypeStruct((hidden, d), BF16),
        ],
        scratch_shapes=[
            pltpu.VMEM((d, t), BF16),
            pltpu.VMEM((d, total), BF16),
            pltpu.VMEM((d, total), BF16),
            pltpu.VMEM((total, d), BF16),
            pltpu.SemaphoreType.DMA((n_copies,)),
        ],
        input_output_aliases={2 + len(flat) + i: i for i in range(len(prev))},
        compiler_params=params(34),
        cost_estimate=cost(3 * t * d * total, 6 * d * total),
        name="weight_part",
    )(x, g, *flat, *prev, *after)


def add_kernel(keep, got, *refs):
    refs[-1][...] = (keep[...] + got[...].astype(F32)).astype(BF16)


def add_part(keep, got, after=()):
    return pl.pallas_call(
        add_kernel,
        in_specs=[RESIDENT] * 2 + [ANYWHERE] * len(after),
        out_specs=RESIDENT,
        out_shape=jax.ShapeDtypeStruct(keep.shape, BF16),
        compiler_params=params(16),
        cost_estimate=cost(keep.size, 8 * keep.size),
        name="add_part",
    )(keep, got, *after)


def swiglu_kernel(places, tile, n_sums, *refs):
    out = refs[-1]
    for i, place in enumerate(places):
        gate, up, grad_hidden = (
            refs[which * n_sums][:, pl.ds(first, tile)]
            + sum(
                refs[which * n_sums + j][:, pl.ds(first, tile)].astype(F32)
                for j in range(1, n_sums)
            )
            for which, first in place
        )
        sigmoid_gate = jax.nn.sigmoid(gate)
        active = gate * sigmoid_gate
        slope = sigmoid_gate * (1.0 + gate * (1.0 - sigmoid_gate))
        part = pl.ds(i * tile, tile)
        out[0, :, part] = (active * up).astype(BF16)
        out[1, :, part] = (grad_hidden * up * slope).astype(BF16)
        out[2, :, part] = (grad_hidden * active).astype(BF16)


def swiglu_part(places, pieces, tile, after=()):
    width = len(places) * tile
    flat = [array for piece in pieces for array in piece]
    rows = flat[0].shape[0]
    return pl.pallas_call(
        functools.partial(swiglu_kernel, places, tile, len(pieces[0])),
        in_specs=[RESIDENT] * len(flat) + [ANYWHERE] * len(after),
        out_specs=RESIDENT,
        out_shape=jax.ShapeDtypeStruct((3, rows, width), BF16),
        compiler_params=params(20),
        cost_estimate=cost(20 * rows * width, 14 * rows * width),
        name="swiglu_part",
    )(*flat, *after)


def shards(n_hid, n_mod, tokens, grad_output, gate_weight, up_weight, down_weight):
    hidden = gate_weight.shape[1]
    rows = tokens.shape[0]
    far = n_hid // 2
    core = lax.axis_index("mod") % 2

    def swap(value, axis, size, bit):
        return lax.ppermute(value, axis, [(i ^ bit, i) for i in range(size)])

    def from_far(value, k):
        return swap(value, "hid", n_hid, 2 * k)

    def near(value):
        return swap(value, "hid", n_hid, 1)

    def other_core(value):
        return swap(value, "mod", n_mod, 1)

    def along(block):
        return [block] + [from_far(block, k) for k in range(1, far)]

    def across(column):
        own = jnp.concatenate(column, axis=0)
        theirs = near(own)
        return jnp.concatenate(
            [jnp.where(core == 0, own, theirs), jnp.where(core == 0, theirs, own)], axis=0
        )

    column = along(tokens)
    held, _ = lax.optimization_barrier((grad_output, column))
    x = across(column)
    g = across(along(held))
    gate_key, up_key, down_key = ("x", 0), ("x", 1), ("g", 2)
    weights = {
        gate_key: pinned(gate_weight),
        up_key: pinned(up_weight),
        down_key: pinned(down_weight),
    }

    tile = next((n for n in (256, 128) if hidden % n == 0), hidden)
    n_tiles = hidden // tile

    def ranges(edges):
        bounds = [round(e * n_tiles / edges[-1]) for e in edges]
        return list(zip(bounds[:-1], bounds[1:]))

    spans = [(a, b) for a, b in ranges(SPAN_EDGES) if b > a]

    def exchanged(jobs, after=()):
        keep, send = forward_part({"x": x, "g": g}, weights, jobs, tile, after)
        got = other_core(send)
        narrow = add_part(keep, got)
        others = [swap(narrow, "mod", n_mod, 2 * k) for k in range(1, n_mod // 2)]
        return (keep, got, *others), send, narrow

    n = len(spans)
    pieces, sends, narrows = [], [], []
    where = {gate_key: [], up_key: [], down_key: []}
    for (a, b), (c, d) in zip(ranges(GATE_EDGES), ranges(DOWN_EDGES)):
        jobs = [(gate_key, a, b - a), (up_key, a, b - a), (down_key, c, d - c)]
        jobs = [job for job in jobs if job[2]]
        if not jobs:
            continue
        k, at = len(pieces), 0
        for key, _, tiles in jobs:
            where[key] += [(k, at + i * tile) for i in range(tiles)]
            at += tiles * tile
        after = narrows[-1:] + [piece[-1] for piece in pieces[-2:-1]]
        for held, value in zip((pieces, sends, narrows), exchanged(jobs, after)):
            held.append(value)

    def act(i, after=()):
        places = list(zip(*(where[key][slice(*spans[i])] for key in (gate_key, up_key, down_key))))
        used = sorted({which for place in places for which, _ in place})
        local = [[(used.index(which), first) for which, first in place] for place in places]
        mine = swiglu_part(local, [pieces[which] for which in used], tile, after)
        return mine, other_core(mine)

    def weight_grads(prev, group, after):
        return weight_part(
            prev,
            x,
            g,
            [acts[j] for j in group],
            [spans[j][0] * tile for j in group],
            tile,
            hidden,
            after,
        )

    def tokens_grad(prev, i, after):
        mine, peer = acts[i]
        first = spans[i][0] * tile
        return input_part(prev, mine, peer, weights[gate_key], weights[up_key], first, after)

    acts = [act(0, sends[-1:])]
    waited = [piece[-1] for piece in pieces[-2:-1]]
    total = tokens_grad(None, 0, narrows[-1:] + waited)
    for i in range(1, n):
        acts.append(act(i, [total] if i == 1 else [acts[-1][0]]))
    for i in range(1, n):
        total = tokens_grad(total, i, [acts[-1][0]])

    half = total.shape[0] // 2
    top, bottom = total[:half], total[half:]
    own = jnp.where(core == 0, top, bottom)
    theirs = jnp.where(core == 0, bottom, top).astype(BF16)
    own = own + near(theirs).astype(F32)
    result = own[:rows]
    for k in range(1, far):
        block = own[k * rows : (k + 1) * rows].astype(BF16)
        result = result + from_far(block, k).astype(F32)

    grads = None
    for group in ([0], list(range(1, n))):
        if group:
            grads = weight_grads(grads, group, [theirs])
    grad_gate, grad_up, grad_down = grads
    return (result.astype(BF16), grad_gate, grad_up, grad_down)


def solution(mesh):
    placed = (P("hid", "mod"), P("hid", "mod"), P("mod", "hid"), P("mod", "hid"), P("hid", "mod"))
    return jax.shard_map(
        functools.partial(shards, mesh.shape["hid"], mesh.shape["mod"]),
        mesh=mesh,
        in_specs=placed,
        out_specs=(P("hid", "mod"), P("mod", "hid"), P("mod", "hid"), P("hid", "mod")),
        check_vma=False,
    )
```

time: 311 us -> 121 us (0.39)
  waiting for transfers between devices: 118 us -> 28.4 us
  matrix products: 68.4 us -> 0 us
  blocking collectives: 64.6 us -> 0 us
  Pallas kernels: 0 us -> 62.3 us
  local copies, waits for them, and re-layouts: 38.9 us -> 1.81 us
  starting transfers between devices: 0.26 us -> 25.7 us
  between operations: 14.1 us -> 0.96 us
  other arithmetic: 5.1 us -> 1.2 us
    psum x1 -> x0, waiting for transfers between devices: 108 us -> none  [shards(): gate, up, grad_hidden = lax.psum((part_gate, part_up, part_hidden), 'mod')]
    dot_general x8 -> x0, matrix products: 68.4 us -> none  [the longest x1 11.3 us: shards(): lax.dot_general(cotangent, down_weight, contract_cols, preferred_element_...]
    all_gather x2 -> x0, blocking collectives: 64.6 us -> none  [the longest x1 33.2 us: shards(): lax.all_gather(tokens, 'hid', axis=0, tiled=True)]
    pallas_call x0 -> x18, Pallas kernels: none -> 62.3 us  [the longest x5 27.7 us: forward_part(): pl.pallas_call(functools.partial(forward_kernel, jobs, tile, kinds), in_s...]
    unnamed x6, local copies, waits for them, and re-layouts: 38.9 us -> 1.78 us
    ppermute x0 -> x25, waiting for transfers between devices: none -> 28.4 us  [swap(): return lax.ppermute(value, axis, [(i ^ bit, i) for i in range(size)])]
    ppermute x0 -> x25, starting transfers between devices: none -> 25.7 us  [swap(): return lax.ppermute(value, axis, [(i ^ bit, i) for i in range(size)])]
    reduce_scatter x1 -> x0, waiting for transfers between devices: 9.67 us -> none  [shards(): lax.psum_scatter(total + lax.dot_general(up_back, up_weight, contract_col...]
  transfers between devices with their start and end apart: 2 -> 25, of which waited for: 2 -> 13; matrix products, arithmetic and copies ran while one was open for 17% -> 2% of each run, Pallas kernels for 0% -> 39%
where the time goes in v1:
time: 121 us; the launch traced here: 120 us
  Pallas kernels  62.3 us (51%)
  waiting for transfers between devices  28.4 us (23%)
  starting transfers between devices  25.7 us (21%)
  local copies, waits for them, and re-layouts  1.81 us (1%)
    ppermute x25, waiting for transfers between devices, swap(): return lax.ppermute(value, axis, [(i ^ bit, i) for i in range(size)])  28.4 us
    pallas_call x5, Pallas kernels, forward_part(): pl.pallas_call(functools.partial(forward_kernel, jobs, tile, kinds), in_s...  27.7 us
    ppermute x25, starting transfers between devices, swap(): return lax.ppermute(value, axis, [(i ^ bit, i) for i in range(size)])  25.7 us
    pallas_call x3, Pallas kernels, input_part(): pl.pallas_call(functools.partial(input_kernel, has_prev, first), in_specs...  17 us
    pallas_call x2, Pallas kernels, weight_part(): pl.pallas_call(functools.partial(weight_kernel, firsts, tile), in_specs=[...  16.4 us
  transfers between devices with their start and end apart: 25, of which 13 were waited for; matrix products, arithmetic and copies ran while one was open for 2% of the time, Pallas kernels for 39%

profile of v1, /device:TPU:0, one launch (start us, length us, event | category | flops | bytes accessed | tf_op | source)
XLA Modules:
  0.0 120.4 jit_solution(5637766640848113448)
XLA Ops:
  0.6 5.1 %collective-permute-start.2 = (bf16[16,2048]{1,0:T(8,128)(2,1)}, bf16[16,2048]{1,0:T(8,128)(2,1)S(1)}, u32[]{:S(2)}, u32[]{:S(2)}) collective-permute-start(bf16[16,2048]{1,0:T(8,128)(2,1)} %param.5), channel_id=1, source_target_pairs={{24,0},{28,4},{16,8},{20,12},{8,16},{12,20},{0,24},{4,28},{25,1},{... | collective-permute-start | bytes 196616 | tf_op jit(solution)/shard_map/ppermute | solution.py:277
  7.3 1.3 %collective-permute-done.2 = bf16[16,2048]{1,0:T(8,128)(2,1)S(1)} collective-permute-done((bf16[16,2048]{1,0:T(8,128)(2,1)}, bf16[16,2048]{1,0:T(8,128)(2,1)S(1)}, u32[]{:S(2)}, u32[]{:S(2)}) %collective-permute-start.2) | collective-permute-done | bytes 65568 | tf_op jit(solution)/shard_map/ppermute | solution.py:277
  8.6 3.0 %collective-permute-done.1 = bf16[16,2048]{1,0:T(8,128)(2,1)S(1)} collective-permute-done((bf16[16,2048]{1,0:T(8,128)(2,1)}, bf16[16,2048]{1,0:T(8,128)(2,1)S(1)}, u32[]{:S(2)}, u32[]{:S(2)}) %collective-permute-start.1) | collective-permute-done | bytes 65568 | tf_op jit(solution)/shard_map/ppermute | solution.py:277
  11.6 2.7 %collective-permute-start.5 = (bf16[16,2048]{1,0:T(8,128)(2,1)}, bf16[16,2048]{1,0:T(8,128)(2,1)S(1)}, u32[]{:S(2)}, u32[]{:S(2)}) collective-permute-start(bf16[16,2048]{1,0:T(8,128)(2,1)} %param.6), channel_id=1, source_target_pairs={{24,0},{28,4},{16,8},{20,12},{8,16},{12,20},{0,24},{4,28},{25,1},{... | collective-permute-start | bytes 196616 | tf_op jit(solution)/shard_map/ppermute | solution.py:277
  14.3 1.7 %collective-permute-start.3 = (bf16[16,2048]{1,0:T(8,128)(2,1)}, bf16[16,2048]{1,0:T(8,128)(2,1)S(1)}, u32[]{:S(2)}, u32[]{:S(2)}) collective-permute-start(bf16[16,2048]{1,0:T(8,128)(2,1)} %param.6), channel_id=1, source_target_pairs={{8,0},{12,4},{0,8},{4,12},{24,16},{28,20},{16,24},{20,28},{9,1},{1... | collective-permute-start | bytes 196616 | tf_op jit(solution)/shard_map/ppermute | solution.py:277
  16.9 1.6 %collective-permute-start.7 = (bf16[64,2048]{1,0:T(8,128)(2,1)S(1)}, bf16[64,2048]{1,0:T(8,128)(2,1)S(1)}, u32[]{:S(2)}, u32[]{:S(2)}) collective-permute-start(bf16[64,2048]{1,0:T(8,128)(2,1)S(1)} %constant_dynamic-update-slice_fusion.4), channel_id=1, source_target_pairs={{4,0},{0,4},{12,8},{8,12},{20,16},{16,20},{28,24},{24,28},{5,1},{1... | collective-permute-start | bytes 786440 | tf_op jit(solution)/shard_map/ppermute | solution.py:277
  19.2 1.6 %collective-permute-done.4 = bf16[16,2048]{1,0:T(8,128)(2,1)S(1)} collective-permute-done((bf16[16,2048]{1,0:T(8,128)(2,1)}, bf16[16,2048]{1,0:T(8,128)(2,1)S(1)}, u32[]{:S(2)}, u32[]{:S(2)}) %collective-permute-start.4) | collective-permute-done | bytes 65568 | tf_op jit(solution)/shard_map/ppermute | solution.py:277
  20.8 1.6 %collective-permute-start.6 = (bf16[64,2048]{1,0:T(8,128)(2,1)S(1)}, bf16[64,2048]{1,0:T(8,128)(2,1)S(1)}, u32[]{:S(2)}, u32[]{:S(2)}) collective-permute-start(bf16[64,2048]{1,0:T(8,128)(2,1)S(1)} %constant_dynamic-update-slice_fusion), channel_id=1, source_target_pairs={{4,0},{0,4},{12,8},{8,12},{20,16},{16,20},{28,24},{24,28},{5,1},{1... | collective-permute-start | bytes 786440 | tf_op jit(solution)/shard_map/ppermute | solution.py:277
  22.4 2.6 %collective-permute-done.7 = bf16[64,2048]{1,0:T(8,128)(2,1)S(1)} collective-permute-done((bf16[64,2048]{1,0:T(8,128)(2,1)S(1)}, bf16[64,2048]{1,0:T(8,128)(2,1)S(1)}, u32[]{:S(2)}, u32[]{:S(2)}) %collective-permute-start.7) | collective-permute-done | bytes 262176 | tf_op jit(solution)/shard_map/ppermute | solution.py:277
  25.1 6.4 %forward_part.5 = (f32[64,3072]{1,0:T(8,128)S(1)}, bf16[64,3072]{1,0:T(8,128)(2,1)S(1)}) custom-call(bf16[128,2048]{1,0:T(8,128)(2,1)S(1)} %pad_maximum_fusion.1.refs_0_.refs_1_, bf16[2048,3584]{1,0:T(8,128)(2,1)} %refs_2_.15, bf16[2048,3584]{1,0:T(8,128)(2,1)} %refs_3_.13), custom_call_target="tpu_custom_call" | custom-call | flops 100663296 | bytes 393216 | tf_op jit(solution)/shard_map/forward_part/pallas_call | solution.py:72
  31.6 1.6 %collective-permute-done.8.got.refs_1_ = bf16[64,3072]{1,0:T(8,128)(2,1)S(1)} collective-permute-done((bf16[64,3072]{1,0:T(8,128)(2,1)S(1)}, bf16[64,3072]{1,0:T(8,128)(2,1)S(1)}, u32[]{:S(2)}, u32[]{:S(2)}) %collective-permute-start.8) | collective-permute-done | bytes 393248 | tf_op jit(solution)/shard_map/ppermute | solution.py:277
  33.4 1.7 %collective-permute-start.10 = (bf16[64,3072]{1,0:T(8,128)(2,1)S(1)}, bf16[64,3072]{1,0:T(8,128)(2,1)S(1)}, u32[]{:S(2)}, u32[]{:S(2)}) collective-permute-start(bf16[64,3072]{1,0:T(8,128)(2,1)S(1)} %add_part.5.refs_5_), channel_id=1, source_target_pairs={{2,0},{3,1},{0,2},{1,3},{6,4},{7,5},{4,6},{5,7},{10,8},{11,9},{8,1... | collective-permute-start | bytes 1179656 | tf_op jit(solution)/shard_map/ppermute | solution.py:277
  35.1 7.2 %forward_part.6 = (f32[64,2560]{1,0:T(8,128)S(1)}, bf16[64,2560]{1,0:T(8,128)(2,1)S(1)}) custom-call(bf16[128,2048]{1,0:T(8,128)(2,1)S(1)} %pad_maximum_fusion.refs_0_.refs_1_, bf16[128,2048]{1,0:T(8,128)(2,1)S(1)} %pad_maximum_fusion.1.refs_0_.refs_1_, bf16[3584,2048]{1,0:T(8,128)(2,1)} %refs_2_.12, bf16[2048,3584]{1,0:T(8,128)(2,1)} %refs_2_.15, ...), custom_call_target="tpu_custom_call" | custom-call | flops 83886080 | bytes 327680 | tf_op jit(solution)/shard_map/forward_part/pallas_call | solution.py:72
  42.4 1.6 %collective-permute-done.9.got.refs_4_.refs_1_ = bf16[64,2560]{1,0:T(8,128)(2,1)S(1)} collective-permute-done((bf16[64,2560]{1,0:T(8,128)(2,1)S(1)}, bf16[64,2560]{1,0:T(8,128)(2,1)S(1)}, u32[]{:S(2)}, u32[]{:S(2)}) %collective-permute-start.9) | collective-permute-done | bytes 327712 | tf_op jit(solution)/shard_map/ppermute | solution.py:277
  44.6 5.2 %forward_part.7 = (f32[64,2048]{1,0:T(8,128)S(1)}, bf16[64,2048]{1,0:T(8,128)(2,1)S(1)}) custom-call(bf16[128,2048]{1,0:T(8,128)(2,1)S(1)} %pad_maximum_fusion.refs_0_.refs_1_, bf16[128,2048]{1,0:T(8,128)(2,1)S(1)} %pad_maximum_fusion.1.refs_0_.refs_1_, bf16[3584,2048]{1,0:T(8,128)(2,1)} %refs_2_.12, bf16[2048,3584]{1,0:T(8,128)(2,1)} %refs_2_.15, ...), custom_call_target="tpu_custom_call" | custom-call | flops 67108864 | bytes 262144 | tf_op jit(solution)/shard_map/forward_part/pallas_call | solution.py:72
  49.9 1.5 %collective-permute-done.11.got.refs_4_ = bf16[64,2048]{1,0:T(8,128)(2,1)S(1)} collective-permute-done((bf16[64,2048]{1,0:T(8,128)(2,1)S(1)}, bf16[64,2048]{1,0:T(8,128)(2,1)S(1)}, u32[]{:S(2)}, u32[]{:S(2)}) %collective-permute-start.11) | collective-permute-done | bytes 262176 | tf_op jit(solution)/shard_map/ppermute | solution.py:277
  51.5 1.7 %collective-permute-start.15 = (bf16[64,2048]{1,0:T(8,128)(2,1)S(1)}, bf16[64,2048]{1,0:T(8,128)(2,1)S(1)}, u32[]{:S(2)}, u32[]{:S(2)}) collective-permute-start(bf16[64,2048]{1,0:T(8,128)(2,1)S(1)} %add_part.7.refs_5_), channel_id=1, source_target_pairs={{2,0},{3,1},{0,2},{1,3},{6,4},{7,5},{4,6},{5,7},{10,8},{11,9},{8,1... | collective-permute-start | bytes 786440 | tf_op jit(solution)/shard_map/ppermute | solution.py:277
  53.9 4.9 %forward_part.8 = (f32[64,1792]{1,0:T(8,128)S(1)}, bf16[64,1792]{1,0:T(8,128)(2,1)S(1)}) custom-call(bf16[128,2048]{1,0:T(8,128)(2,1)S(1)} %pad_maximum_fusion.refs_0_.refs_1_, bf16[128,2048]{1,0:T(8,128)(2,1)S(1)} %pad_maximum_fusion.1.refs_0_.refs_1_, bf16[3584,2048]{1,0:T(8,128)(2,1)} %refs_2_.12, bf16[2048,3584]{1,0:T(8,128)(2,1)} %refs_2_.15, ...), custom_call_target="tpu_custom_call" | custom-call | flops 58720256 | bytes 229376 | tf_op jit(solution)/shard_map/forward_part/pallas_call | solution.py:72
  58.9 1.5 %collective-permute-done.13.got.refs_7_.refs_1_ = bf16[64,1792]{1,0:T(8,128)(2,1)S(1)} collective-permute-done((bf16[64,1792]{1,0:T(8,128)(2,1)S(1)}, bf16[64,1792]{1,0:T(8,128)(2,1)S(1)}, u32[]{:S(2)}, u32[]{:S(2)}) %collective-permute-start.13) | collective-permute-done | bytes 229408 | tf_op jit(solution)/shard_map/ppermute | solution.py:277
  60.4 4.0 %forward_part.9 = (f32[64,1280]{1,0:T(8,128)S(1)}, bf16[64,1280]{1,0:T(8,128)(2,1)S(1)}) custom-call(bf16[128,2048]{1,0:T(8,128)(2,1)S(1)} %pad_maximum_fusion.refs_0_.refs_1_, bf16[128,2048]{1,0:T(8,128)(2,1)S(1)} %pad_maximum_fusion.1.refs_0_.refs_1_, bf16[3584,2048]{1,0:T(8,128)(2,1)} %refs_2_.12, bf16[2048,3584]{1,0:T(8,128)(2,1)} %refs_2_.15, ...), custom_call_target="tpu_custom_call" | custom-call | flops 41943040 | bytes 163840 | tf_op jit(solution)/shard_map/forward_part/pallas_call | solution.py:72
  66.4 1.2 %collective-permute-done.16.got.refs_4_ = bf16[64,1280]{1,0:T(8,128)(2,1)S(1)} collective-permute-done((bf16[64,1280]{1,0:T(8,128)(2,1)S(1)}, bf16[64,1280]{1,0:T(8,128)(2,1)S(1)}, u32[]{:S(2)}, u32[]{:S(2)}) %collective-permute-start.16) | collective-permute-done | bytes 163872 | tf_op jit(solution)/shard_map/ppermute | solution.py:277
  67.6 5.4 %collective-permute-done.14.refs_5_.refs_8_.refs_2_ = bf16[64,1792]{1,0:T(8,128)(2,1)S(1)} collective-permute-done((bf16[64,1792]{1,0:T(8,128)(2,1)S(1)}, bf16[64,1792]{1,0:T(8,128)(2,1)S(1)}, u32[]{:S(2)}, u32[]{:S(2)}) %collective-permute-start.14) | collective-permute-done | bytes 229408 | tf_op jit(solution)/shard_map/ppermute | solution.py:277
  73.0 6.9 %input_part.3.refs_9_.refs_4_ = f32[128,2048]{1,0:T(8,128)S(1)} custom-call(bf16[3,64,1536]{2,1,0:T(8,128)(2,1)S(1)} %swiglu_part.3.refs_0_.refs_2_, bf16[3,64,1536]{2,1,0:T(8,128)(2,1)S(1)} %collective-permute-done.18.refs_1_.refs_3_, bf16[2048,3584]{1,0:T(8,128)(2,1)} %refs_2_.15, bf16[2048,3584]{1,0:T(8,128)(2,1)} %refs_3_.13, ...), custom_call_target="tpu_custom_call" | custom-call | flops 1610612736 | bytes 12582912 | tf_op jit(solution)/shard_map/input_part/pallas_call | solution.py:129
  80.3 1.2 collective-permute-start.17
  81.5 5.4 %collective-permute-done.17.refs_5_ = bf16[64,1280]{1,0:T(8,128)(2,1)S(1)} collective-permute-done((bf16[64,1280]{1,0:T(8,128)(2,1)S(1)}, bf16[64,1280]{1,0:T(8,128)(2,1)S(1)}, u32[]{:S(2)}, u32[]{:S(2)}) %collective-permute-start.17) | collective-permute-done | bytes 163872 | tf_op jit(solution)/shard_map/ppermute | solution.py:277
  87.2 6.0 %input_part.4.refs_4_ = f32[128,2048]{1,0:T(8,128)S(1)} custom-call(bf16[3,64,1280]{2,1,0:T(8,128)(2,1)S(1)} %swiglu_part.4.refs_6_.refs_0_.refs_2_, bf16[3,64,1280]{2,1,0:T(8,128)(2,1)S(1)} %collective-permute-done.20.refs_1_.refs_3_, bf16[2048,3584]{1,0:T(8,128)(2,1)} %refs_2_.15, bf16[2048,3584]{1,0:T(8,128)(2,1)} %refs_3_.13, ...), custom_call_target="tpu_custom_call" | custom-call | flops 1342177280 | bytes 10485760 | tf_op jit(solution)/shard_map/input_part/pallas_call | solution.py:129
  93.1 4.2 %input_part.5 = f32[128,2048]{1,0:T(8,128)S(1)} custom-call(bf16[3,64,768]{2,1,0:T(8,128)(2,1)S(1)} %swiglu_part.5.refs_5_.refs_0_.refs_4_, bf16[3,64,768]{2,1,0:T(8,128)(2,1)S(1)} %collective-permute-done.19.refs_1_.refs_5_, bf16[2048,3584]{1,0:T(8,128)(2,1)} %refs_2_.15, bf16[2048,3584]{1,0:T(8,128)(2,1)} %refs_3_.13, f32[128,2048]{1,0:T(8,128)S(1)} %input_part.4.refs_4_, ...), custom_call_target="tpu_custom_call" | custom-call | flops 805306368 | bytes 6291456 | tf_op jit(solution)/shard_map/input_part/pallas_call | solution.py:129
  97.4 1.6 %collective-permute-start.21 = (bf16[64,2048]{1,0:T(8,128)(2,1)S(1)}, bf16[64,2048]{1,0:T(8,128)(2,1)S(1)}, u32[]{:S(2)}, u32[]{:S(2)}) collective-permute-start(bf16[64,2048]{1,0:T(8,128)(2,1)S(1)} %select_convert_fusion.refs_4_.refs_9_), channel_id=1, source_target_pairs={{4,0},{0,4},{12,8},{8,12},{20,16},{16,20},{28,24},{24,28},{5,1},{1... | collective-permute-start | bytes 786440 | tf_op jit(solution)/shard_map/ppermute | solution.py:277
  99.0 7.2 %weight_part.2 = (bf16[2048,3584]{1,0:T(8,128)(2,1)}, bf16[2048,3584]{1,0:T(8,128)(2,1)}, bf16[3584,2048]{1,0:T(8,128)(2,1)}) custom-call(bf16[128,2048]{1,0:T(8,128)(2,1)S(1)} %pad_maximum_fusion.1.refs_0_.refs_1_, bf16[128,2048]{1,0:T(8,128)(2,1)S(1)} %pad_maximum_fusion.refs_0_.refs_1_, bf16[3,64,1536]{2,1,0:T(8,128)(2,1)S(1)} %swiglu_part.3.refs_0_.refs_2_, ...), custom_call_target="tpu_custom_call" | custom-call | flops 2415919104 | bytes 18874368 | tf_op jit(solution)/shard_map/weight_part/pallas_call | solution.py:196
  106.5 1.5 %collective-permute-start.22 = (bf16[16,2048]{1,0:T(8,128)(2,1)S(1)}, bf16[16,2048]{1,0:T(8,128)(2,1)S(1)}, u32[]{:S(2)}, u32[]{:S(2)}) collective-permute-start(bf16[16,2048]{1,0:T(8,128)(2,1)S(1)} %get-tuple-element.44), channel_id=1, source_target_pairs={{8,0},{12,4},{0,8},{4,12},{24,16},{28,20},{16,24},{20,28},{9,1},{1... | collective-permute-start | bytes 196616 | tf_op jit(solution)/shard_map/ppermute | solution.py:277
  108.0 2.0 %collective-permute-start.24 = (bf16[16,2048]{1,0:T(8,128)(2,1)S(1)}, bf16[16,2048]{1,0:T(8,128)(2,1)S(1)}, u32[]{:S(2)}, u32[]{:S(2)}) collective-permute-start(bf16[16,2048]{1,0:T(8,128)(2,1)S(1)} %get-tuple-element.45), channel_id=1, source_target_pairs={{24,0},{28,4},{16,8},{20,12},{8,16},{12,20},{0,24},{4,28},{25,1},{... | collective-permute-start | bytes 196616 | tf_op jit(solution)/shard_map/ppermute | solution.py:277
  110.5 9.2 %weight_part.3 = (bf16[2048,3584]{1,0:T(8,128)(2,1)}, bf16[2048,3584]{1,0:T(8,128)(2,1)}, bf16[3584,2048]{1,0:T(8,128)(2,1)}) custom-call(bf16[128,2048]{1,0:T(8,128)(2,1)S(1)} %pad_maximum_fusion.1.refs_0_.refs_1_, bf16[128,2048]{1,0:T(8,128)(2,1)S(1)} %pad_maximum_fusion.refs_0_.refs_1_, ...), custom_call_target="tpu_custom_call", output_to_operand_aliasing={{0}: (6, {}), {1}: (7, {}), {2}: (8, {})} | custom-call | flops 3221225472 | bytes 25165824 | tf_op jit(solution)/shard_map/weight_part/pallas_call | solution.py:196
  (52 shorter events, 9.2 us)
Async XLA Ops:
  0.6 7.9 %collective-permute-start.2 = (bf16[16,2048]{1,0:T(8,128)(2,1)}, bf16[16,2048]{1,0:T(8,128)(2,1)S(1)}, u32[]{:S(2)}, u32[]{:S(2)}) collective-permute-start(bf16[16,2048]{1,0:T(8,128)(2,1)} %param.5), channel_id=1, source_target_pairs={{24,0},{28,4},{16,8},{20,12},{8,16},{12,20},{0,24},{4,28},{25,1},{... | collective-permute-start | bytes 196616 | tf_op jit(solution)/shard_map/ppermute | solution.py:277
  5.7 5.8 %collective-permute-start.1 = (bf16[16,2048]{1,0:T(8,128)(2,1)}, bf16[16,2048]{1,0:T(8,128)(2,1)S(1)}, u32[]{:S(2)}, u32[]{:S(2)}) collective-permute-start(bf16[16,2048]{1,0:T(8,128)(2,1)} %param.5), channel_id=1, source_target_pairs={{16,0},{20,4},{24,8},{28,12},{0,16},{4,20},{8,24},{12,28},{17,1},{... | collective-permute-start | bytes 196616 | tf_op jit(solution)/shard_map/ppermute | solution.py:277
  5.7 5.8 %collective-permute-start = (bf16[16,2048]{1,0:T(8,128)(2,1)}, bf16[16,2048]{1,0:T(8,128)(2,1)S(1)}, u32[]{:S(2)}, u32[]{:S(2)}) collective-permute-start(bf16[16,2048]{1,0:T(8,128)(2,1)} %param.5), channel_id=1, source_target_pairs={{8,0},{12,4},{0,8},{4,12},{24,16},{28,20},{16,24},{20,28},{9,1},{1... | collective-permute-start | bytes 196616 | tf_op jit(solution)/shard_map/ppermute | solution.py:277
  11.6 9.2 %collective-permute-start.5 = (bf16[16,2048]{1,0:T(8,128)(2,1)}, bf16[16,2048]{1,0:T(8,128)(2,1)S(1)}, u32[]{:S(2)}, u32[]{:S(2)}) collective-permute-start(bf16[16,2048]{1,0:T(8,128)(2,1)} %param.6), channel_id=1, source_target_pairs={{24,0},{28,4},{16,8},{20,12},{8,16},{12,20},{0,24},{4,28},{25,1},{... | collective-permute-start | bytes 196616 | tf_op jit(solution)/shard_map/ppermute | solution.py:277
  14.3 6.5 %collective-permute-start.4 = (bf16[16,2048]{1,0:T(8,128)(2,1)}, bf16[16,2048]{1,0:T(8,128)(2,1)S(1)}, u32[]{:S(2)}, u32[]{:S(2)}) collective-permute-start(bf16[16,2048]{1,0:T(8,128)(2,1)} %param.6), channel_id=1, source_target_pairs={{16,0},{20,4},{24,8},{28,12},{0,16},{4,20},{8,24},{12,28},{17,1},{... | collective-permute-start | bytes 196616 | tf_op jit(solution)/shard_map/ppermute | solution.py:277
  14.3 4.9 %collective-permute-start.3 = (bf16[16,2048]{1,0:T(8,128)(2,1)}, bf16[16,2048]{1,0:T(8,128)(2,1)S(1)}, u32[]{:S(2)}, u32[]{:S(2)}) collective-permute-start(bf16[16,2048]{1,0:T(8,128)(2,1)} %param.6), channel_id=1, source_target_pairs={{8,0},{12,4},{0,8},{4,12},{24,16},{28,20},{16,24},{20,28},{9,1},{1... | collective-permute-start | bytes 196616 | tf_op jit(solution)/shard_map/ppermute | solution.py:277
  16.9 8.1 %collective-permute-start.7 = (bf16[64,2048]{1,0:T(8,128)(2,1)S(1)}, bf16[64,2048]{1,0:T(8,128)(2,1)S(1)}, u32[]{:S(2)}, u32[]{:S(2)}) collective-permute-start(bf16[64,2048]{1,0:T(8,128)(2,1)S(1)} %constant_dynamic-update-slice_fusion.4), channel_id=1, source_target_pairs={{4,0},{0,4},{12,8},{8,12},{20,16},{16,20},{28,24},{24,28},{5,1},{1... | collective-permute-start | bytes 786440 | tf_op jit(solution)/shard_map/ppermute | solution.py:277
  20.8 10.8 %collective-permute-start.6 = (bf16[64,2048]{1,0:T(8,128)(2,1)S(1)}, bf16[64,2048]{1,0:T(8,128)(2,1)S(1)}, u32[]{:S(2)}, u32[]{:S(2)}) collective-permute-start(bf16[64,2048]{1,0:T(8,128)(2,1)S(1)} %constant_dynamic-update-slice_fusion), channel_id=1, source_target_pairs={{4,0},{0,4},{12,8},{8,12},{20,16},{16,20},{28,24},{24,28},{5,1},{1... | collective-permute-start | bytes 786440 | tf_op jit(solution)/shard_map/ppermute | solution.py:277
  31.5 1.8 %collective-permute-start.8 = (bf16[64,3072]{1,0:T(8,128)(2,1)S(1)}, bf16[64,3072]{1,0:T(8,128)(2,1)S(1)}, u32[]{:S(2)}, u32[]{:S(2)}) collective-permute-start(bf16[64,3072]{1,0:T(8,128)(2,1)S(1)} %get-tuple-element.23), channel_id=1, source_target_pairs={{1,0},{0,1},{3,2},{2,3},{5,4},{4,5},{7,6},{6,7},{9,8},{8,9},{11,10... | collective-permute-start | bytes 1179656 | tf_op jit(solution)/shard_map/ppermute | solution.py:277
  33.4 11.2 %collective-permute-start.10 = (bf16[64,3072]{1,0:T(8,128)(2,1)S(1)}, bf16[64,3072]{1,0:T(8,128)(2,1)S(1)}, u32[]{:S(2)}, u32[]{:S(2)}) collective-permute-start(bf16[64,3072]{1,0:T(8,128)(2,1)S(1)} %add_part.5.refs_5_), channel_id=1, source_target_pairs={{2,0},{3,1},{0,2},{1,3},{6,4},{7,5},{4,6},{5,7},{10,8},{11,9},{8,1... | collective-permute-start | bytes 1179656 | tf_op jit(solution)/shard_map/ppermute | solution.py:277
  42.4 1.7 %collective-permute-start.9 = (bf16[64,2560]{1,0:T(8,128)(2,1)S(1)}, bf16[64,2560]{1,0:T(8,128)(2,1)S(1)}, u32[]{:S(2)}, u32[]{:S(2)}) collective-permute-start(bf16[64,2560]{1,0:T(8,128)(2,1)S(1)} %get-tuple-element.25), channel_id=1, source_target_pairs={{1,0},{0,1},{3,2},{2,3},{5,4},{4,5},{7,6},{6,7},{9,8},{8,9},{11,10... | collective-permute-start | bytes 983048 | tf_op jit(solution)/shard_map/ppermute | solution.py:277
  44.1 9.8 %collective-permute-start.12 = (bf16[64,2560]{1,0:T(8,128)(2,1)S(1)}, bf16[64,2560]{1,0:T(8,128)(2,1)S(1)}, u32[]{:S(2)}, u32[]{:S(2)}) collective-permute-start(bf16[64,2560]{1,0:T(8,128)(2,1)S(1)} %add_part.6.refs_5_), channel_id=1, source_target_pairs={{2,0},{3,1},{0,2},{1,3},{6,4},{7,5},{4,6},{5,7},{10,8},{11,9},{8,1... | collective-permute-start | bytes 983048 | tf_op jit(solution)/shard_map/ppermute | solution.py:277
  49.8 1.6 %collective-permute-start.11 = (bf16[64,2048]{1,0:T(8,128)(2,1)S(1)}, bf16[64,2048]{1,0:T(8,128)(2,1)S(1)}, u32[]{:S(2)}, u32[]{:S(2)}) collective-permute-start(bf16[64,2048]{1,0:T(8,128)(2,1)S(1)} %get-tuple-element.27), channel_id=1, source_target_pairs={{1,0},{0,1},{3,2},{2,3},{5,4},{4,5},{7,6},{6,7},{9,8},{8,9},{11,10... | collective-permute-start | bytes 786440 | tf_op jit(solution)/shard_map/ppermute | solution.py:277
  51.5 8.9 %collective-permute-start.15 = (bf16[64,2048]{1,0:T(8,128)(2,1)S(1)}, bf16[64,2048]{1,0:T(8,128)(2,1)S(1)}, u32[]{:S(2)}, u32[]{:S(2)}) collective-permute-start(bf16[64,2048]{1,0:T(8,128)(2,1)S(1)} %add_part.7.refs_5_), channel_id=1, source_target_pairs={{2,0},{3,1},{0,2},{1,3},{6,4},{7,5},{4,6},{5,7},{10,8},{11,9},{8,1... | collective-permute-start | bytes 786440 | tf_op jit(solution)/shard_map/ppermute | solution.py:277
  58.8 1.6 %collective-permute-start.13 = (bf16[64,1792]{1,0:T(8,128)(2,1)S(1)}, bf16[64,1792]{1,0:T(8,128)(2,1)S(1)}, u32[]{:S(2)}, u32[]{:S(2)}) collective-permute-start(bf16[64,1792]{1,0:T(8,128)(2,1)S(1)} %get-tuple-element.29), channel_id=1, source_target_pairs={{1,0},{0,1},{3,2},{2,3},{5,4},{4,5},{7,6},{6,7},{9,8},{8,9},{11,10... | collective-permute-start | bytes 688136 | tf_op jit(solution)/shard_map/ppermute | solution.py:277
  65.0 8.1 %collective-permute-start.18 = (bf16[3,64,1536]{2,1,0:T(8,128)(2,1)S(1)}, bf16[3,64,1536]{2,1,0:T(8,128)(2,1)S(1)}, u32[]{:S(2)}, u32[]{:S(2)}) collective-permute-start(bf16[3,64,1536]{2,1,0:T(8,128)(2,1)S(1)} %swiglu_part.3.refs_0_.refs_2_), channel_id=1, source_target_pairs={{1,0},{0,1},{3,2},{2,3},{5,4},{4,5},{7,6},{6,7},{9,8},{8,9},{11,10... | collective-permute-start | bytes 1769480 | tf_op jit(solution)/shard_map/ppermute | solution.py:277
  65.2 7.9 %collective-permute-start.14 = (bf16[64,1792]{1,0:T(8,128)(2,1)S(1)}, bf16[64,1792]{1,0:T(8,128)(2,1)S(1)}, u32[]{:S(2)}, u32[]{:S(2)}) collective-permute-start(bf16[64,1792]{1,0:T(8,128)(2,1)S(1)} %add_part.8.refs_5_), channel_id=1, source_target_pairs={{2,0},{3,1},{0,2},{1,3},{6,4},{7,5},{4,6},{5,7},{10,8},{11,9},{8,1... | collective-permute-start | bytes 688136 | tf_op jit(solution)/shard_map/ppermute | solution.py:277
  66.2 1.4 %collective-permute-start.16 = (bf16[64,1280]{1,0:T(8,128)(2,1)S(1)}, bf16[64,1280]{1,0:T(8,128)(2,1)S(1)}, u32[]{:S(2)}, u32[]{:S(2)}) collective-permute-start(bf16[64,1280]{1,0:T(8,128)(2,1)S(1)} %get-tuple-element.31.refs_6_), channel_id=1, source_target_pairs={{1,0},{0,1},{3,2},{2,3},{5,4},{4,5},{7,6},{6,7},{9,8},{8,9},{11,10... | collective-permute-start | bytes 491528 | tf_op jit(solution)/shard_map/ppermute | solution.py:277
  80.2 7.0 %collective-permute-start.20 = (bf16[3,64,1280]{2,1,0:T(8,128)(2,1)S(1)}, bf16[3,64,1280]{2,1,0:T(8,128)(2,1)S(1)}, u32[]{:S(2)}, u32[]{:S(2)}) collective-permute-start(bf16[3,64,1280]{2,1,0:T(8,128)(2,1)S(1)} %swiglu_part.4.refs_6_.refs_0_.refs_2_), channel_id=1, source_target_pairs={{1,0},{0,1},{3,2},{2,3},{5,4},{4,5},{7,6},{6,7},{9,8},{8,9},{11,10... | collective-permute-start | bytes 1474568 | tf_op jit(solution)/shard_map/ppermute | solution.py:277
  80.3 6.6 %collective-permute-start.17 = (bf16[64,1280]{1,0:T(8,128)(2,1)S(1)}, bf16[64,1280]{1,0:T(8,128)(2,1)S(1)}, u32[]{:S(2)}, u32[]{:S(2)}) collective-permute-start(bf16[64,1280]{1,0:T(8,128)(2,1)S(1)} %add_part.9.refs_4_), channel_id=1, source_target_pairs={{2,0},{3,1},{0,2},{1,3},{6,4},{7,5},{4,6},{5,7},{10,8},{11,9},{8,1... | collective-permute-start | bytes 491528 | tf_op jit(solution)/shard_map/ppermute | solution.py:277
  87.1 6.1 %collective-permute-start.19 = (bf16[3,64,768]{2,1,0:T(8,128)(2,1)S(1)}, bf16[3,64,768]{2,1,0:T(8,128)(2,1)S(1)}, u32[]{:S(2)}, u32[]{:S(2)}) collective-permute-start(bf16[3,64,768]{2,1,0:T(8,128)(2,1)S(1)} %swiglu_part.5.refs_5_.refs_0_.refs_4_), channel_id=1, source_target_pairs={{1,0},{0,1},{3,2},{2,3},{5,4},{4,5},{7,6},{6,7},{9,8},{8,9},{11,10... | collective-permute-start | bytes 884744 | tf_op jit(solution)/shard_map/ppermute | solution.py:277
  97.4 8.8 %collective-permute-start.21 = (bf16[64,2048]{1,0:T(8,128)(2,1)S(1)}, bf16[64,2048]{1,0:T(8,128)(2,1)S(1)}, u32[]{:S(2)}, u32[]{:S(2)}) collective-permute-start(bf16[64,2048]{1,0:T(8,128)(2,1)S(1)} %select_convert_fusion.refs_4_.refs_9_), channel_id=1, source_target_pairs={{4,0},{0,4},{12,8},{8,12},{20,16},{16,20},{28,24},{24,28},{5,1},{1... | collective-permute-start | bytes 786440 | tf_op jit(solution)/shard_map/ppermute | solution.py:277
  106.5 13.2 %collective-permute-start.22 = (bf16[16,2048]{1,0:T(8,128)(2,1)S(1)}, bf16[16,2048]{1,0:T(8,128)(2,1)S(1)}, u32[]{:S(2)}, u32[]{:S(2)}) collective-permute-start(bf16[16,2048]{1,0:T(8,128)(2,1)S(1)} %get-tuple-element.44), channel_id=1, source_target_pairs={{8,0},{12,4},{0,8},{4,12},{24,16},{28,20},{16,24},{20,28},{9,1},{1... | collective-permute-start | bytes 196616 | tf_op jit(solution)/shard_map/ppermute | solution.py:277
  108.0 11.7 %collective-permute-start.24 = (bf16[16,2048]{1,0:T(8,128)(2,1)S(1)}, bf16[16,2048]{1,0:T(8,128)(2,1)S(1)}, u32[]{:S(2)}, u32[]{:S(2)}) collective-permute-start(bf16[16,2048]{1,0:T(8,128)(2,1)S(1)} %get-tuple-element.45), channel_id=1, source_target_pairs={{24,0},{28,4},{16,8},{20,12},{8,16},{12,20},{0,24},{4,28},{25,1},{... | collective-permute-start | bytes 196616 | tf_op jit(solution)/shard_map/ppermute | solution.py:277
  110.0 9.7 %collective-permute-start.23 = (bf16[16,2048]{1,0:T(8,128)(2,1)S(1)}, bf16[16,2048]{1,0:T(8,128)(2,1)S(1)}, u32[]{:S(2)}, u32[]{:S(2)}) collective-permute-start(bf16[16,2048]{1,0:T(8,128)(2,1)S(1)} %get-tuple-element.46), channel_id=1, source_target_pairs={{16,0},{20,4},{24,8},{28,12},{0,16},{4,20},{8,24},{12,28},{17,1},{... | collective-permute-start | bytes 196616 | tf_op jit(solution)/shard_map/ppermute | solution.py:277

commit v2 on v1

--- a/solution.py
+++ b/solution.py
@@ -11,9 +11,10 @@
 BF16 = jnp.bfloat16
 ROWS = (((1,), (0,)), ((), ()))
 COLS = (((1,), (1,)), ((), ()))
-GATE_EDGES = (0, 6, 8, 11, 13, 14)
-DOWN_EDGES = (0, 0, 6, 8, 11, 14)
-SPAN_EDGES = (0, 6, 11, 14)
+GATE_EDGES = (0, 7, 9, 12, 14)
+DOWN_EDGES = (0, 0, 7, 10, 14)
+SPAN_EDGES = (0, 7, 14)
+FLIGHT = 6
 ANYWHERE = pl.BlockSpec(memory_space=pl.ANY)
 RESIDENT = pl.BlockSpec(memory_space=pltpu.VMEM)
 
@@ -32,55 +33,197 @@
     return pltpu.with_memory_space_constraint(weight, pltpu.HBM)
 
 
+def row_blocks(d):
+    step = step_of(d)
+    return [pl.ds(at, step) for at in range(0, d, step)]
+
+
+def load_kernel(first, gate, up, gate_out, up_out, mark, sems):
+    mark[...] = jnp.zeros_like(mark)
+    take = pl.ds(first, gate_out.shape[1])
+    copies = [
+        pltpu.make_async_copy(source.at[part, take], target.at[part], sems.at[which, i])
+        for which, (source, target) in enumerate(((gate, gate_out), (up, up_out)))
+        for i, part in enumerate(row_blocks(gate.shape[0]))
+    ]
+    for copy in copies:
+        copy.start()
+    for copy in copies:
+        copy.wait()
+
+
+def load_part(gate, up, first, width):
+    d = gate.shape[0]
+    loaded = pl.pallas_call(
+        functools.partial(load_kernel, first),
+        in_specs=[ANYWHERE] * 2,
+        out_specs=[RESIDENT] * 3,
+        out_shape=[pltpu.VMEM((d, width), BF16)] * 2 + [jax.ShapeDtypeStruct((8, 128), F32)],
+        scratch_shapes=[pltpu.SemaphoreType.DMA((2, len(row_blocks(d))))],
+        compiler_params=params(2),
+        cost_estimate=cost(0, 4 * d * width),
+        name="load_part",
+    )(gate, up)
+    *values, mark = loaded
+    return [pltpu.with_memory_space_constraint(value, pltpu.VMEM) for value in values], mark
+
+
+def stack_kernel(n, *refs):
+    out = refs[-1]
+    rows = refs[0].shape[0]
+    for i in range(n):
+        out[pl.ds(i * rows, rows), :] = refs[i][...]
+
+
+def stack_part(blocks, after):
+    rows, d = blocks[0].shape
+    return pl.pallas_call(
+        functools.partial(stack_kernel, len(blocks)),
+        in_specs=[RESIDENT] * len(blocks) + [ANYWHERE] * len(after),
+        out_specs=RESIDENT,
+        out_shape=jax.ShapeDtypeStruct((len(blocks) * rows, d), BF16),
+        compiler_params=params(12),
+        cost_estimate=cost(0, 4 * rows * d, 32),
+        name="stack_part",
+    )(*blocks, *after)
+
+
+def join_kernel(own, theirs, out, turned):
+    half = own.shape[0]
+    core = lax.rem(lax.axis_index("mod"), 2)
+    out[pl.ds(pl.multiple_of(core * half, half), half), :] = own[...]
+    out[pl.ds(pl.multiple_of((1 - core) * half, half), half), :] = theirs[...]
+    turned[...] = out[...].T
+
+
+def join_part(own, theirs):
+    half, d = own.shape
+    return pl.pallas_call(
+        join_kernel,
+        in_specs=[RESIDENT] * 2,
+        out_specs=[RESIDENT] * 2,
+        out_shape=[
+            jax.ShapeDtypeStruct((2 * half, d), BF16),
+            jax.ShapeDtypeStruct((d, 2 * half), BF16),
+        ],
+        compiler_params=params(24),
+        cost_estimate=cost(0, 8 * half * d, 32),
+        name="join_part",
+    )(own, theirs)
+
+
+def split_rows(value, keep, send, at):
+    half = keep.shape[0]
+    put = pl.ds(at, value.shape[1])
+    keep[:, put] = value[:half]
+    send[:, put] = value[half:].astype(BF16)
+
+
+def first_kernel(tile, has_prev, x, weight, *refs):
+    keep, send = refs[-2:]
+    width = weight.shape[1]
+    if has_prev:
+        keep[:, :width] = refs[0][:, :width]
+        send[:, :width] = refs[1][:, :width]
+    start = width if has_prev else 0
+    for at in range(0, width, tile):
+        value = lax.dot_general(
+            x[...], weight[:, pl.ds(at, tile)], ROWS, preferred_element_type=F32
+        )
+        split_rows(value, keep, send, start + at)
+
+
+def piece_shapes(tokens, total):
+    return [
+        jax.ShapeDtypeStruct((tokens // 2, total), F32),
+        jax.ShapeDtypeStruct((tokens // 2, total), BF16),
+    ]
+
+
+def first_part(x, weight, prev, tile, after):
+    t, d = x.shape
+    width = weight.shape[1]
+    return pl.pallas_call(
+        functools.partial(first_kernel, tile, len(prev) > 0),
+        in_specs=[RESIDENT] * (2 + len(prev)) + [ANYWHERE] * len(after),
+        out_specs=[RESIDENT] * 2,
+        out_shape=piece_shapes(t, 2 * width),
+        compiler_params=params(8),
+        cost_estimate=cost(t * d * width, 2 * d * width, 32),
+        name="first_part",
+    )(x, weight, *prev, *after)
+
+
 def forward_kernel(jobs, tile, kinds, *refs):
     n = len(kinds)
     rows = dict(zip(sorted({kind for kind, _ in kinds}), refs))
     weights = dict(zip(kinds, refs[len(rows) : len(rows) + n]))
-    keep, send, tall, wide, sems = refs[-5:]
-    half = keep.shape[0]
-    steps, used = [], [0, 0]
+    keep, send, tall, wide, sums, sems = refs[-6:]
+    blocks = row_blocks(tall.shape[0])
+    steps, start, used = [], 0, 0
+
+    def step(source, target, work):
+        steps.append((pltpu.make_async_copy(source, target, sems.at[len(steps)]), work))
+
+    def tall_work(i, part, at, width):
+        for col in range(at, at + width, tile):
+            put = pl.ds(col, tile)
+            value = lax.dot_general(
+                rows["x"][:, part], tall[part, put], ROWS, preferred_element_type=F32
+            )
+            if i:
+                value += sums[:, put]
+            if i + 1 < len(blocks):
+                sums[:, put] = value
+            else:
+                split_rows(value, keep, send, col)
+
+    def wide_work(target, at):
+        value = lax.dot_general(target[...], rows["g"][...], ROWS, preferred_element_type=F32)
+        split_rows(value.T, keep, send, at)
+
     for (kind, name), first, tiles in jobs:
-        for i in range(tiles):
-            take = pl.ds((first + i) * tile, tile)
-            down = int(kind == "g")
-            source = weights[(kind, name)].at[(take,) if down else (slice(None), take)]
-            target = (tall, wide)[down].at[used[down]]
-            used[down] += 1
-            steps.append((kind, target, pltpu.make_async_copy(source, target, sems.at[len(steps)])))
-    for _, _, copy in steps:
+        weight, width = weights[(kind, name)], tiles * tile
+        if kind == "x":
+            put = pl.ds(start, width)
+            for i, part in enumerate(blocks):
+                source = weight.at[part, pl.ds(first * tile, width)]
+                work = functools.partial(tall_work, i, part, start, width)
+                step(source, tall.at[part, put], work)
+        else:
+            for i in range(tiles):
+                source = weight.at[pl.ds((first + i) * tile, tile)]
+                target = wide.at[used]
+                step(source, target, functools.partial(wide_work, target, start + i * tile))
+                used += 1
+        start += width
+    for copy, _ in steps[:FLIGHT]:
         copy.start()
-    for i, (kind, target, copy) in enumerate(steps):
+    for i, (copy, work) in enumerate(steps):
         copy.wait()
-        value = lax.dot_general(
-            rows[kind][...],
-            target[...],
-            ROWS if kind == "x" else COLS,
-            preferred_element_type=F32,
-        )
-        put = pl.ds(i * tile, tile)
-        keep[:, put] = value[:half]
-        send[:, put] = value[half:].astype(BF16)
-
-
-def forward_part(rows, weights, jobs, tile, after=()):
+        for later, _ in steps[i + FLIGHT : i + FLIGHT + 1]:
+            later.start()
+        work()
+
+
+def forward_part(rows, weights, jobs, tile, half, after=()):
     kinds = sorted({key for key, _, _ in jobs})
     used = [rows[kind] for kind in sorted({kind for kind, _ in kinds})]
-    t, d = used[0].shape
+    d, t = weights[kinds[0]].shape[1 if kinds[0][0] == "g" else 0], 2 * half
     n_wide = sum(tiles for key, _, tiles in jobs if key[0] == "g")
-    n_tall = sum(tiles for key, _, tiles in jobs if key[0] == "x")
-    total = (n_wide + n_tall) * tile
+    tall_jobs = [tiles for key, _, tiles in jobs if key[0] == "x"]
+    tall_width = max(sum(tall_jobs), 1) * tile
+    total = (n_wide + sum(tall_jobs)) * tile
     return pl.pallas_call(
         functools.partial(forward_kernel, jobs, tile, kinds),
         in_specs=[RESIDENT] * len(used) + [ANYWHERE] * (len(kinds) + len(after)),
         out_specs=[RESIDENT] * 2,
-        out_shape=[
-            jax.ShapeDtypeStruct((t // 2, total), F32),
-            jax.ShapeDtypeStruct((t // 2, total), BF16),
-        ],
+        out_shape=piece_shapes(t, total),
         scratch_shapes=[
-            pltpu.VMEM((max(n_tall, 1), d, tile), BF16),
+            pltpu.VMEM((d, tall_width), BF16),
             pltpu.VMEM((max(n_wide, 1), tile, d), BF16),
-            pltpu.SemaphoreType.DMA((n_tall + n_wide,)),
+            pltpu.VMEM((t, tall_width), F32),
+            pltpu.SemaphoreType.DMA((n_wide + len(tall_jobs) * len(row_blocks(d)),)),
         ],
         compiler_params=params(28),
         cost_estimate=cost(2 * t * d * total, 2 * d * total, 32),
@@ -100,8 +243,7 @@
     mine, peer, wg, wu, *others = refs
     prev = others[0]
     out, gate_buf, up_buf, sems = refs[-4:]
-    step = step_of(out.shape[1])
-    parts = [pl.ds(at, step) for at in range(0, out.shape[1], step)]
+    parts = row_blocks(wg.shape[0])
     cols = pl.ds(first, mine.shape[2])
     copies = [
         (
@@ -110,15 +252,18 @@
         )
         for i, part in enumerate(parts)
     ]
-    for pair in copies:
+    for pair in copies[: FLIGHT // 2]:
         for copy in pair:
             copy.start()
     gb = joined(mine, peer, 1)
     ub = joined(mine, peer, 2)
-    for part, pair in zip(parts, copies):
-        pair[0].wait()
+    for i, (part, pair) in enumerate(zip(parts, copies)):
+        for copy in pair:
+            copy.wait()
+        for later in copies[i + FLIGHT // 2 : i + FLIGHT // 2 + 1]:
+            for copy in later:
+                copy.start()
         value = lax.dot_general(gb, gate_buf[part, :], COLS, preferred_element_type=F32)
-        pair[1].wait()
         value += lax.dot_general(ub, up_buf[part, :], COLS, preferred_element_type=F32)
         out[:, part] = value + prev[:, part] if has_prev else value
 
@@ -137,7 +282,7 @@
         scratch_shapes=[
             pltpu.VMEM((d, span), BF16),
             pltpu.VMEM((d, span), BF16),
-            pltpu.SemaphoreType.DMA((2, d // step_of(d))),
+            pltpu.SemaphoreType.DMA((2, len(row_blocks(d)))),
         ],
         compiler_params=params(28),
         cost_estimate=cost(2 * t * d * span, 4 * d * span),
@@ -147,12 +292,11 @@
 
 def weight_kernel(firsts, tile, *refs):
     n = len(firsts)
-    x, g = refs[:2]
+    xt, g = refs[:2]
     acts = [(refs[2 + 2 * i], refs[3 + 2 * i]) for i in range(n)]
-    grad_gate, grad_up, grad_down, xt, gate_buf, up_buf, down_buf, sems = refs[-8:]
-    d = x.shape[1]
+    grad_gate, grad_up, grad_down, gate_buf, up_buf, down_buf, sems = refs[-7:]
+    d = xt.shape[0]
     step = step_of(d)
-    xt[...] = x[...].T
     copies = []
 
     def out(source, target):
@@ -186,8 +330,8 @@
         copy.wait()
 
 
-def weight_part(prev, x, g, acts, firsts, tile, hidden, after):
-    t, d = x.shape
+def weight_part(prev, xt, g, acts, firsts, tile, hidden, after):
+    t, d = g.shape
     prev = [] if prev is None else list(prev)
     spans = [mine.shape[2] for mine, _ in acts]
     total = sum(spans)
@@ -203,7 +347,6 @@
             jax.ShapeDtypeStruct((hidden, d), BF16),
         ],
         scratch_shapes=[
-            pltpu.VMEM((d, t), BF16),
             pltpu.VMEM((d, total), BF16),
             pltpu.VMEM((d, total), BF16),
             pltpu.VMEM((total, d), BF16),
@@ -213,7 +356,7 @@
         compiler_params=params(34),
         cost_estimate=cost(3 * t * d * total, 6 * d * total),
         name="weight_part",
-    )(x, g, *flat, *prev, *after)
+    )(xt, g, *flat, *prev, *after)
 
 
 def add_kernel(keep, got, *refs):
@@ -227,7 +370,7 @@
         out_specs=RESIDENT,
         out_shape=jax.ShapeDtypeStruct(keep.shape, BF16),
         compiler_params=params(16),
-        cost_estimate=cost(keep.size, 8 * keep.size),
+        cost_estimate=cost(keep.size, 8 * keep.size, 64),
         name="add_part",
     )(keep, got, *after)
 
@@ -262,7 +405,7 @@
         out_specs=RESIDENT,
         out_shape=jax.ShapeDtypeStruct((3, rows, width), BF16),
         compiler_params=params(20),
-        cost_estimate=cost(20 * rows * width, 14 * rows * width),
+        cost_estimate=cost(20 * rows * width, 14 * rows * width, 64),
         name="swiglu_part",
     )(*flat, *after)
 
@@ -288,17 +431,10 @@
     def along(block):
         return [block] + [from_far(block, k) for k in range(1, far)]
 
-    def across(column):
-        own = jnp.concatenate(column, axis=0)
-        theirs = near(own)
-        return jnp.concatenate(
-            [jnp.where(core == 0, own, theirs), jnp.where(core == 0, theirs, own)], axis=0
-        )
-
-    column = along(tokens)
-    held, _ = lax.optimization_barrier((grad_output, column))
-    x = across(column)
-    g = across(along(held))
+    def across(column, after):
+        own = stack_part(column, after)
+        return join_part(own, near(own))
+
     gate_key, up_key, down_key = ("x", 0), ("x", 1), ("g", 2)
     weights = {
         gate_key: pinned(gate_weight),
@@ -314,11 +450,21 @@
         return list(zip(bounds[:-1], bounds[1:]))
 
     spans = [(a, b) for a, b in ranges(SPAN_EDGES) if b > a]
+    a, b = next((a, b) for a, b in ranges(GATE_EDGES) if b > a)
+    loaded, mark = load_part(weights[gate_key], weights[up_key], a * tile, (b - a) * tile)
+
+    x, x_turned = across(along(tokens), [mark])
+    column = along(grad_output)
+    rows_of = {"x": x}
 
     def exchanged(jobs, after=()):
-        keep, send = forward_part({"x": x, "g": g}, weights, jobs, tile, after)
+        if pieces:
+            keep, send = forward_part(rows_of, weights, jobs, tile, rows * far, after)
+        else:
+            half = first_part(x, loaded[0], [], tile, [])
+            keep, send = first_part(x, loaded[1], half, tile, after)
         got = other_core(send)
-        narrow = add_part(keep, got)
+        narrow = add_part(keep, got, pieces[-1][-1:] if len(pieces) == 3 else ())
         others = [swap(narrow, "mod", n_mod, 2 * k) for k in range(1, n_mod // 2)]
         return (keep, got, *others), send, narrow
 
@@ -335,8 +481,11 @@
             where[key] += [(k, at + i * tile) for i in range(tiles)]
             at += tiles * tile
         after = narrows[-1:] + [piece[-1] for piece in pieces[-2:-1]]
-        for held, value in zip((pieces, sends, narrows), exchanged(jobs, after)):
-            held.append(value)
+        after = after if pieces else column[1:]
+        for kept, value in zip((pieces, sends, narrows), exchanged(jobs, after)):
+            kept.append(value)
+        if k == 0:
+            g, rows_of["g"] = across(column, sends[:1])
 
     def act(i, after=()):
         places = list(zip(*(where[key][slice(*spans[i])] for key in (gate_key, up_key, down_key))))
@@ -348,7 +497,7 @@
     def weight_grads(prev, group, after):
         return weight_part(
             prev,
-            x,
+            x_turned,
             g,
             [acts[j] for j in group],
             [spans[j][0] * tile for j in group],
@@ -362,13 +511,12 @@
         first = spans[i][0] * tile
         return input_part(prev, mine, peer, weights[gate_key], weights[up_key], first, after)
 
-    acts = [act(0, sends[-1:])]
-    waited = [piece[-1] for piece in pieces[-2:-1]]
-    total = tokens_grad(None, 0, narrows[-1:] + waited)
+    acts = [act(0, narrows[-2:-1])]
+    total = tokens_grad(None, 0, narrows[-1:])
     for i in range(1, n):
-        acts.append(act(i, [total] if i == 1 else [acts[-1][0]]))
+        acts.append(act(i, [total]))
     for i in range(1, n):
-        total = tokens_grad(total, i, [acts[-1][0]])
+        total = tokens_grad(total, i, [])
 
     half = total.shape[0] // 2
     top, bottom = total[:half], total[half:]

time: 121 us -> 104 us (0.86)
  waiting for transfers between devices: 28.4 us -> 21.1 us
  Pallas kernels: 62.3 us -> 57.2 us
  starting transfers between devices: 25.7 us -> 23.3 us
    pallas_call x5 -> x3, Pallas kernels: 27.7 us -> 16.6 us  [forward_part(): pl.pallas_call(functools.partial(forward_kernel, jobs, tile, kinds), in_s...]
    pallas_call x0 -> x7, Pallas kernels: none -> 8.2 us  [the longest x1 5.36 us: load_part(): pl.pallas_call(functools.partial(load_kernel, first), in_specs=[ANYWHERE]...]
    ppermute x25 -> x22, waiting for transfers between devices: 28.4 us -> 21.1 us  [swap(): return lax.ppermute(value, axis, [(i ^ bit, i) for i in range(size)])]
    ppermute x25 -> x22, starting transfers between devices: 25.7 us -> 23.3 us  [swap(): return lax.ppermute(value, axis, [(i ^ bit, i) for i in range(size)])]
    pallas_call x3 -> x2, Pallas kernels: 17 us -> 14.9 us  [input_part(): pl.pallas_call(functools.partial(input_kernel, has_prev, first), in_specs...]
  transfers between devices with their start and end apart: 25 -> 22, of which waited for: 13 -> 13; matrix products, arithmetic and copies ran while one was open for 2% -> 0% of each run, Pallas kernels for 39% -> 46%
where the time goes in v2:
time: 104 us
  Pallas kernels  57.2 us (55%)
  starting transfers between devices  23.3 us (22%)
  waiting for transfers between devices  21.1 us (20%)
    ppermute x22, starting transfers between devices, swap(): return lax.ppermute(value, axis, [(i ^ bit, i) for i in range(size)])  23.3 us
    ppermute x22, waiting for transfers between devices, swap(): return lax.ppermute(value, axis, [(i ^ bit, i) for i in range(size)])  21.1 us
    pallas_call x3, Pallas kernels, forward_part(): pl.pallas_call(functools.partial(forward_kernel, jobs, tile, kinds), in_s...  16.6 us
    pallas_call x2, Pallas kernels, weight_part(): pl.pallas_call(functools.partial(weight_kernel, firsts, tile), in_specs=[...  16.5 us
    pallas_call x2, Pallas kernels, input_part(): pl.pallas_call(functools.partial(input_kernel, has_prev, first), in_specs...  14.9 us
    pallas_call x1, Pallas kernels, load_part(): pl.pallas_call(functools.partial(load_kernel, first), in_specs=[ANYWHERE]...  5.36 us
    pallas_call x2, Pallas kernels, first_part(): pl.pallas_call(functools.partial(first_kernel, tile, len(prev) > 0), in_s...  2.3 us
  transfers between devices with their start and end apart: 22, of which 13 were waited for; matrix products, arithmetic and copies ran while one was open for 0% of the time, Pallas kernels for 46%

profile of v2, /device:TPU:0, one launch (start us, length us, event | category | flops | bytes accessed | tf_op | source)
XLA Modules:
  0.0 104.2 jit_solution(12915386113750983459)
XLA Ops:
  0.7 4.1 %collective-permute-start.4 = (bf16[16,2048]{1,0:T(8,128)(2,1)}, bf16[16,2048]{1,0:T(8,128)(2,1)S(1)}, u32[]{:S(2)}, u32[]{:S(2)}) collective-permute-start(bf16[16,2048]{1,0:T(8,128)(2,1)} %refs_0_.2), channel_id=1, source_target_pairs={{16,0},{20,4},{24,8},{28,12},{0,16},{4,20},{8,24},{12,28},{17,1},{... | collective-permute-start | bytes 196616 | tf_op jit(solution)/shard_map/ppermute | solution.py:420
  4.8 1.6 %collective-permute-start.3 = (bf16[16,2048]{1,0:T(8,128)(2,1)}, bf16[16,2048]{1,0:T(8,128)(2,1)S(1)}, u32[]{:S(2)}, u32[]{:S(2)}) collective-permute-start(bf16[16,2048]{1,0:T(8,128)(2,1)} %refs_0_.2), channel_id=1, source_target_pairs={{8,0},{12,4},{0,8},{4,12},{24,16},{28,20},{16,24},{20,28},{9,1},{1... | collective-permute-start | bytes 196616 | tf_op jit(solution)/shard_map/ppermute | solution.py:420
  6.3 5.4 %load_part.1 = (bf16[2048,1792]{1,0:T(8,128)(2,1)S(1)}, bf16[2048,1792]{1,0:T(8,128)(2,1)S(1)}, f32[8,128]{1,0:T(8,128)S(1)}) custom-call(bf16[2048,3584]{1,0:T(8,128)(2,1)} %refs_2_.9, bf16[2048,3584]{1,0:T(8,128)(2,1)} %refs_3_.9), custom_call_target="tpu_custom_call" | custom-call | bytes 14680064 | tf_op jit(solution)/shard_map/load_part/pallas_call | solution.py:57
  11.7 0.9 collective-permute-done.5.refs_3_
  12.6 1.6 %collective-permute-start.6 = (bf16[64,2048]{1,0:T(8,128)(2,1)S(1)}, bf16[64,2048]{1,0:T(8,128)(2,1)S(1)}, u32[]{:S(2)}, u32[]{:S(2)}) collective-permute-start(bf16[64,2048]{1,0:T(8,128)(2,1)S(1)} %stack_part.2.own), channel_id=1, source_target_pairs={{4,0},{0,4},{12,8},{8,12},{20,16},{16,20},{28,24},{24,28},{5,1},{1... | collective-permute-start | bytes 786440 | tf_op jit(solution)/shard_map/ppermute | solution.py:420
  14.2 1.3 %collective-permute-start.1 = (bf16[16,2048]{1,0:T(8,128)(2,1)S(1)}, bf16[16,2048]{1,0:T(8,128)(2,1)S(1)}, u32[]{:S(2)}, u32[]{:S(2)}) collective-permute-start(bf16[16,2048]{1,0:T(8,128)(2,1)S(1)} %copy-done.7), channel_id=1, source_target_pairs={{16,0},{20,4},{24,8},{28,12},{0,16},{4,20},{8,24},{12,28},{17,1},{... | collective-permute-start | bytes 196616 | tf_op jit(solution)/shard_map/ppermute | solution.py:420
  15.5 2.2 %collective-permute-start = (bf16[16,2048]{1,0:T(8,128)(2,1)S(1)}, bf16[16,2048]{1,0:T(8,128)(2,1)S(1)}, u32[]{:S(2)}, u32[]{:S(2)}) collective-permute-start(bf16[16,2048]{1,0:T(8,128)(2,1)S(1)} %copy-done.7), channel_id=1, source_target_pairs={{8,0},{12,4},{0,8},{4,12},{24,16},{28,20},{16,24},{20,28},{9,1},{1... | collective-permute-start | bytes 196616 | tf_op jit(solution)/shard_map/ppermute | solution.py:420
  17.7 0.9 collective-permute-start.2
  19.6 1.1 %first_part.2 = (f32[64,3584]{1,0:T(8,128)S(1)}, bf16[64,3584]{1,0:T(8,128)(2,1)S(1)}) custom-call(bf16[128,2048]{1,0:T(8,128)(2,1)S(1)} %get-tuple-element.28.x.refs_1_, bf16[2048,1792]{1,0:T(8,128)(2,1)S(1)} %get-tuple-element.30.weight), custom_call_target="tpu_custom_call" | custom-call | flops 29360128 | bytes 229376 | tf_op jit(solution)/shard_map/first_part/pallas_call | solution.py:146
  20.9 2.9 %collective-permute-done.2.refs_4_.refs_3_ = bf16[16,2048]{1,0:T(8,128)(2,1)S(1)} collective-permute-done((bf16[16,2048]{1,0:T(8,128)(2,1)S(1)}, bf16[16,2048]{1,0:T(8,128)(2,1)S(1)}, u32[]{:S(2)}, u32[]{:S(2)}) %collective-permute-start.2) | collective-permute-done | bytes 65568 | tf_op jit(solution)/shard_map/ppermute | solution.py:420
  23.8 1.2 %first_part.3 = (f32[64,3584]{1,0:T(8,128)S(1)}, bf16[64,3584]{1,0:T(8,128)(2,1)S(1)}) custom-call(bf16[128,2048]{1,0:T(8,128)(2,1)S(1)} %get-tuple-element.28.x.refs_1_, bf16[2048,1792]{1,0:T(8,128)(2,1)S(1)} %get-tuple-element.29.weight, f32[64,3584]{1,0:T(8,128)S(1)} %get-tuple-element.31.refs_0_, bf16[64,3584]{1,0:T(8,128)(2,1)S(1)} %get-tuple-element.32.refs_1_, ...), custom_call_target="tpu_custom_call" | custom-call | flops 29360128 | bytes 229376 | tf_op jit(solution)/shard_map/first_part/pallas_call | solution.py:146
  25.7 1.2 %collective-permute-done.8.got.refs_1_ = bf16[64,3584]{1,0:T(8,128)(2,1)S(1)} collective-permute-done((bf16[64,3584]{1,0:T(8,128)(2,1)S(1)}, bf16[64,3584]{1,0:T(8,128)(2,1)S(1)}, u32[]{:S(2)}, u32[]{:S(2)}) %collective-permute-start.8) | collective-permute-done | bytes 458784 | tf_op jit(solution)/shard_map/ppermute | solution.py:420
  26.9 1.6 %collective-permute-start.11 = (bf16[64,3584]{1,0:T(8,128)(2,1)S(1)}, bf16[64,3584]{1,0:T(8,128)(2,1)S(1)}, u32[]{:S(2)}, u32[]{:S(2)}) collective-permute-start(bf16[64,3584]{1,0:T(8,128)(2,1)S(1)} %add_part.4.refs_5_), channel_id=1, source_target_pairs={{2,0},{3,1},{0,2},{1,3},{6,4},{7,5},{4,6},{5,7},{10,8},{11,9},{8,1... | collective-permute-start | bytes 1376264 | tf_op jit(solution)/shard_map/ppermute | solution.py:420
  28.5 5.3 %collective-permute-done.7.theirs = bf16[64,2048]{1,0:T(8,128)(2,1)S(1)} collective-permute-done((bf16[64,2048]{1,0:T(8,128)(2,1)S(1)}, bf16[64,2048]{1,0:T(8,128)(2,1)S(1)}, u32[]{:S(2)}, u32[]{:S(2)}) %collective-permute-start.7) | collective-permute-done | bytes 262176 | tf_op jit(solution)/shard_map/ppermute | solution.py:420
  34.9 6.3 %forward_part.3 = (f32[64,2816]{1,0:T(8,128)S(1)}, bf16[64,2816]{1,0:T(8,128)(2,1)S(1)}) custom-call(bf16[2048,128]{1,0:T(8,128)(2,1)S(1)} %get-tuple-element.34.refs_0_, bf16[128,2048]{1,0:T(8,128)(2,1)S(1)} %get-tuple-element.28.x.refs_1_, bf16[3584,2048]{1,0:T(8,128)(2,1)} %refs_2_.7, bf16[2048,3584]{1,0:T(8,128)(2,1)} %refs_2_.9, ...), custom_call_target="tpu_custom_call" | custom-call | flops 92274688 | bytes 360448 | tf_op jit(solution)/shard_map/forward_part/pallas_call | solution.py:217
  41.3 1.7 %collective-permute-done.9.got.refs_4_.refs_1_ = bf16[64,2816]{1,0:T(8,128)(2,1)S(1)} collective-permute-done((bf16[64,2816]{1,0:T(8,128)(2,1)S(1)}, bf16[64,2816]{1,0:T(8,128)(2,1)S(1)}, u32[]{:S(2)}, u32[]{:S(2)}) %collective-permute-start.9) | collective-permute-done | bytes 360480 | tf_op jit(solution)/shard_map/ppermute | solution.py:420
  43.0 1.6 %collective-permute-start.10 = (bf16[64,2816]{1,0:T(8,128)(2,1)S(1)}, bf16[64,2816]{1,0:T(8,128)(2,1)S(1)}, u32[]{:S(2)}, u32[]{:S(2)}) collective-permute-start(bf16[64,2816]{1,0:T(8,128)(2,1)S(1)} %add_part.5.refs_5_), channel_id=1, source_target_pairs={{2,0},{3,1},{0,2},{1,3},{6,4},{7,5},{4,6},{5,7},{10,8},{11,9},{8,1... | collective-permute-start | bytes 1081352 | tf_op jit(solution)/shard_map/ppermute | solution.py:420
  44.6 5.2 %forward_part.4 = (f32[64,2304]{1,0:T(8,128)S(1)}, bf16[64,2304]{1,0:T(8,128)(2,1)S(1)}) custom-call(bf16[2048,128]{1,0:T(8,128)(2,1)S(1)} %get-tuple-element.34.refs_0_, bf16[128,2048]{1,0:T(8,128)(2,1)S(1)} %get-tuple-element.28.x.refs_1_, bf16[3584,2048]{1,0:T(8,128)(2,1)} %refs_2_.7, bf16[2048,3584]{1,0:T(8,128)(2,1)} %refs_2_.9, ...), custom_call_target="tpu_custom_call" | custom-call | flops 75497472 | bytes 294912 | tf_op jit(solution)/shard_map/forward_part/pallas_call | solution.py:217
  49.9 1.6 %collective-permute-done.12.got.refs_4_ = bf16[64,2304]{1,0:T(8,128)(2,1)S(1)} collective-permute-done((bf16[64,2304]{1,0:T(8,128)(2,1)S(1)}, bf16[64,2304]{1,0:T(8,128)(2,1)S(1)}, u32[]{:S(2)}, u32[]{:S(2)}) %collective-permute-start.12) | collective-permute-done | bytes 294944 | tf_op jit(solution)/shard_map/ppermute | solution.py:420
  51.6 2.0 %collective-permute-done.10.refs_6_.refs_5_.refs_2_ = bf16[64,2816]{1,0:T(8,128)(2,1)S(1)} collective-permute-done((bf16[64,2816]{1,0:T(8,128)(2,1)S(1)}, bf16[64,2816]{1,0:T(8,128)(2,1)S(1)}, u32[]{:S(2)}, u32[]{:S(2)}) %collective-permute-start.10) | collective-permute-done | bytes 360480 | tf_op jit(solution)/shard_map/ppermute | solution.py:420
  54.0 1.6 %collective-permute-start.13 = (bf16[64,2304]{1,0:T(8,128)(2,1)S(1)}, bf16[64,2304]{1,0:T(8,128)(2,1)S(1)}, u32[]{:S(2)}, u32[]{:S(2)}) collective-permute-start(bf16[64,2304]{1,0:T(8,128)(2,1)S(1)} %add_part.6.refs_5_.refs_6_), channel_id=1, source_target_pairs={{2,0},{3,1},{0,2},{1,3},{6,4},{7,5},{4,6},{5,7},{10,8},{11,9},{8,1... | collective-permute-start | bytes 884744 | tf_op jit(solution)/shard_map/ppermute | solution.py:420
  55.6 5.0 %forward_part.5 = (f32[64,2048]{1,0:T(8,128)S(1)}, bf16[64,2048]{1,0:T(8,128)(2,1)S(1)}) custom-call(bf16[2048,128]{1,0:T(8,128)(2,1)S(1)} %get-tuple-element.34.refs_0_, bf16[128,2048]{1,0:T(8,128)(2,1)S(1)} %get-tuple-element.28.x.refs_1_, bf16[3584,2048]{1,0:T(8,128)(2,1)} %refs_2_.7, bf16[2048,3584]{1,0:T(8,128)(2,1)} %refs_2_.9, ...), custom_call_target="tpu_custom_call" | custom-call | flops 67108864 | bytes 262144 | tf_op jit(solution)/shard_map/forward_part/pallas_call | solution.py:217
  60.9 1.4 %collective-permute-done.14.got.refs_7_ = bf16[64,2048]{1,0:T(8,128)(2,1)S(1)} collective-permute-done((bf16[64,2048]{1,0:T(8,128)(2,1)S(1)}, bf16[64,2048]{1,0:T(8,128)(2,1)S(1)}, u32[]{:S(2)}, u32[]{:S(2)}) %collective-permute-start.14) | collective-permute-done | bytes 262176 | tf_op jit(solution)/shard_map/ppermute | solution.py:420
  62.2 1.2 %collective-permute-done.13.refs_0_.refs_5_ = bf16[64,2304]{1,0:T(8,128)(2,1)S(1)} collective-permute-done((bf16[64,2304]{1,0:T(8,128)(2,1)S(1)}, bf16[64,2304]{1,0:T(8,128)(2,1)S(1)}, u32[]{:S(2)}, u32[]{:S(2)}) %collective-permute-start.13) | collective-permute-done | bytes 294944 | tf_op jit(solution)/shard_map/ppermute | solution.py:420
  63.5 1.6 %collective-permute-start.15 = (bf16[64,2048]{1,0:T(8,128)(2,1)S(1)}, bf16[64,2048]{1,0:T(8,128)(2,1)S(1)}, u32[]{:S(2)}, u32[]{:S(2)}) collective-permute-start(bf16[64,2048]{1,0:T(8,128)(2,1)S(1)} %add_part.7.refs_4_), channel_id=1, source_target_pairs={{2,0},{3,1},{0,2},{1,3},{6,4},{7,5},{4,6},{5,7},{10,8},{11,9},{8,1... | collective-permute-start | bytes 786440 | tf_op jit(solution)/shard_map/ppermute | solution.py:420
  65.1 7.6 %input_part.2.refs_9_.refs_4_ = f32[128,2048]{1,0:T(8,128)S(1)} custom-call(bf16[3,64,1792]{2,1,0:T(8,128)(2,1)S(1)} %swiglu_part.2.refs_0_.refs_2_, bf16[3,64,1792]{2,1,0:T(8,128)(2,1)S(1)} %collective-permute-done.16.refs_1_.refs_3_, bf16[2048,3584]{1,0:T(8,128)(2,1)} %refs_2_.9, bf16[2048,3584]{1,0:T(8,128)(2,1)} %refs_3_.9, ...), custom_call_target="tpu_custom_call" | custom-call | flops 1879048192 | bytes 14680064 | tf_op jit(solution)/shard_map/input_part/pallas_call | solution.py:274
  73.2 2.1 %collective-permute-done.17.refs_1_.refs_3_ = bf16[3,64,1792]{2,1,0:T(8,128)(2,1)S(1)} collective-permute-done((bf16[3,64,1792]{2,1,0:T(8,128)(2,1)S(1)}, bf16[3,64,1792]{2,1,0:T(8,128)(2,1)S(1)}, u32[]{:S(2)}, u32[]{:S(2)}) %collective-permute-start.17) | collective-permute-done | bytes 688160 | tf_op jit(solution)/shard_map/ppermute | solution.py:420
  75.3 7.3 %input_part.3 = f32[128,2048]{1,0:T(8,128)S(1)} custom-call(bf16[3,64,1792]{2,1,0:T(8,128)(2,1)S(1)} %swiglu_part.3.refs_0_.refs_2_, bf16[3,64,1792]{2,1,0:T(8,128)(2,1)S(1)} %collective-permute-done.17.refs_1_.refs_3_, bf16[2048,3584]{1,0:T(8,128)(2,1)} %refs_2_.9, bf16[2048,3584]{1,0:T(8,128)(2,1)} %refs_3_.9, f32[128,2048]{1,0:T(8,128)S(1)} %input_part.2.refs_9_.refs_4_), custom_call_target="tpu_custom_call" | custom-call | flops 1879048192 | bytes 14680064 | tf_op jit(solution)/shard_map/input_part/pallas_call | solution.py:274
  83.3 8.3 %weight_part.2 = (bf16[2048,3584]{1,0:T(8,128)(2,1)}, bf16[2048,3584]{1,0:T(8,128)(2,1)}, bf16[3584,2048]{1,0:T(8,128)(2,1)}) custom-call(bf16[2048,128]{1,0:T(8,128)(2,1)S(1)} %copy-done.3, bf16[128,2048]{1,0:T(8,128)(2,1)S(1)} %copy-done.5, bf16[3,64,1792]{2,1,0:T(8,128)(2,1)S(1)} %swiglu_part.2.refs_0_.refs_2_, bf16[3,64,1792]{2,1,0:T(8,128)(2,1)S(1)} %copy-done.1, ...), custom_call_target="tpu_custom_call" | custom-call | flops 2818572288 | bytes 22020096 | tf_op jit(solution)/shard_map/weight_part/pallas_call | solution.py:340
  91.8 1.9 %collective-permute-start.21 = (bf16[16,2048]{1,0:T(8,128)(2,1)S(1)}, bf16[16,2048]{1,0:T(8,128)(2,1)S(1)}, u32[]{:S(2)}, u32[]{:S(2)}) collective-permute-start(bf16[16,2048]{1,0:T(8,128)(2,1)S(1)} %get-tuple-element.53), channel_id=1, source_target_pairs={{24,0},{28,4},{16,8},{20,12},{8,16},{12,20},{0,24},{4,28},{25,1},{... | collective-permute-start | bytes 196616 | tf_op jit(solution)/shard_map/ppermute | solution.py:420
  93.7 1.5 %collective-permute-start.20 = (bf16[16,2048]{1,0:T(8,128)(2,1)S(1)}, bf16[16,2048]{1,0:T(8,128)(2,1)S(1)}, u32[]{:S(2)}, u32[]{:S(2)}) collective-permute-start(bf16[16,2048]{1,0:T(8,128)(2,1)S(1)} %get-tuple-element.54), channel_id=1, source_target_pairs={{16,0},{20,4},{24,8},{28,12},{0,16},{4,20},{8,24},{12,28},{17,1},{... | collective-permute-start | bytes 196616 | tf_op jit(solution)/shard_map/ppermute | solution.py:420
  95.3 8.3 %weight_part.3 = (bf16[2048,3584]{1,0:T(8,128)(2,1)}, bf16[2048,3584]{1,0:T(8,128)(2,1)}, bf16[3584,2048]{1,0:T(8,128)(2,1)}) custom-call(bf16[2048,128]{1,0:T(8,128)(2,1)S(1)} %copy-done.3, bf16[128,2048]{1,0:T(8,128)(2,1)S(1)} %copy-done.5, ...), custom_call_target="tpu_custom_call", output_to_operand_aliasing={{0}: (4, {}), {1}: (5, {}), {2}: (6, {})} | custom-call | flops 2818572288 | bytes 22020096 | tf_op jit(solution)/shard_map/weight_part/pallas_call | solution.py:340
  (52 shorter events, 6.0 us)
Async XLA Ops:
  0.6 12.0 %copy-start.6 = (bf16[16,2048]{1,0:T(8,128)(2,1)S(1)}, bf16[16,2048]{1,0:T(8,128)(2,1)}, u32[]{:S(2)}) copy-start(bf16[16,2048]{1,0:T(8,128)(2,1)} %refs_0_.2) | copy-start | bytes 196612
  0.6 13.5 %copy-start.7 = (bf16[16,2048]{1,0:T(8,128)(2,1)S(1)}, bf16[16,2048]{1,0:T(8,128)(2,1)}, u32[]{:S(2)}) copy-start(bf16[16,2048]{1,0:T(8,128)(2,1)} %refs_0_.3) | copy-start | bytes 196612
  0.7 11.0 %collective-permute-start.4 = (bf16[16,2048]{1,0:T(8,128)(2,1)}, bf16[16,2048]{1,0:T(8,128)(2,1)S(1)}, u32[]{:S(2)}, u32[]{:S(2)}) collective-permute-start(bf16[16,2048]{1,0:T(8,128)(2,1)} %refs_0_.2), channel_id=1, source_target_pairs={{16,0},{20,4},{24,8},{28,12},{0,16},{4,20},{8,24},{12,28},{17,1},{... | collective-permute-start | bytes 196616 | tf_op jit(solution)/shard_map/ppermute | solution.py:420
  4.8 7.0 %collective-permute-start.3 = (bf16[16,2048]{1,0:T(8,128)(2,1)}, bf16[16,2048]{1,0:T(8,128)(2,1)S(1)}, u32[]{:S(2)}, u32[]{:S(2)}) collective-permute-start(bf16[16,2048]{1,0:T(8,128)(2,1)} %refs_0_.2), channel_id=1, source_target_pairs={{8,0},{12,4},{0,8},{4,12},{24,16},{28,20},{16,24},{20,28},{9,1},{1... | collective-permute-start | bytes 196616 | tf_op jit(solution)/shard_map/ppermute | solution.py:420
  6.3 6.3 %collective-permute-start.5 = (bf16[16,2048]{1,0:T(8,128)(2,1)}, bf16[16,2048]{1,0:T(8,128)(2,1)S(1)}, u32[]{:S(2)}, u32[]{:S(2)}) collective-permute-start(bf16[16,2048]{1,0:T(8,128)(2,1)} %refs_0_.2), channel_id=1, source_target_pairs={{24,0},{28,4},{16,8},{20,12},{8,16},{12,20},{0,24},{4,28},{25,1},{... | collective-permute-start | bytes 196616 | tf_op jit(solution)/shard_map/ppermute | solution.py:420
  12.6 6.7 %collective-permute-start.6 = (bf16[64,2048]{1,0:T(8,128)(2,1)S(1)}, bf16[64,2048]{1,0:T(8,128)(2,1)S(1)}, u32[]{:S(2)}, u32[]{:S(2)}) collective-permute-start(bf16[64,2048]{1,0:T(8,128)(2,1)S(1)} %stack_part.2.own), channel_id=1, source_target_pairs={{4,0},{0,4},{12,8},{8,12},{20,16},{16,20},{28,24},{24,28},{5,1},{1... | collective-permute-start | bytes 786440 | tf_op jit(solution)/shard_map/ppermute | solution.py:420
  14.2 6.6 %collective-permute-start.1 = (bf16[16,2048]{1,0:T(8,128)(2,1)S(1)}, bf16[16,2048]{1,0:T(8,128)(2,1)S(1)}, u32[]{:S(2)}, u32[]{:S(2)}) collective-permute-start(bf16[16,2048]{1,0:T(8,128)(2,1)S(1)} %copy-done.7), channel_id=1, source_target_pairs={{16,0},{20,4},{24,8},{28,12},{0,16},{4,20},{8,24},{12,28},{17,1},{... | collective-permute-start | bytes 196616 | tf_op jit(solution)/shard_map/ppermute | solution.py:420
  15.5 5.4 %collective-permute-start = (bf16[16,2048]{1,0:T(8,128)(2,1)S(1)}, bf16[16,2048]{1,0:T(8,128)(2,1)S(1)}, u32[]{:S(2)}, u32[]{:S(2)}) collective-permute-start(bf16[16,2048]{1,0:T(8,128)(2,1)S(1)} %copy-done.7), channel_id=1, source_target_pairs={{8,0},{12,4},{0,8},{4,12},{24,16},{28,20},{16,24},{20,28},{9,1},{1... | collective-permute-start | bytes 196616 | tf_op jit(solution)/shard_map/ppermute | solution.py:420
  17.7 6.1 %collective-permute-start.2 = (bf16[16,2048]{1,0:T(8,128)(2,1)S(1)}, bf16[16,2048]{1,0:T(8,128)(2,1)S(1)}, u32[]{:S(2)}, u32[]{:S(2)}) collective-permute-start(bf16[16,2048]{1,0:T(8,128)(2,1)S(1)} %copy-done.7), channel_id=1, source_target_pairs={{24,0},{28,4},{16,8},{20,12},{8,16},{12,20},{0,24},{4,28},{25,1},{... | collective-permute-start | bytes 196616 | tf_op jit(solution)/shard_map/ppermute | solution.py:420
  19.6 8.9 %copy-start.2 = (bf16[2048,128]{1,0:T(8,128)(2,1)}, bf16[2048,128]{1,0:T(8,128)(2,1)S(1)}, u32[]{:S(2)}) copy-start(bf16[2048,128]{1,0:T(8,128)(2,1)S(1)} %get-tuple-element.42.refs_0_) | copy-start | bytes 1572868
  25.0 1.9 %collective-permute-start.8 = (bf16[64,3584]{1,0:T(8,128)(2,1)S(1)}, bf16[64,3584]{1,0:T(8,128)(2,1)S(1)}, u32[]{:S(2)}, u32[]{:S(2)}) collective-permute-start(bf16[64,3584]{1,0:T(8,128)(2,1)S(1)} %get-tuple-element.33.refs_4_), channel_id=1, source_target_pairs={{1,0},{0,1},{3,2},{2,3},{5,4},{4,5},{7,6},{6,7},{9,8},{8,9},{11,10... | collective-permute-start | bytes 1376264 | tf_op jit(solution)/shard_map/ppermute | solution.py:420
  25.1 8.8 %collective-permute-start.7 = (bf16[64,2048]{1,0:T(8,128)(2,1)S(1)}, bf16[64,2048]{1,0:T(8,128)(2,1)S(1)}, u32[]{:S(2)}, u32[]{:S(2)}) collective-permute-start(bf16[64,2048]{1,0:T(8,128)(2,1)S(1)} %stack_part.3.own), channel_id=1, source_target_pairs={{4,0},{0,4},{12,8},{8,12},{20,16},{16,20},{28,24},{24,28},{5,1},{1... | collective-permute-start | bytes 786440 | tf_op jit(solution)/shard_map/ppermute | solution.py:420
  26.9 17.7 %collective-permute-start.11 = (bf16[64,3584]{1,0:T(8,128)(2,1)S(1)}, bf16[64,3584]{1,0:T(8,128)(2,1)S(1)}, u32[]{:S(2)}, u32[]{:S(2)}) collective-permute-start(bf16[64,3584]{1,0:T(8,128)(2,1)S(1)} %add_part.4.refs_5_), channel_id=1, source_target_pairs={{2,0},{3,1},{0,2},{1,3},{6,4},{7,5},{4,6},{5,7},{10,8},{11,9},{8,1... | collective-permute-start | bytes 1376264 | tf_op jit(solution)/shard_map/ppermute | solution.py:420
  34.1 0.8 copy-start.4
  41.2 1.7 %collective-permute-start.9 = (bf16[64,2816]{1,0:T(8,128)(2,1)S(1)}, bf16[64,2816]{1,0:T(8,128)(2,1)S(1)}, u32[]{:S(2)}, u32[]{:S(2)}) collective-permute-start(bf16[64,2816]{1,0:T(8,128)(2,1)S(1)} %get-tuple-element.37), channel_id=1, source_target_pairs={{1,0},{0,1},{3,2},{2,3},{5,4},{4,5},{7,6},{6,7},{9,8},{8,9},{11,10... | collective-permute-start | bytes 1081352 | tf_op jit(solution)/shard_map/ppermute | solution.py:420
  43.0 10.5 %collective-permute-start.10 = (bf16[64,2816]{1,0:T(8,128)(2,1)S(1)}, bf16[64,2816]{1,0:T(8,128)(2,1)S(1)}, u32[]{:S(2)}, u32[]{:S(2)}) collective-permute-start(bf16[64,2816]{1,0:T(8,128)(2,1)S(1)} %add_part.5.refs_5_), channel_id=1, source_target_pairs={{2,0},{3,1},{0,2},{1,3},{6,4},{7,5},{4,6},{5,7},{10,8},{11,9},{8,1... | collective-permute-start | bytes 1081352 | tf_op jit(solution)/shard_map/ppermute | solution.py:420
  49.9 1.6 %collective-permute-start.12 = (bf16[64,2304]{1,0:T(8,128)(2,1)S(1)}, bf16[64,2304]{1,0:T(8,128)(2,1)S(1)}, u32[]{:S(2)}, u32[]{:S(2)}) collective-permute-start(bf16[64,2304]{1,0:T(8,128)(2,1)S(1)} %get-tuple-element.39), channel_id=1, source_target_pairs={{1,0},{0,1},{3,2},{2,3},{5,4},{4,5},{7,6},{6,7},{9,8},{8,9},{11,10... | collective-permute-start | bytes 884744 | tf_op jit(solution)/shard_map/ppermute | solution.py:420
  54.0 11.1 %collective-permute-start.16 = (bf16[3,64,1792]{2,1,0:T(8,128)(2,1)S(1)}, bf16[3,64,1792]{2,1,0:T(8,128)(2,1)S(1)}, u32[]{:S(2)}, u32[]{:S(2)}) collective-permute-start(bf16[3,64,1792]{2,1,0:T(8,128)(2,1)S(1)} %swiglu_part.2.refs_0_.refs_2_), channel_id=1, source_target_pairs={{1,0},{0,1},{3,2},{2,3},{5,4},{4,5},{7,6},{6,7},{9,8},{8,9},{11,10... | collective-permute-start | bytes 2064392 | tf_op jit(solution)/shard_map/ppermute | solution.py:420
  54.0 9.4 %collective-permute-start.13 = (bf16[64,2304]{1,0:T(8,128)(2,1)S(1)}, bf16[64,2304]{1,0:T(8,128)(2,1)S(1)}, u32[]{:S(2)}, u32[]{:S(2)}) collective-permute-start(bf16[64,2304]{1,0:T(8,128)(2,1)S(1)} %add_part.6.refs_5_.refs_6_), channel_id=1, source_target_pairs={{2,0},{3,1},{0,2},{1,3},{6,4},{7,5},{4,6},{5,7},{10,8},{11,9},{8,1... | collective-permute-start | bytes 884744 | tf_op jit(solution)/shard_map/ppermute | solution.py:420
  60.6 1.6 %collective-permute-start.14 = (bf16[64,2048]{1,0:T(8,128)(2,1)S(1)}, bf16[64,2048]{1,0:T(8,128)(2,1)S(1)}, u32[]{:S(2)}, u32[]{:S(2)}) collective-permute-start(bf16[64,2048]{1,0:T(8,128)(2,1)S(1)} %get-tuple-element.41), channel_id=1, source_target_pairs={{1,0},{0,1},{3,2},{2,3},{5,4},{4,5},{7,6},{6,7},{9,8},{8,9},{11,10... | collective-permute-start | bytes 786440 | tf_op jit(solution)/shard_map/ppermute | solution.py:420
  63.5 9.2 %collective-permute-start.15 = (bf16[64,2048]{1,0:T(8,128)(2,1)S(1)}, bf16[64,2048]{1,0:T(8,128)(2,1)S(1)}, u32[]{:S(2)}, u32[]{:S(2)}) collective-permute-start(bf16[64,2048]{1,0:T(8,128)(2,1)S(1)} %add_part.7.refs_4_), channel_id=1, source_target_pairs={{2,0},{3,1},{0,2},{1,3},{6,4},{7,5},{4,6},{5,7},{10,8},{11,9},{8,1... | collective-permute-start | bytes 786440 | tf_op jit(solution)/shard_map/ppermute | solution.py:420
  65.1 7.6 %copy-start = (bf16[3,64,1792]{2,1,0:T(8,128)(2,1)}, bf16[3,64,1792]{2,1,0:T(8,128)(2,1)S(1)}, u32[]{:S(2)}) copy-start(bf16[3,64,1792]{2,1,0:T(8,128)(2,1)S(1)} %collective-permute-done.16.refs_1_.refs_3_) | copy-start | bytes 2064388
  73.1 2.2 %collective-permute-start.17 = (bf16[3,64,1792]{2,1,0:T(8,128)(2,1)S(1)}, bf16[3,64,1792]{2,1,0:T(8,128)(2,1)S(1)}, u32[]{:S(2)}, u32[]{:S(2)}) collective-permute-start(bf16[3,64,1792]{2,1,0:T(8,128)(2,1)S(1)} %swiglu_part.3.refs_0_.refs_2_), channel_id=1, source_target_pairs={{1,0},{0,1},{3,2},{2,3},{5,4},{4,5},{7,6},{6,7},{9,8},{8,9},{11,10... | collective-permute-start | bytes 2064392 | tf_op jit(solution)/shard_map/ppermute | solution.py:420
  73.2 10.1 %copy-start.1 = (bf16[3,64,1792]{2,1,0:T(8,128)(2,1)S(1)}, bf16[3,64,1792]{2,1,0:T(8,128)(2,1)}, u32[]{:S(2)}) copy-start(bf16[3,64,1792]{2,1,0:T(8,128)(2,1)} %copy-done) | copy-start | bytes 2064388
  73.2 10.1 %copy-start.3 = (bf16[2048,128]{1,0:T(8,128)(2,1)S(1)}, bf16[2048,128]{1,0:T(8,128)(2,1)}, u32[]{:S(2)}) copy-start(bf16[2048,128]{1,0:T(8,128)(2,1)} %copy-done.2) | copy-start | bytes 1572868
  73.2 10.1 %copy-start.5 = (bf16[128,2048]{1,0:T(8,128)(2,1)S(1)}, bf16[128,2048]{1,0:T(8,128)(2,1)}, u32[]{:S(2)}) copy-start(bf16[128,2048]{1,0:T(8,128)(2,1)} %copy-done.4) | copy-start | bytes 1572868
  82.7 8.9 %collective-permute-start.18 = (bf16[64,2048]{1,0:T(8,128)(2,1)S(1)}, bf16[64,2048]{1,0:T(8,128)(2,1)S(1)}, u32[]{:S(2)}, u32[]{:S(2)}) collective-permute-start(bf16[64,2048]{1,0:T(8,128)(2,1)S(1)} %select_convert_fusion.refs_4_.refs_7_), channel_id=1, source_target_pairs={{4,0},{0,4},{12,8},{8,12},{20,16},{16,20},{28,24},{24,28},{5,1},{1... | collective-permute-start | bytes 786440 | tf_op jit(solution)/shard_map/ppermute | solution.py:420
  91.7 11.8 %collective-permute-start.19 = (bf16[16,2048]{1,0:T(8,128)(2,1)S(1)}, bf16[16,2048]{1,0:T(8,128)(2,1)S(1)}, u32[]{:S(2)}, u32[]{:S(2)}) collective-permute-start(bf16[16,2048]{1,0:T(8,128)(2,1)S(1)} %get-tuple-element.52), channel_id=1, source_target_pairs={{8,0},{12,4},{0,8},{4,12},{24,16},{28,20},{16,24},{20,28},{9,1},{1... | collective-permute-start | bytes 196616 | tf_op jit(solution)/shard_map/ppermute | solution.py:420
  91.8 11.8 %collective-permute-start.21 = (bf16[16,2048]{1,0:T(8,128)(2,1)S(1)}, bf16[16,2048]{1,0:T(8,128)(2,1)S(1)}, u32[]{:S(2)}, u32[]{:S(2)}) collective-permute-start(bf16[16,2048]{1,0:T(8,128)(2,1)S(1)} %get-tuple-element.53), channel_id=1, source_target_pairs={{24,0},{28,4},{16,8},{20,12},{8,16},{12,20},{0,24},{4,28},{25,1},{... | collective-permute-start | bytes 196616 | tf_op jit(solution)/shard_map/ppermute | solution.py:420
  93.7 9.8 %collective-permute-start.20 = (bf16[16,2048]{1,0:T(8,128)(2,1)S(1)}, bf16[16,2048]{1,0:T(8,128)(2,1)S(1)}, u32[]{:S(2)}, u32[]{:S(2)}) collective-permute-start(bf16[16,2048]{1,0:T(8,128)(2,1)S(1)} %get-tuple-element.54), channel_id=1, source_target_pairs={{16,0},{20,4},{24,8},{28,12},{0,16},{4,20},{8,24},{12,28},{17,1},{... | collective-permute-start | bytes 196616 | tf_op jit(solution)/shard_map/ppermute | solution.py:420

commit v3 on v2

--- a/solution.py
+++ b/solution.py
@@ -11,10 +11,11 @@
 BF16 = jnp.bfloat16
 ROWS = (((1,), (0,)), ((), ()))
 COLS = (((1,), (1,)), ((), ()))
-GATE_EDGES = (0, 7, 9, 12, 14)
-DOWN_EDGES = (0, 0, 7, 10, 14)
+GATE_EDGES = (0, 7, 13, 13, 14)
+DOWN_EDGES = (0, 0, 0, 9, 14)
 SPAN_EDGES = (0, 7, 14)
-FLIGHT = 6
+FLIGHT = 3
+PAIRS = 2
 ANYWHERE = pl.BlockSpec(memory_space=pl.ANY)
 RESIDENT = pl.BlockSpec(memory_space=pltpu.VMEM)
 
@@ -252,7 +253,7 @@
         )
         for i, part in enumerate(parts)
     ]
-    for pair in copies[: FLIGHT // 2]:
+    for pair in copies[:PAIRS]:
         for copy in pair:
             copy.start()
     gb = joined(mine, peer, 1)
@@ -260,7 +261,7 @@
     for i, (part, pair) in enumerate(zip(parts, copies)):
         for copy in pair:
             copy.wait()
-        for later in copies[i + FLIGHT // 2 : i + FLIGHT // 2 + 1]:
+        for later in copies[i + PAIRS : i + PAIRS + 1]:
             for copy in later:
                 copy.start()
         value = lax.dot_general(gb, gate_buf[part, :], COLS, preferred_element_type=F32)
@@ -511,7 +512,7 @@
         first = spans[i][0] * tile
         return input_part(prev, mine, peer, weights[gate_key], weights[up_key], first, after)
 
-    acts = [act(0, narrows[-2:-1])]
+    acts = [act(0, narrows[-1:])]
     total = tokens_grad(None, 0, narrows[-1:])
     for i in range(1, n):
         acts.append(act(i, [total]))

time: 104 us -> 103 us (level)
  starting transfers between devices: 23.3 us -> 20.9 us
  Pallas kernels: 57.2 us -> 58.5 us
    ppermute x22, starting transfers between devices: 23.3 us -> 20.9 us  [swap(): return lax.ppermute(value, axis, [(i ^ bit, i) for i in range(size)])]
    pallas_call x3, Pallas kernels: 16.6 us -> 17.8 us  [forward_part(): pl.pallas_call(functools.partial(forward_kernel, jobs, tile, kinds), in_s...]
  transfers between devices with their start and end apart: 22 -> 22, of which waited for: 13 -> 13; matrix products, arithmetic and copies ran while one was open for 0% -> 0% of each run, Pallas kernels for 46% -> 48%
where the time goes in v3:
time: 103 us
  Pallas kernels  58.5 us (57%)
  starting transfers between devices  20.9 us (20%)
  waiting for transfers between devices  20.4 us (20%)
    ppermute x22, starting transfers between devices, swap(): return lax.ppermute(value, axis, [(i ^ bit, i) for i in range(size)])  20.9 us
    ppermute x22, waiting for transfers between devices, swap(): return lax.ppermute(value, axis, [(i ^ bit, i) for i in range(size)])  20.4 us
    pallas_call x3, Pallas kernels, forward_part(): pl.pallas_call(functools.partial(forward_kernel, jobs, tile, kinds), in_s...  17.8 us
    pallas_call x2, Pallas kernels, weight_part(): pl.pallas_call(functools.partial(weight_kernel, firsts, tile), in_specs=[...  16.5 us
    pallas_call x2, Pallas kernels, input_part(): pl.pallas_call(functools.partial(input_kernel, has_prev, first), in_specs...  14.9 us
    pallas_call x1, Pallas kernels, load_part(): pl.pallas_call(functools.partial(load_kernel, first), in_specs=[ANYWHERE]...  5.36 us
    pallas_call x2, Pallas kernels, first_part(): pl.pallas_call(functools.partial(first_kernel, tile, len(prev) > 0), in_s...  2.3 us
  transfers between devices with their start and end apart: 22, of which 13 were waited for; matrix products, arithmetic and copies ran while one was open for 0% of the time, Pallas kernels for 48%

profile of v3, /device:TPU:0, one launch (start us, length us, event | category | flops | bytes accessed | tf_op | source)
XLA Modules:
  0.0 102.6 jit_solution(11114573986635506788)
XLA Ops:
  0.7 4.1 %collective-permute-start.1 = (bf16[16,2048]{1,0:T(8,128)(2,1)}, bf16[16,2048]{1,0:T(8,128)(2,1)S(1)}, u32[]{:S(2)}, u32[]{:S(2)}) collective-permute-start(bf16[16,2048]{1,0:T(8,128)(2,1)} %refs_0_.2), channel_id=1, source_target_pairs={{16,0},{20,4},{24,8},{28,12},{0,16},{4,20},{8,24},{12,28},{17,1},{... | collective-permute-start | bytes 196616 | tf_op jit(solution)/shard_map/ppermute | solution.py:421
  4.8 1.6 %collective-permute-start = (bf16[16,2048]{1,0:T(8,128)(2,1)}, bf16[16,2048]{1,0:T(8,128)(2,1)S(1)}, u32[]{:S(2)}, u32[]{:S(2)}) collective-permute-start(bf16[16,2048]{1,0:T(8,128)(2,1)} %refs_0_.2), channel_id=1, source_target_pairs={{8,0},{12,4},{0,8},{4,12},{24,16},{28,20},{16,24},{20,28},{9,1},{1... | collective-permute-start | bytes 196616 | tf_op jit(solution)/shard_map/ppermute | solution.py:421
  6.3 5.4 %load_part.1 = (bf16[2048,1792]{1,0:T(8,128)(2,1)S(1)}, bf16[2048,1792]{1,0:T(8,128)(2,1)S(1)}, f32[8,128]{1,0:T(8,128)S(1)}) custom-call(bf16[2048,3584]{1,0:T(8,128)(2,1)} %refs_2_.7, bf16[2048,3584]{1,0:T(8,128)(2,1)} %refs_3_.5), custom_call_target="tpu_custom_call" | custom-call | bytes 14680064 | tf_op jit(solution)/shard_map/load_part/pallas_call | solution.py:58
  11.7 0.9 collective-permute-done.2.refs_3_
  12.6 1.6 %collective-permute-start.3 = (bf16[64,2048]{1,0:T(8,128)(2,1)S(1)}, bf16[64,2048]{1,0:T(8,128)(2,1)S(1)}, u32[]{:S(2)}, u32[]{:S(2)}) collective-permute-start(bf16[64,2048]{1,0:T(8,128)(2,1)S(1)} %stack_part.2.own), channel_id=1, source_target_pairs={{4,0},{0,4},{12,8},{8,12},{20,16},{16,20},{28,24},{24,28},{5,1},{1... | collective-permute-start | bytes 786440 | tf_op jit(solution)/shard_map/ppermute | solution.py:421
  14.2 1.3 %collective-permute-start.5 = (bf16[16,2048]{1,0:T(8,128)(2,1)S(1)}, bf16[16,2048]{1,0:T(8,128)(2,1)S(1)}, u32[]{:S(2)}, u32[]{:S(2)}) collective-permute-start(bf16[16,2048]{1,0:T(8,128)(2,1)S(1)} %copy-done.7), channel_id=1, source_target_pairs={{16,0},{20,4},{24,8},{28,12},{0,16},{4,20},{8,24},{12,28},{17,1},{... | collective-permute-start | bytes 196616 | tf_op jit(solution)/shard_map/ppermute | solution.py:421
  15.5 2.2 %collective-permute-start.4 = (bf16[16,2048]{1,0:T(8,128)(2,1)S(1)}, bf16[16,2048]{1,0:T(8,128)(2,1)S(1)}, u32[]{:S(2)}, u32[]{:S(2)}) collective-permute-start(bf16[16,2048]{1,0:T(8,128)(2,1)S(1)} %copy-done.7), channel_id=1, source_target_pairs={{8,0},{12,4},{0,8},{4,12},{24,16},{28,20},{16,24},{20,28},{9,1},{1... | collective-permute-start | bytes 196616 | tf_op jit(solution)/shard_map/ppermute | solution.py:421
  17.7 0.9 collective-permute-start.6
  18.6 0.7 collective-permute-done.3.theirs
  19.6 1.1 %first_part.2 = (f32[64,3584]{1,0:T(8,128)S(1)}, bf16[64,3584]{1,0:T(8,128)(2,1)S(1)}) custom-call(bf16[128,2048]{1,0:T(8,128)(2,1)S(1)} %get-tuple-element.28.x.refs_0_.refs_1_, bf16[2048,1792]{1,0:T(8,128)(2,1)S(1)} %get-tuple-element.30.weight), custom_call_target="tpu_custom_call" | custom-call | flops 29360128 | bytes 229376 | tf_op jit(solution)/shard_map/first_part/pallas_call | solution.py:147
  20.9 2.9 %collective-permute-done.6.refs_4_.refs_3_ = bf16[16,2048]{1,0:T(8,128)(2,1)S(1)} collective-permute-done((bf16[16,2048]{1,0:T(8,128)(2,1)S(1)}, bf16[16,2048]{1,0:T(8,128)(2,1)S(1)}, u32[]{:S(2)}, u32[]{:S(2)}) %collective-permute-start.6) | collective-permute-done | bytes 65568 | tf_op jit(solution)/shard_map/ppermute | solution.py:421
  23.8 1.2 %first_part.3 = (f32[64,3584]{1,0:T(8,128)S(1)}, bf16[64,3584]{1,0:T(8,128)(2,1)S(1)}) custom-call(bf16[128,2048]{1,0:T(8,128)(2,1)S(1)} %get-tuple-element.28.x.refs_0_.refs_1_, bf16[2048,1792]{1,0:T(8,128)(2,1)S(1)} %get-tuple-element.29.weight, f32[64,3584]{1,0:T(8,128)S(1)} %get-tuple-element.31.refs_0_, bf16[64,3584]{1,0:T(8,128)(2,1)S(1)} %get-tuple-element.32.refs_1_, ...), custom_call_target="tpu_custom_call" | custom-call | flops 29360128 | bytes 229376 | tf_op jit(solution)/shard_map/first_part/pallas_call | solution.py:147
  25.0 1.8 %collective-permute-done.7.got.refs_1_ = bf16[64,3584]{1,0:T(8,128)(2,1)S(1)} collective-permute-done((bf16[64,3584]{1,0:T(8,128)(2,1)S(1)}, bf16[64,3584]{1,0:T(8,128)(2,1)S(1)}, u32[]{:S(2)}, u32[]{:S(2)}) %collective-permute-start.7) | collective-permute-done | bytes 458784 | tf_op jit(solution)/shard_map/ppermute | solution.py:421
  26.9 1.6 %collective-permute-start.11 = (bf16[64,3584]{1,0:T(8,128)(2,1)S(1)}, bf16[64,3584]{1,0:T(8,128)(2,1)S(1)}, u32[]{:S(2)}, u32[]{:S(2)}) collective-permute-start(bf16[64,3584]{1,0:T(8,128)(2,1)S(1)} %add_part.4.refs_3_), channel_id=1, source_target_pairs={{2,0},{3,1},{0,2},{1,3},{6,4},{7,5},{4,6},{5,7},{10,8},{11,9},{8,1... | collective-permute-start | bytes 1376264 | tf_op jit(solution)/shard_map/ppermute | solution.py:421
  28.5 5.6 %forward_part.3 = (f32[64,3072]{1,0:T(8,128)S(1)}, bf16[64,3072]{1,0:T(8,128)(2,1)S(1)}) custom-call(bf16[128,2048]{1,0:T(8,128)(2,1)S(1)} %get-tuple-element.28.x.refs_0_.refs_1_, bf16[2048,3584]{1,0:T(8,128)(2,1)} %refs_2_.7, bf16[2048,3584]{1,0:T(8,128)(2,1)} %refs_3_.5, bf16[64,3584]{1,0:T(8,128)(2,1)S(1)} %add_part.4.refs_3_), custom_call_target="tpu_custom_call" | custom-call | flops 100663296 | bytes 393216 | tf_op jit(solution)/shard_map/forward_part/pallas_call | solution.py:218
  34.8 1.1 %collective-permute-done.8.got.refs_1_ = bf16[64,3072]{1,0:T(8,128)(2,1)S(1)} collective-permute-done((bf16[64,3072]{1,0:T(8,128)(2,1)S(1)}, bf16[64,3072]{1,0:T(8,128)(2,1)S(1)}, u32[]{:S(2)}, u32[]{:S(2)}) %collective-permute-start.8) | collective-permute-done | bytes 393248 | tf_op jit(solution)/shard_map/ppermute | solution.py:421
  36.5 6.4 %collective-permute-done.10.theirs = bf16[64,2048]{1,0:T(8,128)(2,1)S(1)} collective-permute-done((bf16[64,2048]{1,0:T(8,128)(2,1)S(1)}, bf16[64,2048]{1,0:T(8,128)(2,1)S(1)}, u32[]{:S(2)}, u32[]{:S(2)}) %collective-permute-start.10) | collective-permute-done | bytes 262176 | tf_op jit(solution)/shard_map/ppermute | solution.py:421
  43.2 0.8 copy-done.4
  44.0 5.7 %forward_part.4 = (f32[64,2304]{1,0:T(8,128)S(1)}, bf16[64,2304]{1,0:T(8,128)(2,1)S(1)}) custom-call(bf16[2048,128]{1,0:T(8,128)(2,1)S(1)} %get-tuple-element.37.refs_0_, bf16[3584,2048]{1,0:T(8,128)(2,1)} %refs_2_.5, bf16[64,3072]{1,0:T(8,128)(2,1)S(1)} %add_part.5.refs_2_, bf16[64,3584]{1,0:T(8,128)(2,1)S(1)} %collective-permute-done.11.refs_3_.refs_2_), custom_call_target="tpu_custom_call" | custom-call | flops 75497472 | bytes 294912 | tf_op jit(solution)/shard_map/forward_part/pallas_call | solution.py:218
  49.9 1.6 %collective-permute-done.12.got.refs_4_ = bf16[64,2304]{1,0:T(8,128)(2,1)S(1)} collective-permute-done((bf16[64,2304]{1,0:T(8,128)(2,1)S(1)}, bf16[64,2304]{1,0:T(8,128)(2,1)S(1)}, u32[]{:S(2)}, u32[]{:S(2)}) %collective-permute-start.12) | collective-permute-done | bytes 294944 | tf_op jit(solution)/shard_map/ppermute | solution.py:421
  52.1 6.5 %forward_part.5 = (f32[64,1792]{1,0:T(8,128)S(1)}, bf16[64,1792]{1,0:T(8,128)(2,1)S(1)}) custom-call(bf16[2048,128]{1,0:T(8,128)(2,1)S(1)} %get-tuple-element.37.refs_0_, bf16[128,2048]{1,0:T(8,128)(2,1)S(1)} %get-tuple-element.28.x.refs_0_.refs_1_, bf16[3584,2048]{1,0:T(8,128)(2,1)} %refs_2_.5, bf16[2048,3584]{1,0:T(8,128)(2,1)} %refs_2_.7, ...), custom_call_target="tpu_custom_call" | custom-call | flops 58720256 | bytes 229376 | tf_op jit(solution)/shard_map/forward_part/pallas_call | solution.py:218
  58.7 1.5 %collective-permute-done.14.got.refs_7_ = bf16[64,1792]{1,0:T(8,128)(2,1)S(1)} collective-permute-done((bf16[64,1792]{1,0:T(8,128)(2,1)S(1)}, bf16[64,1792]{1,0:T(8,128)(2,1)S(1)}, u32[]{:S(2)}, u32[]{:S(2)}) %collective-permute-start.14) | collective-permute-done | bytes 229408 | tf_op jit(solution)/shard_map/ppermute | solution.py:421
  61.1 1.2 %collective-permute-start.15 = (bf16[64,1792]{1,0:T(8,128)(2,1)S(1)}, bf16[64,1792]{1,0:T(8,128)(2,1)S(1)}, u32[]{:S(2)}, u32[]{:S(2)}) collective-permute-start(bf16[64,1792]{1,0:T(8,128)(2,1)S(1)} %add_part.7.refs_6_.refs_4_), channel_id=1, source_target_pairs={{2,0},{3,1},{0,2},{1,3},{6,4},{7,5},{4,6},{5,7},{10,8},{11,9},{8,1... | collective-permute-start | bytes 688136 | tf_op jit(solution)/shard_map/ppermute | solution.py:421
  62.3 0.9 collective-permute-done.16.refs_1_.refs_3_
  63.3 7.6 %input_part.2.refs_9_.refs_4_ = f32[128,2048]{1,0:T(8,128)S(1)} custom-call(bf16[3,64,1792]{2,1,0:T(8,128)(2,1)S(1)} %swiglu_part.2.refs_0_.refs_2_, bf16[3,64,1792]{2,1,0:T(8,128)(2,1)S(1)} %collective-permute-done.16.refs_1_.refs_3_, bf16[2048,3584]{1,0:T(8,128)(2,1)} %refs_2_.7, bf16[2048,3584]{1,0:T(8,128)(2,1)} %refs_3_.5, ...), custom_call_target="tpu_custom_call" | custom-call | flops 1879048192 | bytes 14680064 | tf_op jit(solution)/shard_map/input_part/pallas_call | solution.py:275
  71.5 2.0 %collective-permute-done.17.refs_1_.refs_3_ = bf16[3,64,1792]{2,1,0:T(8,128)(2,1)S(1)} collective-permute-done((bf16[3,64,1792]{2,1,0:T(8,128)(2,1)S(1)}, bf16[3,64,1792]{2,1,0:T(8,128)(2,1)S(1)}, u32[]{:S(2)}, u32[]{:S(2)}) %collective-permute-start.17) | collective-permute-done | bytes 688160 | tf_op jit(solution)/shard_map/ppermute | solution.py:421
  73.5 7.3 %input_part.3 = f32[128,2048]{1,0:T(8,128)S(1)} custom-call(bf16[3,64,1792]{2,1,0:T(8,128)(2,1)S(1)} %swiglu_part.3.refs_0_.refs_2_, bf16[3,64,1792]{2,1,0:T(8,128)(2,1)S(1)} %collective-permute-done.17.refs_1_.refs_3_, bf16[2048,3584]{1,0:T(8,128)(2,1)} %refs_2_.7, bf16[2048,3584]{1,0:T(8,128)(2,1)} %refs_3_.5, f32[128,2048]{1,0:T(8,128)S(1)} %input_part.2.refs_9_.refs_4_), custom_call_target="tpu_custom_call" | custom-call | flops 1879048192 | bytes 14680064 | tf_op jit(solution)/shard_map/input_part/pallas_call | solution.py:275
  81.5 8.3 %weight_part.2 = (bf16[2048,3584]{1,0:T(8,128)(2,1)}, bf16[2048,3584]{1,0:T(8,128)(2,1)}, bf16[3584,2048]{1,0:T(8,128)(2,1)}) custom-call(bf16[2048,128]{1,0:T(8,128)(2,1)S(1)} %copy-done.3, bf16[128,2048]{1,0:T(8,128)(2,1)S(1)} %copy-done.5, bf16[3,64,1792]{2,1,0:T(8,128)(2,1)S(1)} %swiglu_part.2.refs_0_.refs_2_, bf16[3,64,1792]{2,1,0:T(8,128)(2,1)S(1)} %copy-done.1, ...), custom_call_target="tpu_custom_call" | custom-call | flops 2818572288 | bytes 22020096 | tf_op jit(solution)/shard_map/weight_part/pallas_call | solution.py:341
  90.2 1.9 %collective-permute-start.21 = (bf16[16,2048]{1,0:T(8,128)(2,1)S(1)}, bf16[16,2048]{1,0:T(8,128)(2,1)S(1)}, u32[]{:S(2)}, u32[]{:S(2)}) collective-permute-start(bf16[16,2048]{1,0:T(8,128)(2,1)S(1)} %get-tuple-element.53), channel_id=1, source_target_pairs={{24,0},{28,4},{16,8},{20,12},{8,16},{12,20},{0,24},{4,28},{25,1},{... | collective-permute-start | bytes 196616 | tf_op jit(solution)/shard_map/ppermute | solution.py:421
  92.1 1.5 %collective-permute-start.20 = (bf16[16,2048]{1,0:T(8,128)(2,1)S(1)}, bf16[16,2048]{1,0:T(8,128)(2,1)S(1)}, u32[]{:S(2)}, u32[]{:S(2)}) collective-permute-start(bf16[16,2048]{1,0:T(8,128)(2,1)S(1)} %get-tuple-element.54), channel_id=1, source_target_pairs={{16,0},{20,4},{24,8},{28,12},{0,16},{4,20},{8,24},{12,28},{17,1},{... | collective-permute-start | bytes 196616 | tf_op jit(solution)/shard_map/ppermute | solution.py:421
  93.6 8.3 %weight_part.3 = (bf16[2048,3584]{1,0:T(8,128)(2,1)}, bf16[2048,3584]{1,0:T(8,128)(2,1)}, bf16[3584,2048]{1,0:T(8,128)(2,1)}) custom-call(bf16[2048,128]{1,0:T(8,128)(2,1)S(1)} %copy-done.3, bf16[128,2048]{1,0:T(8,128)(2,1)S(1)} %copy-done.5, ...), custom_call_target="tpu_custom_call", output_to_operand_aliasing={{0}: (4, {}), {1}: (5, {}), {2}: (6, {})} | custom-call | flops 2818572288 | bytes 22020096 | tf_op jit(solution)/shard_map/weight_part/pallas_call | solution.py:341
  101.9 0.7 fusion.2
  (52 shorter events, 5.6 us)
Async XLA Ops:
  0.6 12.0 %copy-start.6 = (bf16[16,2048]{1,0:T(8,128)(2,1)S(1)}, bf16[16,2048]{1,0:T(8,128)(2,1)}, u32[]{:S(2)}) copy-start(bf16[16,2048]{1,0:T(8,128)(2,1)} %refs_0_.2) | copy-start | bytes 196612
  0.6 13.5 %copy-start.7 = (bf16[16,2048]{1,0:T(8,128)(2,1)S(1)}, bf16[16,2048]{1,0:T(8,128)(2,1)}, u32[]{:S(2)}) copy-start(bf16[16,2048]{1,0:T(8,128)(2,1)} %refs_0_.3) | copy-start | bytes 196612
  0.7 11.0 %collective-permute-start.1 = (bf16[16,2048]{1,0:T(8,128)(2,1)}, bf16[16,2048]{1,0:T(8,128)(2,1)S(1)}, u32[]{:S(2)}, u32[]{:S(2)}) collective-permute-start(bf16[16,2048]{1,0:T(8,128)(2,1)} %refs_0_.2), channel_id=1, source_target_pairs={{16,0},{20,4},{24,8},{28,12},{0,16},{4,20},{8,24},{12,28},{17,1},{... | collective-permute-start | bytes 196616 | tf_op jit(solution)/shard_map/ppermute | solution.py:421
  4.8 7.0 %collective-permute-start = (bf16[16,2048]{1,0:T(8,128)(2,1)}, bf16[16,2048]{1,0:T(8,128)(2,1)S(1)}, u32[]{:S(2)}, u32[]{:S(2)}) collective-permute-start(bf16[16,2048]{1,0:T(8,128)(2,1)} %refs_0_.2), channel_id=1, source_target_pairs={{8,0},{12,4},{0,8},{4,12},{24,16},{28,20},{16,24},{20,28},{9,1},{1... | collective-permute-start | bytes 196616 | tf_op jit(solution)/shard_map/ppermute | solution.py:421
  6.3 6.3 %collective-permute-start.2 = (bf16[16,2048]{1,0:T(8,128)(2,1)}, bf16[16,2048]{1,0:T(8,128)(2,1)S(1)}, u32[]{:S(2)}, u32[]{:S(2)}) collective-permute-start(bf16[16,2048]{1,0:T(8,128)(2,1)} %refs_0_.2), channel_id=1, source_target_pairs={{24,0},{28,4},{16,8},{20,12},{8,16},{12,20},{0,24},{4,28},{25,1},{... | collective-permute-start | bytes 196616 | tf_op jit(solution)/shard_map/ppermute | solution.py:421
  12.6 6.7 %collective-permute-start.3 = (bf16[64,2048]{1,0:T(8,128)(2,1)S(1)}, bf16[64,2048]{1,0:T(8,128)(2,1)S(1)}, u32[]{:S(2)}, u32[]{:S(2)}) collective-permute-start(bf16[64,2048]{1,0:T(8,128)(2,1)S(1)} %stack_part.2.own), channel_id=1, source_target_pairs={{4,0},{0,4},{12,8},{8,12},{20,16},{16,20},{28,24},{24,28},{5,1},{1... | collective-permute-start | bytes 786440 | tf_op jit(solution)/shard_map/ppermute | solution.py:421
  14.2 6.6 %collective-permute-start.5 = (bf16[16,2048]{1,0:T(8,128)(2,1)S(1)}, bf16[16,2048]{1,0:T(8,128)(2,1)S(1)}, u32[]{:S(2)}, u32[]{:S(2)}) collective-permute-start(bf16[16,2048]{1,0:T(8,128)(2,1)S(1)} %copy-done.7), channel_id=1, source_target_pairs={{16,0},{20,4},{24,8},{28,12},{0,16},{4,20},{8,24},{12,28},{17,1},{... | collective-permute-start | bytes 196616 | tf_op jit(solution)/shard_map/ppermute | solution.py:421
  15.5 5.4 %collective-permute-start.4 = (bf16[16,2048]{1,0:T(8,128)(2,1)S(1)}, bf16[16,2048]{1,0:T(8,128)(2,1)S(1)}, u32[]{:S(2)}, u32[]{:S(2)}) collective-permute-start(bf16[16,2048]{1,0:T(8,128)(2,1)S(1)} %copy-done.7), channel_id=1, source_target_pairs={{8,0},{12,4},{0,8},{4,12},{24,16},{28,20},{16,24},{20,28},{9,1},{1... | collective-permute-start | bytes 196616 | tf_op jit(solution)/shard_map/ppermute | solution.py:421
  17.7 6.1 %collective-permute-start.6 = (bf16[16,2048]{1,0:T(8,128)(2,1)S(1)}, bf16[16,2048]{1,0:T(8,128)(2,1)S(1)}, u32[]{:S(2)}, u32[]{:S(2)}) collective-permute-start(bf16[16,2048]{1,0:T(8,128)(2,1)S(1)} %copy-done.7), channel_id=1, source_target_pairs={{24,0},{28,4},{16,8},{20,12},{8,16},{12,20},{0,24},{4,28},{25,1},{... | collective-permute-start | bytes 196616 | tf_op jit(solution)/shard_map/ppermute | solution.py:421
  19.6 7.4 %copy-start.2 = (bf16[2048,128]{1,0:T(8,128)(2,1)}, bf16[2048,128]{1,0:T(8,128)(2,1)S(1)}, u32[]{:S(2)}) copy-start(bf16[2048,128]{1,0:T(8,128)(2,1)S(1)} %get-tuple-element.42.refs_0_) | copy-start | bytes 1572868
  25.0 1.9 %collective-permute-start.7 = (bf16[64,3584]{1,0:T(8,128)(2,1)S(1)}, bf16[64,3584]{1,0:T(8,128)(2,1)S(1)}, u32[]{:S(2)}, u32[]{:S(2)}) collective-permute-start(bf16[64,3584]{1,0:T(8,128)(2,1)S(1)} %get-tuple-element.34.refs_4_), channel_id=1, source_target_pairs={{1,0},{0,1},{3,2},{2,3},{5,4},{4,5},{7,6},{6,7},{9,8},{8,9},{11,10... | collective-permute-start | bytes 1376264 | tf_op jit(solution)/shard_map/ppermute | solution.py:421
  26.9 17.1 %collective-permute-start.11 = (bf16[64,3584]{1,0:T(8,128)(2,1)S(1)}, bf16[64,3584]{1,0:T(8,128)(2,1)S(1)}, u32[]{:S(2)}, u32[]{:S(2)}) collective-permute-start(bf16[64,3584]{1,0:T(8,128)(2,1)S(1)} %add_part.4.refs_3_), channel_id=1, source_target_pairs={{2,0},{3,1},{0,2},{1,3},{6,4},{7,5},{4,6},{5,7},{10,8},{11,9},{8,1... | collective-permute-start | bytes 1376264 | tf_op jit(solution)/shard_map/ppermute | solution.py:421
  34.1 1.8 %collective-permute-start.8 = (bf16[64,3072]{1,0:T(8,128)(2,1)S(1)}, bf16[64,3072]{1,0:T(8,128)(2,1)S(1)}, u32[]{:S(2)}, u32[]{:S(2)}) collective-permute-start(bf16[64,3072]{1,0:T(8,128)(2,1)S(1)} %get-tuple-element.36), channel_id=1, source_target_pairs={{1,0},{0,1},{3,2},{2,3},{5,4},{4,5},{7,6},{6,7},{9,8},{8,9},{11,10... | collective-permute-start | bytes 1179656 | tf_op jit(solution)/shard_map/ppermute | solution.py:421
  34.2 8.8 %collective-permute-start.10 = (bf16[64,2048]{1,0:T(8,128)(2,1)S(1)}, bf16[64,2048]{1,0:T(8,128)(2,1)S(1)}, u32[]{:S(2)}, u32[]{:S(2)}) collective-permute-start(bf16[64,2048]{1,0:T(8,128)(2,1)S(1)} %stack_part.3.own), channel_id=1, source_target_pairs={{4,0},{0,4},{12,8},{8,12},{20,16},{16,20},{28,24},{24,28},{5,1},{1... | collective-permute-start | bytes 786440 | tf_op jit(solution)/shard_map/ppermute | solution.py:421
  36.0 16.1 %collective-permute-start.9 = (bf16[64,3072]{1,0:T(8,128)(2,1)S(1)}, bf16[64,3072]{1,0:T(8,128)(2,1)S(1)}, u32[]{:S(2)}, u32[]{:S(2)}) collective-permute-start(bf16[64,3072]{1,0:T(8,128)(2,1)S(1)} %add_part.5.refs_2_), channel_id=1, source_target_pairs={{2,0},{3,1},{0,2},{1,3},{6,4},{7,5},{4,6},{5,7},{10,8},{11,9},{8,1... | collective-permute-start | bytes 1179656 | tf_op jit(solution)/shard_map/ppermute | solution.py:421
  43.2 0.8 copy-start.4
  49.8 1.6 %collective-permute-start.12 = (bf16[64,2304]{1,0:T(8,128)(2,1)S(1)}, bf16[64,2304]{1,0:T(8,128)(2,1)S(1)}, u32[]{:S(2)}, u32[]{:S(2)}) collective-permute-start(bf16[64,2304]{1,0:T(8,128)(2,1)S(1)} %get-tuple-element.39), channel_id=1, source_target_pairs={{1,0},{0,1},{3,2},{2,3},{5,4},{4,5},{7,6},{6,7},{9,8},{8,9},{11,10... | collective-permute-start | bytes 884744 | tf_op jit(solution)/shard_map/ppermute | solution.py:421
  51.5 9.1 %collective-permute-start.13 = (bf16[64,2304]{1,0:T(8,128)(2,1)S(1)}, bf16[64,2304]{1,0:T(8,128)(2,1)S(1)}, u32[]{:S(2)}, u32[]{:S(2)}) collective-permute-start(bf16[64,2304]{1,0:T(8,128)(2,1)S(1)} %add_part.6.refs_5_), channel_id=1, source_target_pairs={{2,0},{3,1},{0,2},{1,3},{6,4},{7,5},{4,6},{5,7},{10,8},{11,9},{8,1... | collective-permute-start | bytes 884744 | tf_op jit(solution)/shard_map/ppermute | solution.py:421
  58.6 1.6 %collective-permute-start.14 = (bf16[64,1792]{1,0:T(8,128)(2,1)S(1)}, bf16[64,1792]{1,0:T(8,128)(2,1)S(1)}, u32[]{:S(2)}, u32[]{:S(2)}) collective-permute-start(bf16[64,1792]{1,0:T(8,128)(2,1)S(1)} %get-tuple-element.41), channel_id=1, source_target_pairs={{1,0},{0,1},{3,2},{2,3},{5,4},{4,5},{7,6},{6,7},{9,8},{8,9},{11,10... | collective-permute-start | bytes 688136 | tf_op jit(solution)/shard_map/ppermute | solution.py:421
  61.1 2.2 %collective-permute-start.16 = (bf16[3,64,1792]{2,1,0:T(8,128)(2,1)S(1)}, bf16[3,64,1792]{2,1,0:T(8,128)(2,1)S(1)}, u32[]{:S(2)}, u32[]{:S(2)}) collective-permute-start(bf16[3,64,1792]{2,1,0:T(8,128)(2,1)S(1)} %swiglu_part.2.refs_0_.refs_2_), channel_id=1, source_target_pairs={{1,0},{0,1},{3,2},{2,3},{5,4},{4,5},{7,6},{6,7},{9,8},{8,9},{11,10... | collective-permute-start | bytes 2064392 | tf_op jit(solution)/shard_map/ppermute | solution.py:421
  61.1 9.7 %collective-permute-start.15 = (bf16[64,1792]{1,0:T(8,128)(2,1)S(1)}, bf16[64,1792]{1,0:T(8,128)(2,1)S(1)}, u32[]{:S(2)}, u32[]{:S(2)}) collective-permute-start(bf16[64,1792]{1,0:T(8,128)(2,1)S(1)} %add_part.7.refs_6_.refs_4_), channel_id=1, source_target_pairs={{2,0},{3,1},{0,2},{1,3},{6,4},{7,5},{4,6},{5,7},{10,8},{11,9},{8,1... | collective-permute-start | bytes 688136 | tf_op jit(solution)/shard_map/ppermute | solution.py:421
  63.3 7.6 %copy-start = (bf16[3,64,1792]{2,1,0:T(8,128)(2,1)}, bf16[3,64,1792]{2,1,0:T(8,128)(2,1)S(1)}, u32[]{:S(2)}) copy-start(bf16[3,64,1792]{2,1,0:T(8,128)(2,1)S(1)} %collective-permute-done.16.refs_1_.refs_3_) | copy-start | bytes 2064388
  71.3 2.2 %collective-permute-start.17 = (bf16[3,64,1792]{2,1,0:T(8,128)(2,1)S(1)}, bf16[3,64,1792]{2,1,0:T(8,128)(2,1)S(1)}, u32[]{:S(2)}, u32[]{:S(2)}) collective-permute-start(bf16[3,64,1792]{2,1,0:T(8,128)(2,1)S(1)} %swiglu_part.3.refs_0_.refs_2_), channel_id=1, source_target_pairs={{1,0},{0,1},{3,2},{2,3},{5,4},{4,5},{7,6},{6,7},{9,8},{8,9},{11,10... | collective-permute-start | bytes 2064392 | tf_op jit(solution)/shard_map/ppermute | solution.py:421
  71.5 10.0 %copy-start.1 = (bf16[3,64,1792]{2,1,0:T(8,128)(2,1)S(1)}, bf16[3,64,1792]{2,1,0:T(8,128)(2,1)}, u32[]{:S(2)}) copy-start(bf16[3,64,1792]{2,1,0:T(8,128)(2,1)} %copy-done) | copy-start | bytes 2064388
  71.5 10.0 %copy-start.3 = (bf16[2048,128]{1,0:T(8,128)(2,1)S(1)}, bf16[2048,128]{1,0:T(8,128)(2,1)}, u32[]{:S(2)}) copy-start(bf16[2048,128]{1,0:T(8,128)(2,1)} %copy-done.2) | copy-start | bytes 1572868
  71.5 10.0 %copy-start.5 = (bf16[128,2048]{1,0:T(8,128)(2,1)S(1)}, bf16[128,2048]{1,0:T(8,128)(2,1)}, u32[]{:S(2)}) copy-start(bf16[128,2048]{1,0:T(8,128)(2,1)} %copy-done.4) | copy-start | bytes 1572868
  80.9 8.9 %collective-permute-start.18 = (bf16[64,2048]{1,0:T(8,128)(2,1)S(1)}, bf16[64,2048]{1,0:T(8,128)(2,1)S(1)}, u32[]{:S(2)}, u32[]{:S(2)}) collective-permute-start(bf16[64,2048]{1,0:T(8,128)(2,1)S(1)} %select_convert_fusion.refs_4_.refs_7_), channel_id=1, source_target_pairs={{4,0},{0,4},{12,8},{8,12},{20,16},{16,20},{28,24},{24,28},{5,1},{1... | collective-permute-start | bytes 786440 | tf_op jit(solution)/shard_map/ppermute | solution.py:421
  90.1 11.8 %collective-permute-start.19 = (bf16[16,2048]{1,0:T(8,128)(2,1)S(1)}, bf16[16,2048]{1,0:T(8,128)(2,1)S(1)}, u32[]{:S(2)}, u32[]{:S(2)}) collective-permute-start(bf16[16,2048]{1,0:T(8,128)(2,1)S(1)} %get-tuple-element.52), channel_id=1, source_target_pairs={{8,0},{12,4},{0,8},{4,12},{24,16},{28,20},{16,24},{20,28},{9,1},{1... | collective-permute-start | bytes 196616 | tf_op jit(solution)/shard_map/ppermute | solution.py:421
  90.2 11.8 %collective-permute-start.21 = (bf16[16,2048]{1,0:T(8,128)(2,1)S(1)}, bf16[16,2048]{1,0:T(8,128)(2,1)S(1)}, u32[]{:S(2)}, u32[]{:S(2)}) collective-permute-start(bf16[16,2048]{1,0:T(8,128)(2,1)S(1)} %get-tuple-element.53), channel_id=1, source_target_pairs={{24,0},{28,4},{16,8},{20,12},{8,16},{12,20},{0,24},{4,28},{25,1},{... | collective-permute-start | bytes 196616 | tf_op jit(solution)/shard_map/ppermute | solution.py:421
  92.1 9.8 %collective-permute-start.20 = (bf16[16,2048]{1,0:T(8,128)(2,1)S(1)}, bf16[16,2048]{1,0:T(8,128)(2,1)S(1)}, u32[]{:S(2)}, u32[]{:S(2)}) collective-permute-start(bf16[16,2048]{1,0:T(8,128)(2,1)S(1)} %get-tuple-element.54), channel_id=1, source_target_pairs={{16,0},{20,4},{24,8},{28,12},{0,16},{4,20},{8,24},{12,28},{17,1},{... | collective-permute-start | bytes 196616 | tf_op jit(solution)/shard_map/ppermute | solution.py:421

commit v4 on v3

--- a/solution.py
+++ b/solution.py
@@ -11,10 +11,10 @@
 BF16 = jnp.bfloat16
 ROWS = (((1,), (0,)), ((), ()))
 COLS = (((1,), (1,)), ((), ()))
-GATE_EDGES = (0, 7, 13, 13, 14)
-DOWN_EDGES = (0, 0, 0, 9, 14)
+GATE_EDGES = (0, 8, 14, 14, 14)
+DOWN_EDGES = (0, 0, 0, 8, 14)
 SPAN_EDGES = (0, 7, 14)
-FLIGHT = 3
+FLIGHT = 4
 PAIRS = 2
 ANYWHERE = pl.BlockSpec(memory_space=pl.ANY)
 RESIDENT = pl.BlockSpec(memory_space=pltpu.VMEM)

time: 103 us -> 102 us (level)
  waiting for transfers between devices: 20.4 us -> 22.5 us
  Pallas kernels: 58.5 us -> 56.6 us
    pallas_call x3, Pallas kernels: 17.8 us -> 14.8 us  [forward_part(): pl.pallas_call(functools.partial(forward_kernel, jobs, tile, kinds), in_s...]
    ppermute x22, waiting for transfers between devices: 20.4 us -> 22.5 us  [swap(): return lax.ppermute(value, axis, [(i ^ bit, i) for i in range(size)])]
  transfers between devices with their start and end apart: 22 -> 22, of which waited for: 13 -> 11; matrix products, arithmetic and copies ran while one was open for 0% -> 0% of each run, Pallas kernels for 48% -> 46%
where the time goes in v4:
time: 102 us
  Pallas kernels  56.6 us (55%)
  waiting for transfers between devices  22.5 us (22%)
  starting transfers between devices  20.3 us (20%)
    ppermute x22, waiting for transfers between devices, swap(): return lax.ppermute(value, axis, [(i ^ bit, i) for i in range(size)])  22.5 us
    ppermute x22, starting transfers between devices, swap(): return lax.ppermute(value, axis, [(i ^ bit, i) for i in range(size)])  20.3 us
    pallas_call x2, Pallas kernels, weight_part(): pl.pallas_call(functools.partial(weight_kernel, firsts, tile), in_specs=[...  16.5 us
    pallas_call x2, Pallas kernels, input_part(): pl.pallas_call(functools.partial(input_kernel, has_prev, first), in_specs...  14.9 us
    pallas_call x3, Pallas kernels, forward_part(): pl.pallas_call(functools.partial(forward_kernel, jobs, tile, kinds), in_s...  14.8 us
    pallas_call x1, Pallas kernels, load_part(): pl.pallas_call(functools.partial(load_kernel, first), in_specs=[ANYWHERE]...  6.07 us
    pallas_call x2, Pallas kernels, first_part(): pl.pallas_call(functools.partial(first_kernel, tile, len(prev) > 0), in_s...  2.58 us
  transfers between devices with their start and end apart: 22, of which 11 were waited for; matrix products, arithmetic and copies ran while one was open for 0% of the time, Pallas kernels for 46%

profile of v4, /device:TPU:0, one launch (start us, length us, event | category | flops | bytes accessed | tf_op | source)
XLA Modules:
  0.0 102.0 jit_solution(7659253419454122358)
XLA Ops:
  0.7 4.1 %collective-permute-start.1 = (bf16[16,2048]{1,0:T(8,128)(2,1)}, bf16[16,2048]{1,0:T(8,128)(2,1)S(1)}, u32[]{:S(2)}, u32[]{:S(2)}) collective-permute-start(bf16[16,2048]{1,0:T(8,128)(2,1)} %refs_0_.2), channel_id=1, source_target_pairs={{16,0},{20,4},{24,8},{28,12},{0,16},{4,20},{8,24},{12,28},{17,1},{... | collective-permute-start | bytes 196616 | tf_op jit(solution)/shard_map/ppermute | solution.py:421
  4.8 1.6 %collective-permute-start = (bf16[16,2048]{1,0:T(8,128)(2,1)}, bf16[16,2048]{1,0:T(8,128)(2,1)S(1)}, u32[]{:S(2)}, u32[]{:S(2)}) collective-permute-start(bf16[16,2048]{1,0:T(8,128)(2,1)} %refs_0_.2), channel_id=1, source_target_pairs={{8,0},{12,4},{0,8},{4,12},{24,16},{28,20},{16,24},{20,28},{9,1},{1... | collective-permute-start | bytes 196616 | tf_op jit(solution)/shard_map/ppermute | solution.py:421
  6.3 6.1 %load_part.1 = (bf16[2048,2048]{1,0:T(8,128)(2,1)S(1)}, bf16[2048,2048]{1,0:T(8,128)(2,1)S(1)}, f32[8,128]{1,0:T(8,128)S(1)}) custom-call(bf16[2048,3584]{1,0:T(8,128)(2,1)} %refs_2_.5, bf16[2048,3584]{1,0:T(8,128)(2,1)} %refs_3_.3), custom_call_target="tpu_custom_call" | custom-call | bytes 16777216 | tf_op jit(solution)/shard_map/load_part/pallas_call | solution.py:58
  12.6 1.6 %collective-permute-start.3 = (bf16[64,2048]{1,0:T(8,128)(2,1)S(1)}, bf16[64,2048]{1,0:T(8,128)(2,1)S(1)}, u32[]{:S(2)}, u32[]{:S(2)}) collective-permute-start(bf16[64,2048]{1,0:T(8,128)(2,1)S(1)} %stack_part.2.own), channel_id=1, source_target_pairs={{4,0},{0,4},{12,8},{8,12},{20,16},{16,20},{28,24},{24,28},{5,1},{1... | collective-permute-start | bytes 786440 | tf_op jit(solution)/shard_map/ppermute | solution.py:421
  14.3 1.7 %collective-permute-start.5 = (bf16[16,2048]{1,0:T(8,128)(2,1)S(1)}, bf16[16,2048]{1,0:T(8,128)(2,1)S(1)}, u32[]{:S(2)}, u32[]{:S(2)}) collective-permute-start(bf16[16,2048]{1,0:T(8,128)(2,1)S(1)} %copy-done.6), channel_id=1, source_target_pairs={{16,0},{20,4},{24,8},{28,12},{0,16},{4,20},{8,24},{12,28},{17,1},{... | collective-permute-start | bytes 196616 | tf_op jit(solution)/shard_map/ppermute | solution.py:421
  15.9 2.5 %collective-permute-start.4 = (bf16[16,2048]{1,0:T(8,128)(2,1)S(1)}, bf16[16,2048]{1,0:T(8,128)(2,1)S(1)}, u32[]{:S(2)}, u32[]{:S(2)}) collective-permute-start(bf16[16,2048]{1,0:T(8,128)(2,1)S(1)} %copy-done.6), channel_id=1, source_target_pairs={{8,0},{12,4},{0,8},{4,12},{24,16},{28,20},{16,24},{20,28},{9,1},{1... | collective-permute-start | bytes 196616 | tf_op jit(solution)/shard_map/ppermute | solution.py:421
  18.6 1.4 %collective-permute-done.3.theirs = bf16[64,2048]{1,0:T(8,128)(2,1)S(1)} collective-permute-done((bf16[64,2048]{1,0:T(8,128)(2,1)S(1)}, bf16[64,2048]{1,0:T(8,128)(2,1)S(1)}, u32[]{:S(2)}, u32[]{:S(2)}) %collective-permute-start.3) | collective-permute-done | bytes 262176 | tf_op jit(solution)/shard_map/ppermute | solution.py:421
  20.3 1.3 %first_part.2 = (f32[64,4096]{1,0:T(8,128)S(1)}, bf16[64,4096]{1,0:T(8,128)(2,1)S(1)}) custom-call(bf16[128,2048]{1,0:T(8,128)(2,1)S(1)} %get-tuple-element.28.x.refs_0_, bf16[2048,2048]{1,0:T(8,128)(2,1)S(1)} %get-tuple-element.30.weight), custom_call_target="tpu_custom_call" | custom-call | flops 33554432 | bytes 262144 | tf_op jit(solution)/shard_map/first_part/pallas_call | solution.py:147
  21.6 2.9 %collective-permute-done.6.refs_4_.refs_3_ = bf16[16,2048]{1,0:T(8,128)(2,1)S(1)} collective-permute-done((bf16[16,2048]{1,0:T(8,128)(2,1)S(1)}, bf16[16,2048]{1,0:T(8,128)(2,1)S(1)}, u32[]{:S(2)}, u32[]{:S(2)}) %collective-permute-start.6) | collective-permute-done | bytes 65568 | tf_op jit(solution)/shard_map/ppermute | solution.py:421
  24.5 1.3 %first_part.3 = (f32[64,4096]{1,0:T(8,128)S(1)}, bf16[64,4096]{1,0:T(8,128)(2,1)S(1)}) custom-call(bf16[128,2048]{1,0:T(8,128)(2,1)S(1)} %get-tuple-element.28.x.refs_0_, bf16[2048,2048]{1,0:T(8,128)(2,1)S(1)} %get-tuple-element.29.weight, f32[64,4096]{1,0:T(8,128)S(1)} %get-tuple-element.31.refs_0_, bf16[64,4096]{1,0:T(8,128)(2,1)S(1)} %get-tuple-element.32.refs_1_, ...), custom_call_target="tpu_custom_call" | custom-call | flops 33554432 | bytes 262144 | tf_op jit(solution)/shard_map/first_part/pallas_call | solution.py:147
  25.9 1.9 %collective-permute-done.7.got.refs_1_ = bf16[64,4096]{1,0:T(8,128)(2,1)S(1)} collective-permute-done((bf16[64,4096]{1,0:T(8,128)(2,1)S(1)}, bf16[64,4096]{1,0:T(8,128)(2,1)S(1)}, u32[]{:S(2)}, u32[]{:S(2)}) %collective-permute-start.7) | collective-permute-done | bytes 524320 | tf_op jit(solution)/shard_map/ppermute | solution.py:421
  27.9 1.6 %collective-permute-start.8 = (bf16[64,4096]{1,0:T(8,128)(2,1)S(1)}, bf16[64,4096]{1,0:T(8,128)(2,1)S(1)}, u32[]{:S(2)}, u32[]{:S(2)}) collective-permute-start(bf16[64,4096]{1,0:T(8,128)(2,1)S(1)} %add_part.4.refs_3_), channel_id=1, source_target_pairs={{2,0},{3,1},{0,2},{1,3},{6,4},{7,5},{4,6},{5,7},{10,8},{11,9},{8,1... | collective-permute-start | bytes 1572872 | tf_op jit(solution)/shard_map/ppermute | solution.py:421
  29.5 5.3 %forward_part.3 = (f32[64,3072]{1,0:T(8,128)S(1)}, bf16[64,3072]{1,0:T(8,128)(2,1)S(1)}) custom-call(bf16[128,2048]{1,0:T(8,128)(2,1)S(1)} %get-tuple-element.28.x.refs_0_, bf16[2048,3584]{1,0:T(8,128)(2,1)} %refs_2_.5, bf16[2048,3584]{1,0:T(8,128)(2,1)} %refs_3_.3, bf16[64,4096]{1,0:T(8,128)(2,1)S(1)} %add_part.4.refs_3_), custom_call_target="tpu_custom_call" | custom-call | flops 100663296 | bytes 393216 | tf_op jit(solution)/shard_map/forward_part/pallas_call | solution.py:218
  34.9 0.6 collective-permute-start.11
  35.5 1.1 %collective-permute-done.9.got.refs_4_ = bf16[64,3072]{1,0:T(8,128)(2,1)S(1)} collective-permute-done((bf16[64,3072]{1,0:T(8,128)(2,1)S(1)}, bf16[64,3072]{1,0:T(8,128)(2,1)S(1)}, u32[]{:S(2)}, u32[]{:S(2)}) %collective-permute-start.9) | collective-permute-done | bytes 393248 | tf_op jit(solution)/shard_map/ppermute | solution.py:421
  37.2 6.4 %collective-permute-done.11.theirs = bf16[64,2048]{1,0:T(8,128)(2,1)S(1)} collective-permute-done((bf16[64,2048]{1,0:T(8,128)(2,1)S(1)}, bf16[64,2048]{1,0:T(8,128)(2,1)S(1)}, u32[]{:S(2)}, u32[]{:S(2)}) %collective-permute-start.11) | collective-permute-done | bytes 262176 | tf_op jit(solution)/shard_map/ppermute | solution.py:421
  43.9 0.8 copy-done.4
  44.7 5.2 %forward_part.4 = (f32[64,2048]{1,0:T(8,128)S(1)}, bf16[64,2048]{1,0:T(8,128)(2,1)S(1)}) custom-call(bf16[2048,128]{1,0:T(8,128)(2,1)S(1)} %get-tuple-element.37.refs_0_, bf16[3584,2048]{1,0:T(8,128)(2,1)} %refs_1_.5, bf16[64,3072]{1,0:T(8,128)(2,1)S(1)} %add_part.5.refs_2_, bf16[64,4096]{1,0:T(8,128)(2,1)S(1)} %collective-permute-done.8.refs_3_.refs_2_), custom_call_target="tpu_custom_call" | custom-call | flops 67108864 | bytes 262144 | tf_op jit(solution)/shard_map/forward_part/pallas_call | solution.py:218
  50.1 1.5 %collective-permute-done.12.got.refs_4_.refs_7_ = bf16[64,2048]{1,0:T(8,128)(2,1)S(1)} collective-permute-done((bf16[64,2048]{1,0:T(8,128)(2,1)S(1)}, bf16[64,2048]{1,0:T(8,128)(2,1)S(1)}, u32[]{:S(2)}, u32[]{:S(2)}) %collective-permute-start.12) | collective-permute-done | bytes 262176 | tf_op jit(solution)/shard_map/ppermute | solution.py:421
  52.2 4.2 %forward_part.5 = (f32[64,1536]{1,0:T(8,128)S(1)}, bf16[64,1536]{1,0:T(8,128)(2,1)S(1)}) custom-call(bf16[2048,128]{1,0:T(8,128)(2,1)S(1)} %get-tuple-element.37.refs_0_, bf16[3584,2048]{1,0:T(8,128)(2,1)} %refs_1_.5, bf16[64,2048]{1,0:T(8,128)(2,1)S(1)} %add_part.6.refs_2_, bf16[64,3072]{1,0:T(8,128)(2,1)S(1)} %collective-permute-done.10.refs_3_.refs_5_), custom_call_target="tpu_custom_call" | custom-call | flops 50331648 | bytes 196608 | tf_op jit(solution)/shard_map/forward_part/pallas_call | solution.py:218
  56.5 1.4 %collective-permute-done.14.got.refs_10_ = bf16[64,1536]{1,0:T(8,128)(2,1)S(1)} collective-permute-done((bf16[64,1536]{1,0:T(8,128)(2,1)S(1)}, bf16[64,1536]{1,0:T(8,128)(2,1)S(1)}, u32[]{:S(2)}, u32[]{:S(2)}) %collective-permute-start.14) | collective-permute-done | bytes 196640 | tf_op jit(solution)/shard_map/ppermute | solution.py:421
  58.0 2.1 %collective-permute-done.13.refs_0_.refs_5_.refs_8_ = bf16[64,2048]{1,0:T(8,128)(2,1)S(1)} collective-permute-done((bf16[64,2048]{1,0:T(8,128)(2,1)S(1)}, bf16[64,2048]{1,0:T(8,128)(2,1)S(1)}, u32[]{:S(2)}, u32[]{:S(2)}) %collective-permute-start.13) | collective-permute-done | bytes 262176 | tf_op jit(solution)/shard_map/ppermute | solution.py:421
  61.3 1.6 %collective-permute-done.16.refs_1_.refs_3_ = bf16[3,64,1792]{2,1,0:T(8,128)(2,1)S(1)} collective-permute-done((bf16[3,64,1792]{2,1,0:T(8,128)(2,1)S(1)}, bf16[3,64,1792]{2,1,0:T(8,128)(2,1)S(1)}, u32[]{:S(2)}, u32[]{:S(2)}) %collective-permute-start.16) | collective-permute-done | bytes 688160 | tf_op jit(solution)/shard_map/ppermute | solution.py:421
  62.9 7.6 %input_part.2.refs_12_.refs_4_ = f32[128,2048]{1,0:T(8,128)S(1)} custom-call(bf16[3,64,1792]{2,1,0:T(8,128)(2,1)S(1)} %swiglu_part.2.refs_0_.refs_2_, bf16[3,64,1792]{2,1,0:T(8,128)(2,1)S(1)} %collective-permute-done.16.refs_1_.refs_3_, bf16[2048,3584]{1,0:T(8,128)(2,1)} %refs_2_.5, bf16[2048,3584]{1,0:T(8,128)(2,1)} %refs_3_.3, ...), custom_call_target="tpu_custom_call" | custom-call | flops 1879048192 | bytes 14680064 | tf_op jit(solution)/shard_map/input_part/pallas_call | solution.py:275
  71.1 2.0 %collective-permute-done.17.refs_1_.refs_3_ = bf16[3,64,1792]{2,1,0:T(8,128)(2,1)S(1)} collective-permute-done((bf16[3,64,1792]{2,1,0:T(8,128)(2,1)S(1)}, bf16[3,64,1792]{2,1,0:T(8,128)(2,1)S(1)}, u32[]{:S(2)}, u32[]{:S(2)}) %collective-permute-start.17) | collective-permute-done | bytes 688160 | tf_op jit(solution)/shard_map/ppermute | solution.py:421
  73.1 7.3 %input_part.3 = f32[128,2048]{1,0:T(8,128)S(1)} custom-call(bf16[3,64,1792]{2,1,0:T(8,128)(2,1)S(1)} %swiglu_part.3.refs_0_.refs_2_, bf16[3,64,1792]{2,1,0:T(8,128)(2,1)S(1)} %collective-permute-done.17.refs_1_.refs_3_, bf16[2048,3584]{1,0:T(8,128)(2,1)} %refs_2_.5, bf16[2048,3584]{1,0:T(8,128)(2,1)} %refs_3_.3, f32[128,2048]{1,0:T(8,128)S(1)} %input_part.2.refs_12_.refs_4_), custom_call_target="tpu_custom_call" | custom-call | flops 1879048192 | bytes 14680064 | tf_op jit(solution)/shard_map/input_part/pallas_call | solution.py:275
  80.5 0.6 collective-permute-start.18
  81.1 8.3 %weight_part.2 = (bf16[2048,3584]{1,0:T(8,128)(2,1)}, bf16[2048,3584]{1,0:T(8,128)(2,1)}, bf16[3584,2048]{1,0:T(8,128)(2,1)}) custom-call(bf16[2048,128]{1,0:T(8,128)(2,1)S(1)} %copy-done.3, bf16[128,2048]{1,0:T(8,128)(2,1)S(1)} %copy-done.5, bf16[3,64,1792]{2,1,0:T(8,128)(2,1)S(1)} %swiglu_part.2.refs_0_.refs_2_, bf16[3,64,1792]{2,1,0:T(8,128)(2,1)S(1)} %copy-done.1, ...), custom_call_target="tpu_custom_call" | custom-call | flops 2818572288 | bytes 22020096 | tf_op jit(solution)/shard_map/weight_part/pallas_call | solution.py:341
  89.6 1.7 %collective-permute-start.21 = (bf16[16,2048]{1,0:T(8,128)(2,1)S(1)}, bf16[16,2048]{1,0:T(8,128)(2,1)S(1)}, u32[]{:S(2)}, u32[]{:S(2)}) collective-permute-start(bf16[16,2048]{1,0:T(8,128)(2,1)S(1)} %get-tuple-element.53), channel_id=1, source_target_pairs={{24,0},{28,4},{16,8},{20,12},{8,16},{12,20},{0,24},{4,28},{25,1},{... | collective-permute-start | bytes 196616 | tf_op jit(solution)/shard_map/ppermute | solution.py:421
  91.2 1.8 %collective-permute-start.20 = (bf16[16,2048]{1,0:T(8,128)(2,1)S(1)}, bf16[16,2048]{1,0:T(8,128)(2,1)S(1)}, u32[]{:S(2)}, u32[]{:S(2)}) collective-permute-start(bf16[16,2048]{1,0:T(8,128)(2,1)S(1)} %get-tuple-element.54), channel_id=1, source_target_pairs={{16,0},{20,4},{24,8},{28,12},{0,16},{4,20},{8,24},{12,28},{17,1},{... | collective-permute-start | bytes 196616 | tf_op jit(solution)/shard_map/ppermute | solution.py:421
  93.0 8.3 %weight_part.3 = (bf16[2048,3584]{1,0:T(8,128)(2,1)}, bf16[2048,3584]{1,0:T(8,128)(2,1)}, bf16[3584,2048]{1,0:T(8,128)(2,1)}) custom-call(bf16[2048,128]{1,0:T(8,128)(2,1)S(1)} %copy-done.3, bf16[128,2048]{1,0:T(8,128)(2,1)S(1)} %copy-done.5, ...), custom_call_target="tpu_custom_call", output_to_operand_aliasing={{0}: (4, {}), {1}: (5, {}), {2}: (6, {})} | custom-call | flops 2818572288 | bytes 22020096 | tf_op jit(solution)/shard_map/weight_part/pallas_call | solution.py:341
  101.3 0.7 fusion.2
  (52 shorter events, 4.7 us)
Async XLA Ops:
  0.6 12.0 %copy-start.7 = (bf16[16,2048]{1,0:T(8,128)(2,1)S(1)}, bf16[16,2048]{1,0:T(8,128)(2,1)}, u32[]{:S(2)}) copy-start(bf16[16,2048]{1,0:T(8,128)(2,1)} %refs_0_.2) | copy-start | bytes 196612
  0.6 13.6 %copy-start.6 = (bf16[16,2048]{1,0:T(8,128)(2,1)S(1)}, bf16[16,2048]{1,0:T(8,128)(2,1)}, u32[]{:S(2)}) copy-start(bf16[16,2048]{1,0:T(8,128)(2,1)} %refs_0_.3) | copy-start | bytes 196612
  0.7 11.8 %collective-permute-start.1 = (bf16[16,2048]{1,0:T(8,128)(2,1)}, bf16[16,2048]{1,0:T(8,128)(2,1)S(1)}, u32[]{:S(2)}, u32[]{:S(2)}) collective-permute-start(bf16[16,2048]{1,0:T(8,128)(2,1)} %refs_0_.2), channel_id=1, source_target_pairs={{16,0},{20,4},{24,8},{28,12},{0,16},{4,20},{8,24},{12,28},{17,1},{... | collective-permute-start | bytes 196616 | tf_op jit(solution)/shard_map/ppermute | solution.py:421
  4.8 7.7 %collective-permute-start = (bf16[16,2048]{1,0:T(8,128)(2,1)}, bf16[16,2048]{1,0:T(8,128)(2,1)S(1)}, u32[]{:S(2)}, u32[]{:S(2)}) collective-permute-start(bf16[16,2048]{1,0:T(8,128)(2,1)} %refs_0_.2), channel_id=1, source_target_pairs={{8,0},{12,4},{0,8},{4,12},{24,16},{28,20},{16,24},{20,28},{9,1},{1... | collective-permute-start | bytes 196616 | tf_op jit(solution)/shard_map/ppermute | solution.py:421
  6.3 6.3 %collective-permute-start.2 = (bf16[16,2048]{1,0:T(8,128)(2,1)}, bf16[16,2048]{1,0:T(8,128)(2,1)S(1)}, u32[]{:S(2)}, u32[]{:S(2)}) collective-permute-start(bf16[16,2048]{1,0:T(8,128)(2,1)} %refs_0_.2), channel_id=1, source_target_pairs={{24,0},{28,4},{16,8},{20,12},{8,16},{12,20},{0,24},{4,28},{25,1},{... | collective-permute-start | bytes 196616 | tf_op jit(solution)/shard_map/ppermute | solution.py:421
  12.6 7.4 %collective-permute-start.3 = (bf16[64,2048]{1,0:T(8,128)(2,1)S(1)}, bf16[64,2048]{1,0:T(8,128)(2,1)S(1)}, u32[]{:S(2)}, u32[]{:S(2)}) collective-permute-start(bf16[64,2048]{1,0:T(8,128)(2,1)S(1)} %stack_part.2.own), channel_id=1, source_target_pairs={{4,0},{0,4},{12,8},{8,12},{20,16},{16,20},{28,24},{24,28},{5,1},{1... | collective-permute-start | bytes 786440 | tf_op jit(solution)/shard_map/ppermute | solution.py:421
  14.3 7.3 %collective-permute-start.5 = (bf16[16,2048]{1,0:T(8,128)(2,1)S(1)}, bf16[16,2048]{1,0:T(8,128)(2,1)S(1)}, u32[]{:S(2)}, u32[]{:S(2)}) collective-permute-start(bf16[16,2048]{1,0:T(8,128)(2,1)S(1)} %copy-done.6), channel_id=1, source_target_pairs={{16,0},{20,4},{24,8},{28,12},{0,16},{4,20},{8,24},{12,28},{17,1},{... | collective-permute-start | bytes 196616 | tf_op jit(solution)/shard_map/ppermute | solution.py:421
  15.9 5.6 %collective-permute-start.4 = (bf16[16,2048]{1,0:T(8,128)(2,1)S(1)}, bf16[16,2048]{1,0:T(8,128)(2,1)S(1)}, u32[]{:S(2)}, u32[]{:S(2)}) collective-permute-start(bf16[16,2048]{1,0:T(8,128)(2,1)S(1)} %copy-done.6), channel_id=1, source_target_pairs={{8,0},{12,4},{0,8},{4,12},{24,16},{28,20},{16,24},{20,28},{9,1},{1... | collective-permute-start | bytes 196616 | tf_op jit(solution)/shard_map/ppermute | solution.py:421
  18.4 6.1 %collective-permute-start.6 = (bf16[16,2048]{1,0:T(8,128)(2,1)S(1)}, bf16[16,2048]{1,0:T(8,128)(2,1)S(1)}, u32[]{:S(2)}, u32[]{:S(2)}) collective-permute-start(bf16[16,2048]{1,0:T(8,128)(2,1)S(1)} %copy-done.6), channel_id=1, source_target_pairs={{24,0},{28,4},{16,8},{20,12},{8,16},{12,20},{0,24},{4,28},{25,1},{... | collective-permute-start | bytes 196616 | tf_op jit(solution)/shard_map/ppermute | solution.py:421
  20.3 7.6 %copy-start.2 = (bf16[2048,128]{1,0:T(8,128)(2,1)}, bf16[2048,128]{1,0:T(8,128)(2,1)S(1)}, u32[]{:S(2)}) copy-start(bf16[2048,128]{1,0:T(8,128)(2,1)S(1)} %get-tuple-element.42.refs_0_) | copy-start | bytes 1572868
  25.8 2.0 %collective-permute-start.7 = (bf16[64,4096]{1,0:T(8,128)(2,1)S(1)}, bf16[64,4096]{1,0:T(8,128)(2,1)S(1)}, u32[]{:S(2)}, u32[]{:S(2)}) collective-permute-start(bf16[64,4096]{1,0:T(8,128)(2,1)S(1)} %get-tuple-element.34.refs_4_), channel_id=1, source_target_pairs={{1,0},{0,1},{3,2},{2,3},{5,4},{4,5},{7,6},{6,7},{9,8},{8,9},{11,10... | collective-permute-start | bytes 1572872 | tf_op jit(solution)/shard_map/ppermute | solution.py:421
  27.9 16.8 %collective-permute-start.8 = (bf16[64,4096]{1,0:T(8,128)(2,1)S(1)}, bf16[64,4096]{1,0:T(8,128)(2,1)S(1)}, u32[]{:S(2)}, u32[]{:S(2)}) collective-permute-start(bf16[64,4096]{1,0:T(8,128)(2,1)S(1)} %add_part.4.refs_3_), channel_id=1, source_target_pairs={{2,0},{3,1},{0,2},{1,3},{6,4},{7,5},{4,6},{5,7},{10,8},{11,9},{8,1... | collective-permute-start | bytes 1572872 | tf_op jit(solution)/shard_map/ppermute | solution.py:421
  34.8 1.8 %collective-permute-start.9 = (bf16[64,3072]{1,0:T(8,128)(2,1)S(1)}, bf16[64,3072]{1,0:T(8,128)(2,1)S(1)}, u32[]{:S(2)}, u32[]{:S(2)}) collective-permute-start(bf16[64,3072]{1,0:T(8,128)(2,1)S(1)} %get-tuple-element.36), channel_id=1, source_target_pairs={{1,0},{0,1},{3,2},{2,3},{5,4},{4,5},{7,6},{6,7},{9,8},{8,9},{11,10... | collective-permute-start | bytes 1179656 | tf_op jit(solution)/shard_map/ppermute | solution.py:421
  34.9 8.8 %collective-permute-start.11 = (bf16[64,2048]{1,0:T(8,128)(2,1)S(1)}, bf16[64,2048]{1,0:T(8,128)(2,1)S(1)}, u32[]{:S(2)}, u32[]{:S(2)}) collective-permute-start(bf16[64,2048]{1,0:T(8,128)(2,1)S(1)} %stack_part.3.own), channel_id=1, source_target_pairs={{4,0},{0,4},{12,8},{8,12},{20,16},{16,20},{28,24},{24,28},{5,1},{1... | collective-permute-start | bytes 786440 | tf_op jit(solution)/shard_map/ppermute | solution.py:421
  36.7 15.6 %collective-permute-start.10 = (bf16[64,3072]{1,0:T(8,128)(2,1)S(1)}, bf16[64,3072]{1,0:T(8,128)(2,1)S(1)}, u32[]{:S(2)}, u32[]{:S(2)}) collective-permute-start(bf16[64,3072]{1,0:T(8,128)(2,1)S(1)} %add_part.5.refs_2_), channel_id=1, source_target_pairs={{2,0},{3,1},{0,2},{1,3},{6,4},{7,5},{4,6},{5,7},{10,8},{11,9},{8,1... | collective-permute-start | bytes 1179656 | tf_op jit(solution)/shard_map/ppermute | solution.py:421
  43.9 0.8 copy-start.4
  50.0 1.6 %collective-permute-start.12 = (bf16[64,2048]{1,0:T(8,128)(2,1)S(1)}, bf16[64,2048]{1,0:T(8,128)(2,1)S(1)}, u32[]{:S(2)}, u32[]{:S(2)}) collective-permute-start(bf16[64,2048]{1,0:T(8,128)(2,1)S(1)} %get-tuple-element.39), channel_id=1, source_target_pairs={{1,0},{0,1},{3,2},{2,3},{5,4},{4,5},{7,6},{6,7},{9,8},{8,9},{11,10... | collective-permute-start | bytes 786440 | tf_op jit(solution)/shard_map/ppermute | solution.py:421
  51.6 8.4 %collective-permute-start.13 = (bf16[64,2048]{1,0:T(8,128)(2,1)S(1)}, bf16[64,2048]{1,0:T(8,128)(2,1)S(1)}, u32[]{:S(2)}, u32[]{:S(2)}) collective-permute-start(bf16[64,2048]{1,0:T(8,128)(2,1)S(1)} %add_part.6.refs_2_), channel_id=1, source_target_pairs={{2,0},{3,1},{0,2},{1,3},{6,4},{7,5},{4,6},{5,7},{10,8},{11,9},{8,1... | collective-permute-start | bytes 786440 | tf_op jit(solution)/shard_map/ppermute | solution.py:421
  56.5 1.5 %collective-permute-start.14 = (bf16[64,1536]{1,0:T(8,128)(2,1)S(1)}, bf16[64,1536]{1,0:T(8,128)(2,1)S(1)}, u32[]{:S(2)}, u32[]{:S(2)}) collective-permute-start(bf16[64,1536]{1,0:T(8,128)(2,1)S(1)} %get-tuple-element.41), channel_id=1, source_target_pairs={{1,0},{0,1},{3,2},{2,3},{5,4},{4,5},{7,6},{6,7},{9,8},{8,9},{11,10... | collective-permute-start | bytes 589832 | tf_op jit(solution)/shard_map/ppermute | solution.py:421
  60.7 2.2 %collective-permute-start.16 = (bf16[3,64,1792]{2,1,0:T(8,128)(2,1)S(1)}, bf16[3,64,1792]{2,1,0:T(8,128)(2,1)S(1)}, u32[]{:S(2)}, u32[]{:S(2)}) collective-permute-start(bf16[3,64,1792]{2,1,0:T(8,128)(2,1)S(1)} %swiglu_part.2.refs_0_.refs_2_), channel_id=1, source_target_pairs={{1,0},{0,1},{3,2},{2,3},{5,4},{4,5},{7,6},{6,7},{9,8},{8,9},{11,10... | collective-permute-start | bytes 2064392 | tf_op jit(solution)/shard_map/ppermute | solution.py:421
  60.8 9.7 %collective-permute-start.15 = (bf16[64,1536]{1,0:T(8,128)(2,1)S(1)}, bf16[64,1536]{1,0:T(8,128)(2,1)S(1)}, u32[]{:S(2)}, u32[]{:S(2)}) collective-permute-start(bf16[64,1536]{1,0:T(8,128)(2,1)S(1)} %add_part.7.refs_6_.refs_4_), channel_id=1, source_target_pairs={{2,0},{3,1},{0,2},{1,3},{6,4},{7,5},{4,6},{5,7},{10,8},{11,9},{8,1... | collective-permute-start | bytes 589832 | tf_op jit(solution)/shard_map/ppermute | solution.py:421
  62.9 7.6 %copy-start = (bf16[3,64,1792]{2,1,0:T(8,128)(2,1)}, bf16[3,64,1792]{2,1,0:T(8,128)(2,1)S(1)}, u32[]{:S(2)}) copy-start(bf16[3,64,1792]{2,1,0:T(8,128)(2,1)S(1)} %collective-permute-done.16.refs_1_.refs_3_) | copy-start | bytes 2064388
  70.9 2.2 %collective-permute-start.17 = (bf16[3,64,1792]{2,1,0:T(8,128)(2,1)S(1)}, bf16[3,64,1792]{2,1,0:T(8,128)(2,1)S(1)}, u32[]{:S(2)}, u32[]{:S(2)}) collective-permute-start(bf16[3,64,1792]{2,1,0:T(8,128)(2,1)S(1)} %swiglu_part.3.refs_0_.refs_2_), channel_id=1, source_target_pairs={{1,0},{0,1},{3,2},{2,3},{5,4},{4,5},{7,6},{6,7},{9,8},{8,9},{11,10... | collective-permute-start | bytes 2064392 | tf_op jit(solution)/shard_map/ppermute | solution.py:421
  71.1 10.0 %copy-start.1 = (bf16[3,64,1792]{2,1,0:T(8,128)(2,1)S(1)}, bf16[3,64,1792]{2,1,0:T(8,128)(2,1)}, u32[]{:S(2)}) copy-start(bf16[3,64,1792]{2,1,0:T(8,128)(2,1)} %copy-done) | copy-start | bytes 2064388
  71.1 10.0 %copy-start.3 = (bf16[2048,128]{1,0:T(8,128)(2,1)S(1)}, bf16[2048,128]{1,0:T(8,128)(2,1)}, u32[]{:S(2)}) copy-start(bf16[2048,128]{1,0:T(8,128)(2,1)} %copy-done.2) | copy-start | bytes 1572868
  71.1 10.0 %copy-start.5 = (bf16[128,2048]{1,0:T(8,128)(2,1)S(1)}, bf16[128,2048]{1,0:T(8,128)(2,1)}, u32[]{:S(2)}) copy-start(bf16[128,2048]{1,0:T(8,128)(2,1)} %copy-done.4) | copy-start | bytes 1572868
  80.5 8.9 %collective-permute-start.18 = (bf16[64,2048]{1,0:T(8,128)(2,1)S(1)}, bf16[64,2048]{1,0:T(8,128)(2,1)S(1)}, u32[]{:S(2)}, u32[]{:S(2)}) collective-permute-start(bf16[64,2048]{1,0:T(8,128)(2,1)S(1)} %select_convert_fusion.refs_4_.refs_7_), channel_id=1, source_target_pairs={{4,0},{0,4},{12,8},{8,12},{20,16},{16,20},{28,24},{24,28},{5,1},{1... | collective-permute-start | bytes 786440 | tf_op jit(solution)/shard_map/ppermute | solution.py:421
  89.5 11.8 %collective-permute-start.19 = (bf16[16,2048]{1,0:T(8,128)(2,1)S(1)}, bf16[16,2048]{1,0:T(8,128)(2,1)S(1)}, u32[]{:S(2)}, u32[]{:S(2)}) collective-permute-start(bf16[16,2048]{1,0:T(8,128)(2,1)S(1)} %get-tuple-element.52), channel_id=1, source_target_pairs={{8,0},{12,4},{0,8},{4,12},{24,16},{28,20},{16,24},{20,28},{9,1},{1... | collective-permute-start | bytes 196616 | tf_op jit(solution)/shard_map/ppermute | solution.py:421
  89.6 11.8 %collective-permute-start.21 = (bf16[16,2048]{1,0:T(8,128)(2,1)S(1)}, bf16[16,2048]{1,0:T(8,128)(2,1)S(1)}, u32[]{:S(2)}, u32[]{:S(2)}) collective-permute-start(bf16[16,2048]{1,0:T(8,128)(2,1)S(1)} %get-tuple-element.53), channel_id=1, source_target_pairs={{24,0},{28,4},{16,8},{20,12},{8,16},{12,20},{0,24},{4,28},{25,1},{... | collective-permute-start | bytes 196616 | tf_op jit(solution)/shard_map/ppermute | solution.py:421
  91.2 10.1 %collective-permute-start.20 = (bf16[16,2048]{1,0:T(8,128)(2,1)S(1)}, bf16[16,2048]{1,0:T(8,128)(2,1)S(1)}, u32[]{:S(2)}, u32[]{:S(2)}) collective-permute-start(bf16[16,2048]{1,0:T(8,128)(2,1)S(1)} %get-tuple-element.54), channel_id=1, source_target_pairs={{16,0},{20,4},{24,8},{28,12},{0,16},{4,20},{8,24},{12,28},{17,1},{... | collective-permute-start | bytes 196616 | tf_op jit(solution)/shard_map/ppermute | solution.py:421

commit v5 on v4

--- a/solution.py
+++ b/solution.py
@@ -37,6 +37,12 @@
 def row_blocks(d):
     step = step_of(d)
     return [pl.ds(at, step) for at in range(0, d, step)]
+
+
+def early_blocks(d):
+    step = step_of(d)
+    half = step // 2
+    return [pl.ds(0, half), pl.ds(half, half)] + row_blocks(d)[1:]
 
 
 def load_kernel(first, gate, up, gate_out, up_out, mark, sems):
@@ -226,7 +232,7 @@
             pltpu.VMEM((t, tall_width), F32),
             pltpu.SemaphoreType.DMA((n_wide + len(tall_jobs) * len(row_blocks(d)),)),
         ],
-        compiler_params=params(28),
+        compiler_params=params(20 if t <= 256 else 32),
         cost_estimate=cost(2 * t * d * total, 2 * d * total, 32),
         name="forward_part",
     )(*used, *[weights[key] for key in kinds], *after)
@@ -244,7 +250,7 @@
     mine, peer, wg, wu, *others = refs
     prev = others[0]
     out, gate_buf, up_buf, sems = refs[-4:]
-    parts = row_blocks(wg.shape[0])
+    parts = early_blocks(wg.shape[0])
     cols = pl.ds(first, mine.shape[2])
     copies = [
         (
@@ -283,9 +289,9 @@
         scratch_shapes=[
             pltpu.VMEM((d, span), BF16),
             pltpu.VMEM((d, span), BF16),
-            pltpu.SemaphoreType.DMA((2, len(row_blocks(d)))),
+            pltpu.SemaphoreType.DMA((2, len(early_blocks(d)))),
         ],
-        compiler_params=params(28),
+        compiler_params=params(24 if t <= 256 else 32),
         cost_estimate=cost(2 * t * d * span, 4 * d * span),
         name="input_part",
     )(mine, peer, wg, wu, *([prev] if has_prev else []), *after)

time: 102 us -> 102 us (level)
  no operation moved by 1% of the time
where the time goes in v5:
time: 102 us
  Pallas kernels  57.5 us (56%)
  waiting for transfers between devices  22.5 us (22%)
  starting transfers between devices  20.3 us (20%)
    ppermute x22, waiting for transfers between devices, swap(): return lax.ppermute(value, axis, [(i ^ bit, i) for i in range(size)])  22.5 us
    ppermute x22, starting transfers between devices, swap(): return lax.ppermute(value, axis, [(i ^ bit, i) for i in range(size)])  20.3 us
    pallas_call x2, Pallas kernels, weight_part(): pl.pallas_call(functools.partial(weight_kernel, firsts, tile), in_specs=[...  16.5 us
    pallas_call x2, Pallas kernels, input_part(): pl.pallas_call(functools.partial(input_kernel, has_prev, first), in_specs...  15.6 us
    pallas_call x3, Pallas kernels, forward_part(): pl.pallas_call(functools.partial(forward_kernel, jobs, tile, kinds), in_s...  15 us
    pallas_call x1, Pallas kernels, load_part(): pl.pallas_call(functools.partial(load_kernel, first), in_specs=[ANYWHERE]...  6.07 us
    pallas_call x2, Pallas kernels, first_part(): pl.pallas_call(functools.partial(first_kernel, tile, len(prev) > 0), in_s...  2.58 us
  transfers between devices with their start and end apart: 22, of which 11 were waited for; matrix products, arithmetic and copies ran while one was open for 0% of the time, Pallas kernels for 46%

profile of v5, /device:TPU:0, one launch (start us, length us, event | category | flops | bytes accessed | tf_op | source)
XLA Modules:
  0.0 102.1 jit_solution(9520753027669830585)
XLA Ops:
  0.7 4.1 %collective-permute-start.1 = (bf16[16,2048]{1,0:T(8,128)(2,1)}, bf16[16,2048]{1,0:T(8,128)(2,1)S(1)}, u32[]{:S(2)}, u32[]{:S(2)}) collective-permute-start(bf16[16,2048]{1,0:T(8,128)(2,1)} %refs_0_.2), channel_id=1, source_target_pairs={{16,0},{20,4},{24,8},{28,12},{0,16},{4,20},{8,24},{12,28},{17,1},{... | collective-permute-start | bytes 196616 | tf_op jit(solution)/shard_map/ppermute | solution.py:427
  4.8 1.6 %collective-permute-start = (bf16[16,2048]{1,0:T(8,128)(2,1)}, bf16[16,2048]{1,0:T(8,128)(2,1)S(1)}, u32[]{:S(2)}, u32[]{:S(2)}) collective-permute-start(bf16[16,2048]{1,0:T(8,128)(2,1)} %refs_0_.2), channel_id=1, source_target_pairs={{8,0},{12,4},{0,8},{4,12},{24,16},{28,20},{16,24},{20,28},{9,1},{1... | collective-permute-start | bytes 196616 | tf_op jit(solution)/shard_map/ppermute | solution.py:427
  6.3 6.1 %load_part.1 = (bf16[2048,2048]{1,0:T(8,128)(2,1)S(1)}, bf16[2048,2048]{1,0:T(8,128)(2,1)S(1)}, f32[8,128]{1,0:T(8,128)S(1)}) custom-call(bf16[2048,3584]{1,0:T(8,128)(2,1)} %refs_2_.5, bf16[2048,3584]{1,0:T(8,128)(2,1)} %refs_3_.3), custom_call_target="tpu_custom_call" | custom-call | bytes 16777216 | tf_op jit(solution)/shard_map/load_part/pallas_call | solution.py:64
  12.6 1.6 %collective-permute-start.3 = (bf16[64,2048]{1,0:T(8,128)(2,1)S(1)}, bf16[64,2048]{1,0:T(8,128)(2,1)S(1)}, u32[]{:S(2)}, u32[]{:S(2)}) collective-permute-start(bf16[64,2048]{1,0:T(8,128)(2,1)S(1)} %stack_part.2.own), channel_id=1, source_target_pairs={{4,0},{0,4},{12,8},{8,12},{20,16},{16,20},{28,24},{24,28},{5,1},{1... | collective-permute-start | bytes 786440 | tf_op jit(solution)/shard_map/ppermute | solution.py:427
  14.3 1.7 %collective-permute-start.5 = (bf16[16,2048]{1,0:T(8,128)(2,1)S(1)}, bf16[16,2048]{1,0:T(8,128)(2,1)S(1)}, u32[]{:S(2)}, u32[]{:S(2)}) collective-permute-start(bf16[16,2048]{1,0:T(8,128)(2,1)S(1)} %copy-done.6), channel_id=1, source_target_pairs={{16,0},{20,4},{24,8},{28,12},{0,16},{4,20},{8,24},{12,28},{17,1},{... | collective-permute-start | bytes 196616 | tf_op jit(solution)/shard_map/ppermute | solution.py:427
  15.9 2.5 %collective-permute-start.4 = (bf16[16,2048]{1,0:T(8,128)(2,1)S(1)}, bf16[16,2048]{1,0:T(8,128)(2,1)S(1)}, u32[]{:S(2)}, u32[]{:S(2)}) collective-permute-start(bf16[16,2048]{1,0:T(8,128)(2,1)S(1)} %copy-done.6), channel_id=1, source_target_pairs={{8,0},{12,4},{0,8},{4,12},{24,16},{28,20},{16,24},{20,28},{9,1},{1... | collective-permute-start | bytes 196616 | tf_op jit(solution)/shard_map/ppermute | solution.py:427
  18.6 1.4 %collective-permute-done.3.theirs = bf16[64,2048]{1,0:T(8,128)(2,1)S(1)} collective-permute-done((bf16[64,2048]{1,0:T(8,128)(2,1)S(1)}, bf16[64,2048]{1,0:T(8,128)(2,1)S(1)}, u32[]{:S(2)}, u32[]{:S(2)}) %collective-permute-start.3) | collective-permute-done | bytes 262176 | tf_op jit(solution)/shard_map/ppermute | solution.py:427
  20.3 1.3 %first_part.2 = (f32[64,4096]{1,0:T(8,128)S(1)}, bf16[64,4096]{1,0:T(8,128)(2,1)S(1)}) custom-call(bf16[128,2048]{1,0:T(8,128)(2,1)S(1)} %get-tuple-element.28.x.refs_0_, bf16[2048,2048]{1,0:T(8,128)(2,1)S(1)} %get-tuple-element.30.weight), custom_call_target="tpu_custom_call" | custom-call | flops 33554432 | bytes 262144 | tf_op jit(solution)/shard_map/first_part/pallas_call | solution.py:153
  21.6 2.9 %collective-permute-done.6.refs_4_.refs_3_ = bf16[16,2048]{1,0:T(8,128)(2,1)S(1)} collective-permute-done((bf16[16,2048]{1,0:T(8,128)(2,1)S(1)}, bf16[16,2048]{1,0:T(8,128)(2,1)S(1)}, u32[]{:S(2)}, u32[]{:S(2)}) %collective-permute-start.6) | collective-permute-done | bytes 65568 | tf_op jit(solution)/shard_map/ppermute | solution.py:427
  24.5 1.3 %first_part.3 = (f32[64,4096]{1,0:T(8,128)S(1)}, bf16[64,4096]{1,0:T(8,128)(2,1)S(1)}) custom-call(bf16[128,2048]{1,0:T(8,128)(2,1)S(1)} %get-tuple-element.28.x.refs_0_, bf16[2048,2048]{1,0:T(8,128)(2,1)S(1)} %get-tuple-element.29.weight, f32[64,4096]{1,0:T(8,128)S(1)} %get-tuple-element.31.refs_0_, bf16[64,4096]{1,0:T(8,128)(2,1)S(1)} %get-tuple-element.32.refs_1_, ...), custom_call_target="tpu_custom_call" | custom-call | flops 33554432 | bytes 262144 | tf_op jit(solution)/shard_map/first_part/pallas_call | solution.py:153
  25.9 1.9 %collective-permute-done.7.got.refs_1_ = bf16[64,4096]{1,0:T(8,128)(2,1)S(1)} collective-permute-done((bf16[64,4096]{1,0:T(8,128)(2,1)S(1)}, bf16[64,4096]{1,0:T(8,128)(2,1)S(1)}, u32[]{:S(2)}, u32[]{:S(2)}) %collective-permute-start.7) | collective-permute-done | bytes 524320 | tf_op jit(solution)/shard_map/ppermute | solution.py:427
  27.9 1.6 %collective-permute-start.8 = (bf16[64,4096]{1,0:T(8,128)(2,1)S(1)}, bf16[64,4096]{1,0:T(8,128)(2,1)S(1)}, u32[]{:S(2)}, u32[]{:S(2)}) collective-permute-start(bf16[64,4096]{1,0:T(8,128)(2,1)S(1)} %add_part.4.refs_3_), channel_id=1, source_target_pairs={{2,0},{3,1},{0,2},{1,3},{6,4},{7,5},{4,6},{5,7},{10,8},{11,9},{8,1... | collective-permute-start | bytes 1572872 | tf_op jit(solution)/shard_map/ppermute | solution.py:427
  29.5 5.3 %forward_part.3 = (f32[64,3072]{1,0:T(8,128)S(1)}, bf16[64,3072]{1,0:T(8,128)(2,1)S(1)}) custom-call(bf16[128,2048]{1,0:T(8,128)(2,1)S(1)} %get-tuple-element.28.x.refs_0_, bf16[2048,3584]{1,0:T(8,128)(2,1)} %refs_2_.5, bf16[2048,3584]{1,0:T(8,128)(2,1)} %refs_3_.3, bf16[64,4096]{1,0:T(8,128)(2,1)S(1)} %add_part.4.refs_3_), custom_call_target="tpu_custom_call" | custom-call | flops 100663296 | bytes 393216 | tf_op jit(solution)/shard_map/forward_part/pallas_call | solution.py:224
  34.9 0.6 collective-permute-start.11
  35.5 1.1 %collective-permute-done.9.got.refs_4_ = bf16[64,3072]{1,0:T(8,128)(2,1)S(1)} collective-permute-done((bf16[64,3072]{1,0:T(8,128)(2,1)S(1)}, bf16[64,3072]{1,0:T(8,128)(2,1)S(1)}, u32[]{:S(2)}, u32[]{:S(2)}) %collective-permute-start.9) | collective-permute-done | bytes 393248 | tf_op jit(solution)/shard_map/ppermute | solution.py:427
  37.2 6.4 %collective-permute-done.11.theirs = bf16[64,2048]{1,0:T(8,128)(2,1)S(1)} collective-permute-done((bf16[64,2048]{1,0:T(8,128)(2,1)S(1)}, bf16[64,2048]{1,0:T(8,128)(2,1)S(1)}, u32[]{:S(2)}, u32[]{:S(2)}) %collective-permute-start.11) | collective-permute-done | bytes 262176 | tf_op jit(solution)/shard_map/ppermute | solution.py:427
  43.9 5.4 %forward_part.4 = (f32[64,2048]{1,0:T(8,128)S(1)}, bf16[64,2048]{1,0:T(8,128)(2,1)S(1)}) custom-call(bf16[2048,128]{1,0:T(8,128)(2,1)S(1)} %get-tuple-element.37.refs_0_, bf16[3584,2048]{1,0:T(8,128)(2,1)} %refs_1_.5, bf16[64,3072]{1,0:T(8,128)(2,1)S(1)} %add_part.5.refs_2_, bf16[64,4096]{1,0:T(8,128)(2,1)S(1)} %collective-permute-done.8.refs_3_.refs_2_), custom_call_target="tpu_custom_call" | custom-call | flops 67108864 | bytes 262144 | tf_op jit(solution)/shard_map/forward_part/pallas_call | solution.py:224
  49.5 1.5 %collective-permute-done.12.got.refs_4_.refs_7_ = bf16[64,2048]{1,0:T(8,128)(2,1)S(1)} collective-permute-done((bf16[64,2048]{1,0:T(8,128)(2,1)S(1)}, bf16[64,2048]{1,0:T(8,128)(2,1)S(1)}, u32[]{:S(2)}, u32[]{:S(2)}) %collective-permute-start.12) | collective-permute-done | bytes 262176 | tf_op jit(solution)/shard_map/ppermute | solution.py:427
  51.6 4.2 %forward_part.5 = (f32[64,1536]{1,0:T(8,128)S(1)}, bf16[64,1536]{1,0:T(8,128)(2,1)S(1)}) custom-call(bf16[2048,128]{1,0:T(8,128)(2,1)S(1)} %get-tuple-element.37.refs_0_, bf16[3584,2048]{1,0:T(8,128)(2,1)} %refs_1_.5, bf16[64,2048]{1,0:T(8,128)(2,1)S(1)} %add_part.6.refs_2_, bf16[64,3072]{1,0:T(8,128)(2,1)S(1)} %collective-permute-done.10.refs_3_.refs_5_), custom_call_target="tpu_custom_call" | custom-call | flops 50331648 | bytes 196608 | tf_op jit(solution)/shard_map/forward_part/pallas_call | solution.py:224
  56.0 1.4 %collective-permute-done.14.got.refs_10_ = bf16[64,1536]{1,0:T(8,128)(2,1)S(1)} collective-permute-done((bf16[64,1536]{1,0:T(8,128)(2,1)S(1)}, bf16[64,1536]{1,0:T(8,128)(2,1)S(1)}, u32[]{:S(2)}, u32[]{:S(2)}) %collective-permute-start.14) | collective-permute-done | bytes 196640 | tf_op jit(solution)/shard_map/ppermute | solution.py:427
  57.4 2.1 %collective-permute-done.13.refs_0_.refs_5_.refs_8_ = bf16[64,2048]{1,0:T(8,128)(2,1)S(1)} collective-permute-done((bf16[64,2048]{1,0:T(8,128)(2,1)S(1)}, bf16[64,2048]{1,0:T(8,128)(2,1)S(1)}, u32[]{:S(2)}, u32[]{:S(2)}) %collective-permute-start.13) | collective-permute-done | bytes 262176 | tf_op jit(solution)/shard_map/ppermute | solution.py:427
  59.5 0.6 swiglu_part.2.refs_0_.refs_2_
  60.7 1.6 %collective-permute-done.16.refs_1_.refs_3_ = bf16[3,64,1792]{2,1,0:T(8,128)(2,1)S(1)} collective-permute-done((bf16[3,64,1792]{2,1,0:T(8,128)(2,1)S(1)}, bf16[3,64,1792]{2,1,0:T(8,128)(2,1)S(1)}, u32[]{:S(2)}, u32[]{:S(2)}) %collective-permute-start.16) | collective-permute-done | bytes 688160 | tf_op jit(solution)/shard_map/ppermute | solution.py:427
  62.3 7.9 %input_part.2.refs_12_.refs_4_ = f32[128,2048]{1,0:T(8,128)S(1)} custom-call(bf16[3,64,1792]{2,1,0:T(8,128)(2,1)S(1)} %swiglu_part.2.refs_0_.refs_2_, bf16[3,64,1792]{2,1,0:T(8,128)(2,1)S(1)} %collective-permute-done.16.refs_1_.refs_3_, bf16[2048,3584]{1,0:T(8,128)(2,1)} %refs_2_.5, bf16[2048,3584]{1,0:T(8,128)(2,1)} %refs_3_.3, ...), custom_call_target="tpu_custom_call" | custom-call | flops 1879048192 | bytes 14680064 | tf_op jit(solution)/shard_map/input_part/pallas_call | solution.py:281
  70.9 2.0 %collective-permute-done.17.refs_1_.refs_3_ = bf16[3,64,1792]{2,1,0:T(8,128)(2,1)S(1)} collective-permute-done((bf16[3,64,1792]{2,1,0:T(8,128)(2,1)S(1)}, bf16[3,64,1792]{2,1,0:T(8,128)(2,1)S(1)}, u32[]{:S(2)}, u32[]{:S(2)}) %collective-permute-start.17) | collective-permute-done | bytes 688160 | tf_op jit(solution)/shard_map/ppermute | solution.py:427
  72.9 7.7 %input_part.3 = f32[128,2048]{1,0:T(8,128)S(1)} custom-call(bf16[3,64,1792]{2,1,0:T(8,128)(2,1)S(1)} %swiglu_part.3.refs_0_.refs_2_, bf16[3,64,1792]{2,1,0:T(8,128)(2,1)S(1)} %collective-permute-done.17.refs_1_.refs_3_, bf16[2048,3584]{1,0:T(8,128)(2,1)} %refs_2_.5, bf16[2048,3584]{1,0:T(8,128)(2,1)} %refs_3_.3, f32[128,2048]{1,0:T(8,128)S(1)} %input_part.2.refs_12_.refs_4_), custom_call_target="tpu_custom_call" | custom-call | flops 1879048192 | bytes 14680064 | tf_op jit(solution)/shard_map/input_part/pallas_call | solution.py:281
  80.6 0.6 collective-permute-start.18
  81.2 8.3 %weight_part.2 = (bf16[2048,3584]{1,0:T(8,128)(2,1)}, bf16[2048,3584]{1,0:T(8,128)(2,1)}, bf16[3584,2048]{1,0:T(8,128)(2,1)}) custom-call(bf16[2048,128]{1,0:T(8,128)(2,1)S(1)} %copy-done.3, bf16[128,2048]{1,0:T(8,128)(2,1)S(1)} %copy-done.5, bf16[3,64,1792]{2,1,0:T(8,128)(2,1)S(1)} %swiglu_part.2.refs_0_.refs_2_, bf16[3,64,1792]{2,1,0:T(8,128)(2,1)S(1)} %copy-done.1, ...), custom_call_target="tpu_custom_call" | custom-call | flops 2818572288 | bytes 22020096 | tf_op jit(solution)/shard_map/weight_part/pallas_call | solution.py:347
  89.7 1.7 %collective-permute-start.21 = (bf16[16,2048]{1,0:T(8,128)(2,1)S(1)}, bf16[16,2048]{1,0:T(8,128)(2,1)S(1)}, u32[]{:S(2)}, u32[]{:S(2)}) collective-permute-start(bf16[16,2048]{1,0:T(8,128)(2,1)S(1)} %get-tuple-element.53), channel_id=1, source_target_pairs={{24,0},{28,4},{16,8},{20,12},{8,16},{12,20},{0,24},{4,28},{25,1},{... | collective-permute-start | bytes 196616 | tf_op jit(solution)/shard_map/ppermute | solution.py:427
  91.4 1.8 %collective-permute-start.20 = (bf16[16,2048]{1,0:T(8,128)(2,1)S(1)}, bf16[16,2048]{1,0:T(8,128)(2,1)S(1)}, u32[]{:S(2)}, u32[]{:S(2)}) collective-permute-start(bf16[16,2048]{1,0:T(8,128)(2,1)S(1)} %get-tuple-element.54), channel_id=1, source_target_pairs={{16,0},{20,4},{24,8},{28,12},{0,16},{4,20},{8,24},{12,28},{17,1},{... | collective-permute-start | bytes 196616 | tf_op jit(solution)/shard_map/ppermute | solution.py:427
  93.2 8.3 %weight_part.3 = (bf16[2048,3584]{1,0:T(8,128)(2,1)}, bf16[2048,3584]{1,0:T(8,128)(2,1)}, bf16[3584,2048]{1,0:T(8,128)(2,1)}) custom-call(bf16[2048,128]{1,0:T(8,128)(2,1)S(1)} %copy-done.3, bf16[128,2048]{1,0:T(8,128)(2,1)S(1)} %copy-done.5, ...), custom_call_target="tpu_custom_call", output_to_operand_aliasing={{0}: (4, {}), {1}: (5, {}), {2}: (6, {})} | custom-call | flops 2818572288 | bytes 22020096 | tf_op jit(solution)/shard_map/weight_part/pallas_call | solution.py:347
  101.5 0.7 fusion.2
  (52 shorter events, 4.1 us)
Async XLA Ops:
  0.6 12.0 %copy-start.7 = (bf16[16,2048]{1,0:T(8,128)(2,1)S(1)}, bf16[16,2048]{1,0:T(8,128)(2,1)}, u32[]{:S(2)}) copy-start(bf16[16,2048]{1,0:T(8,128)(2,1)} %refs_0_.2) | copy-start | bytes 196612
  0.6 13.6 %copy-start.6 = (bf16[16,2048]{1,0:T(8,128)(2,1)S(1)}, bf16[16,2048]{1,0:T(8,128)(2,1)}, u32[]{:S(2)}) copy-start(bf16[16,2048]{1,0:T(8,128)(2,1)} %refs_0_.3) | copy-start | bytes 196612
  0.7 11.8 %collective-permute-start.1 = (bf16[16,2048]{1,0:T(8,128)(2,1)}, bf16[16,2048]{1,0:T(8,128)(2,1)S(1)}, u32[]{:S(2)}, u32[]{:S(2)}) collective-permute-start(bf16[16,2048]{1,0:T(8,128)(2,1)} %refs_0_.2), channel_id=1, source_target_pairs={{16,0},{20,4},{24,8},{28,12},{0,16},{4,20},{8,24},{12,28},{17,1},{... | collective-permute-start | bytes 196616 | tf_op jit(solution)/shard_map/ppermute | solution.py:427
  4.8 7.7 %collective-permute-start = (bf16[16,2048]{1,0:T(8,128)(2,1)}, bf16[16,2048]{1,0:T(8,128)(2,1)S(1)}, u32[]{:S(2)}, u32[]{:S(2)}) collective-permute-start(bf16[16,2048]{1,0:T(8,128)(2,1)} %refs_0_.2), channel_id=1, source_target_pairs={{8,0},{12,4},{0,8},{4,12},{24,16},{28,20},{16,24},{20,28},{9,1},{1... | collective-permute-start | bytes 196616 | tf_op jit(solution)/shard_map/ppermute | solution.py:427
  6.3 6.3 %collective-permute-start.2 = (bf16[16,2048]{1,0:T(8,128)(2,1)}, bf16[16,2048]{1,0:T(8,128)(2,1)S(1)}, u32[]{:S(2)}, u32[]{:S(2)}) collective-permute-start(bf16[16,2048]{1,0:T(8,128)(2,1)} %refs_0_.2), channel_id=1, source_target_pairs={{24,0},{28,4},{16,8},{20,12},{8,16},{12,20},{0,24},{4,28},{25,1},{... | collective-permute-start | bytes 196616 | tf_op jit(solution)/shard_map/ppermute | solution.py:427
  12.6 7.4 %collective-permute-start.3 = (bf16[64,2048]{1,0:T(8,128)(2,1)S(1)}, bf16[64,2048]{1,0:T(8,128)(2,1)S(1)}, u32[]{:S(2)}, u32[]{:S(2)}) collective-permute-start(bf16[64,2048]{1,0:T(8,128)(2,1)S(1)} %stack_part.2.own), channel_id=1, source_target_pairs={{4,0},{0,4},{12,8},{8,12},{20,16},{16,20},{28,24},{24,28},{5,1},{1... | collective-permute-start | bytes 786440 | tf_op jit(solution)/shard_map/ppermute | solution.py:427
  14.3 7.3 %collective-permute-start.5 = (bf16[16,2048]{1,0:T(8,128)(2,1)S(1)}, bf16[16,2048]{1,0:T(8,128)(2,1)S(1)}, u32[]{:S(2)}, u32[]{:S(2)}) collective-permute-start(bf16[16,2048]{1,0:T(8,128)(2,1)S(1)} %copy-done.6), channel_id=1, source_target_pairs={{16,0},{20,4},{24,8},{28,12},{0,16},{4,20},{8,24},{12,28},{17,1},{... | collective-permute-start | bytes 196616 | tf_op jit(solution)/shard_map/ppermute | solution.py:427
  15.9 5.6 %collective-permute-start.4 = (bf16[16,2048]{1,0:T(8,128)(2,1)S(1)}, bf16[16,2048]{1,0:T(8,128)(2,1)S(1)}, u32[]{:S(2)}, u32[]{:S(2)}) collective-permute-start(bf16[16,2048]{1,0:T(8,128)(2,1)S(1)} %copy-done.6), channel_id=1, source_target_pairs={{8,0},{12,4},{0,8},{4,12},{24,16},{28,20},{16,24},{20,28},{9,1},{1... | collective-permute-start | bytes 196616 | tf_op jit(solution)/shard_map/ppermute | solution.py:427
  18.4 6.1 %collective-permute-start.6 = (bf16[16,2048]{1,0:T(8,128)(2,1)S(1)}, bf16[16,2048]{1,0:T(8,128)(2,1)S(1)}, u32[]{:S(2)}, u32[]{:S(2)}) collective-permute-start(bf16[16,2048]{1,0:T(8,128)(2,1)S(1)} %copy-done.6), channel_id=1, source_target_pairs={{24,0},{28,4},{16,8},{20,12},{8,16},{12,20},{0,24},{4,28},{25,1},{... | collective-permute-start | bytes 196616 | tf_op jit(solution)/shard_map/ppermute | solution.py:427
  20.3 14.5 %copy-start.2 = (bf16[2048,128]{1,0:T(8,128)(2,1)}, bf16[2048,128]{1,0:T(8,128)(2,1)S(1)}, u32[]{:S(2)}) copy-start(bf16[2048,128]{1,0:T(8,128)(2,1)S(1)} %get-tuple-element.42.refs_0_) | copy-start | bytes 1572868
  25.8 2.0 %collective-permute-start.7 = (bf16[64,4096]{1,0:T(8,128)(2,1)S(1)}, bf16[64,4096]{1,0:T(8,128)(2,1)S(1)}, u32[]{:S(2)}, u32[]{:S(2)}) collective-permute-start(bf16[64,4096]{1,0:T(8,128)(2,1)S(1)} %get-tuple-element.34.refs_4_), channel_id=1, source_target_pairs={{1,0},{0,1},{3,2},{2,3},{5,4},{4,5},{7,6},{6,7},{9,8},{8,9},{11,10... | collective-permute-start | bytes 1572872 | tf_op jit(solution)/shard_map/ppermute | solution.py:427
  27.9 16.1 %collective-permute-start.8 = (bf16[64,4096]{1,0:T(8,128)(2,1)S(1)}, bf16[64,4096]{1,0:T(8,128)(2,1)S(1)}, u32[]{:S(2)}, u32[]{:S(2)}) collective-permute-start(bf16[64,4096]{1,0:T(8,128)(2,1)S(1)} %add_part.4.refs_3_), channel_id=1, source_target_pairs={{2,0},{3,1},{0,2},{1,3},{6,4},{7,5},{4,6},{5,7},{10,8},{11,9},{8,1... | collective-permute-start | bytes 1572872 | tf_op jit(solution)/shard_map/ppermute | solution.py:427
  34.8 1.8 %collective-permute-start.9 = (bf16[64,3072]{1,0:T(8,128)(2,1)S(1)}, bf16[64,3072]{1,0:T(8,128)(2,1)S(1)}, u32[]{:S(2)}, u32[]{:S(2)}) collective-permute-start(bf16[64,3072]{1,0:T(8,128)(2,1)S(1)} %get-tuple-element.36), channel_id=1, source_target_pairs={{1,0},{0,1},{3,2},{2,3},{5,4},{4,5},{7,6},{6,7},{9,8},{8,9},{11,10... | collective-permute-start | bytes 1179656 | tf_op jit(solution)/shard_map/ppermute | solution.py:427
  34.9 8.8 %collective-permute-start.11 = (bf16[64,2048]{1,0:T(8,128)(2,1)S(1)}, bf16[64,2048]{1,0:T(8,128)(2,1)S(1)}, u32[]{:S(2)}, u32[]{:S(2)}) collective-permute-start(bf16[64,2048]{1,0:T(8,128)(2,1)S(1)} %stack_part.3.own), channel_id=1, source_target_pairs={{4,0},{0,4},{12,8},{8,12},{20,16},{16,20},{28,24},{24,28},{5,1},{1... | collective-permute-start | bytes 786440 | tf_op jit(solution)/shard_map/ppermute | solution.py:427
  36.7 15.0 %collective-permute-start.10 = (bf16[64,3072]{1,0:T(8,128)(2,1)S(1)}, bf16[64,3072]{1,0:T(8,128)(2,1)S(1)}, u32[]{:S(2)}, u32[]{:S(2)}) collective-permute-start(bf16[64,3072]{1,0:T(8,128)(2,1)S(1)} %add_part.5.refs_2_), channel_id=1, source_target_pairs={{2,0},{3,1},{0,2},{1,3},{6,4},{7,5},{4,6},{5,7},{10,8},{11,9},{8,1... | collective-permute-start | bytes 1179656 | tf_op jit(solution)/shard_map/ppermute | solution.py:427
  43.9 11.9 %copy-start.4 = (bf16[128,2048]{1,0:T(8,128)(2,1)}, bf16[128,2048]{1,0:T(8,128)(2,1)S(1)}, u32[]{:S(2)}) copy-start(bf16[128,2048]{1,0:T(8,128)(2,1)S(1)} %get-tuple-element.43.refs_1_) | copy-start | bytes 1572868
  49.4 1.6 %collective-permute-start.12 = (bf16[64,2048]{1,0:T(8,128)(2,1)S(1)}, bf16[64,2048]{1,0:T(8,128)(2,1)S(1)}, u32[]{:S(2)}, u32[]{:S(2)}) collective-permute-start(bf16[64,2048]{1,0:T(8,128)(2,1)S(1)} %get-tuple-element.39), channel_id=1, source_target_pairs={{1,0},{0,1},{3,2},{2,3},{5,4},{4,5},{7,6},{6,7},{9,8},{8,9},{11,10... | collective-permute-start | bytes 786440 | tf_op jit(solution)/shard_map/ppermute | solution.py:427
  51.0 8.4 %collective-permute-start.13 = (bf16[64,2048]{1,0:T(8,128)(2,1)S(1)}, bf16[64,2048]{1,0:T(8,128)(2,1)S(1)}, u32[]{:S(2)}, u32[]{:S(2)}) collective-permute-start(bf16[64,2048]{1,0:T(8,128)(2,1)S(1)} %add_part.6.refs_2_), channel_id=1, source_target_pairs={{2,0},{3,1},{0,2},{1,3},{6,4},{7,5},{4,6},{5,7},{10,8},{11,9},{8,1... | collective-permute-start | bytes 786440 | tf_op jit(solution)/shard_map/ppermute | solution.py:427
  55.9 1.5 %collective-permute-start.14 = (bf16[64,1536]{1,0:T(8,128)(2,1)S(1)}, bf16[64,1536]{1,0:T(8,128)(2,1)S(1)}, u32[]{:S(2)}, u32[]{:S(2)}) collective-permute-start(bf16[64,1536]{1,0:T(8,128)(2,1)S(1)} %get-tuple-element.41), channel_id=1, source_target_pairs={{1,0},{0,1},{3,2},{2,3},{5,4},{4,5},{7,6},{6,7},{9,8},{8,9},{11,10... | collective-permute-start | bytes 589832 | tf_op jit(solution)/shard_map/ppermute | solution.py:427
  60.1 2.2 %collective-permute-start.16 = (bf16[3,64,1792]{2,1,0:T(8,128)(2,1)S(1)}, bf16[3,64,1792]{2,1,0:T(8,128)(2,1)S(1)}, u32[]{:S(2)}, u32[]{:S(2)}) collective-permute-start(bf16[3,64,1792]{2,1,0:T(8,128)(2,1)S(1)} %swiglu_part.2.refs_0_.refs_2_), channel_id=1, source_target_pairs={{1,0},{0,1},{3,2},{2,3},{5,4},{4,5},{7,6},{6,7},{9,8},{8,9},{11,10... | collective-permute-start | bytes 2064392 | tf_op jit(solution)/shard_map/ppermute | solution.py:427
  60.2 10.1 %collective-permute-start.15 = (bf16[64,1536]{1,0:T(8,128)(2,1)S(1)}, bf16[64,1536]{1,0:T(8,128)(2,1)S(1)}, u32[]{:S(2)}, u32[]{:S(2)}) collective-permute-start(bf16[64,1536]{1,0:T(8,128)(2,1)S(1)} %add_part.7.refs_6_.refs_4_), channel_id=1, source_target_pairs={{2,0},{3,1},{0,2},{1,3},{6,4},{7,5},{4,6},{5,7},{10,8},{11,9},{8,1... | collective-permute-start | bytes 589832 | tf_op jit(solution)/shard_map/ppermute | solution.py:427
  62.3 7.9 %copy-start = (bf16[3,64,1792]{2,1,0:T(8,128)(2,1)}, bf16[3,64,1792]{2,1,0:T(8,128)(2,1)S(1)}, u32[]{:S(2)}) copy-start(bf16[3,64,1792]{2,1,0:T(8,128)(2,1)S(1)} %collective-permute-done.16.refs_1_.refs_3_) | copy-start | bytes 2064388
  70.7 2.2 %collective-permute-start.17 = (bf16[3,64,1792]{2,1,0:T(8,128)(2,1)S(1)}, bf16[3,64,1792]{2,1,0:T(8,128)(2,1)S(1)}, u32[]{:S(2)}, u32[]{:S(2)}) collective-permute-start(bf16[3,64,1792]{2,1,0:T(8,128)(2,1)S(1)} %swiglu_part.3.refs_0_.refs_2_), channel_id=1, source_target_pairs={{1,0},{0,1},{3,2},{2,3},{5,4},{4,5},{7,6},{6,7},{9,8},{8,9},{11,10... | collective-permute-start | bytes 2064392 | tf_op jit(solution)/shard_map/ppermute | solution.py:427
  70.9 10.4 %copy-start.1 = (bf16[3,64,1792]{2,1,0:T(8,128)(2,1)S(1)}, bf16[3,64,1792]{2,1,0:T(8,128)(2,1)}, u32[]{:S(2)}) copy-start(bf16[3,64,1792]{2,1,0:T(8,128)(2,1)} %copy-done) | copy-start | bytes 2064388
  70.9 10.4 %copy-start.3 = (bf16[2048,128]{1,0:T(8,128)(2,1)S(1)}, bf16[2048,128]{1,0:T(8,128)(2,1)}, u32[]{:S(2)}) copy-start(bf16[2048,128]{1,0:T(8,128)(2,1)} %copy-done.2) | copy-start | bytes 1572868
  70.9 10.4 %copy-start.5 = (bf16[128,2048]{1,0:T(8,128)(2,1)S(1)}, bf16[128,2048]{1,0:T(8,128)(2,1)}, u32[]{:S(2)}) copy-start(bf16[128,2048]{1,0:T(8,128)(2,1)} %copy-done.4) | copy-start | bytes 1572868
  80.6 8.9 %collective-permute-start.18 = (bf16[64,2048]{1,0:T(8,128)(2,1)S(1)}, bf16[64,2048]{1,0:T(8,128)(2,1)S(1)}, u32[]{:S(2)}, u32[]{:S(2)}) collective-permute-start(bf16[64,2048]{1,0:T(8,128)(2,1)S(1)} %select_convert_fusion.refs_4_.refs_7_), channel_id=1, source_target_pairs={{4,0},{0,4},{12,8},{8,12},{20,16},{16,20},{28,24},{24,28},{5,1},{1... | collective-permute-start | bytes 786440 | tf_op jit(solution)/shard_map/ppermute | solution.py:427
  89.6 11.8 %collective-permute-start.19 = (bf16[16,2048]{1,0:T(8,128)(2,1)S(1)}, bf16[16,2048]{1,0:T(8,128)(2,1)S(1)}, u32[]{:S(2)}, u32[]{:S(2)}) collective-permute-start(bf16[16,2048]{1,0:T(8,128)(2,1)S(1)} %get-tuple-element.52), channel_id=1, source_target_pairs={{8,0},{12,4},{0,8},{4,12},{24,16},{28,20},{16,24},{20,28},{9,1},{1... | collective-permute-start | bytes 196616 | tf_op jit(solution)/shard_map/ppermute | solution.py:427
  89.7 11.8 %collective-permute-start.21 = (bf16[16,2048]{1,0:T(8,128)(2,1)S(1)}, bf16[16,2048]{1,0:T(8,128)(2,1)S(1)}, u32[]{:S(2)}, u32[]{:S(2)}) collective-permute-start(bf16[16,2048]{1,0:T(8,128)(2,1)S(1)} %get-tuple-element.53), channel_id=1, source_target_pairs={{24,0},{28,4},{16,8},{20,12},{8,16},{12,20},{0,24},{4,28},{25,1},{... | collective-permute-start | bytes 196616 | tf_op jit(solution)/shard_map/ppermute | solution.py:427
  91.4 10.1 %collective-permute-start.20 = (bf16[16,2048]{1,0:T(8,128)(2,1)S(1)}, bf16[16,2048]{1,0:T(8,128)(2,1)S(1)}, u32[]{:S(2)}, u32[]{:S(2)}) collective-permute-start(bf16[16,2048]{1,0:T(8,128)(2,1)S(1)} %get-tuple-element.54), channel_id=1, source_target_pairs={{16,0},{20,4},{24,8},{28,12},{0,16},{4,20},{8,24},{12,28},{17,1},{... | collective-permute-start | bytes 196616 | tf_op jit(solution)/shard_map/ppermute | solution.py:427
